TPU v7x, 32 devices: a whole 2x2x4 slice. The times are simulated.
32 devices in a mesh: parts: 1, dp: 4 (over x, core), expert: 8 (over z, y).
Axes of the slice: x: 2, y: 2, z: 4, core: 2. Of those that a mesh axis runs over, the one named last changes fastest.
Arguments:
- hidden: bfloat16 [64, 2048], P(('parts', 'dp')), may hold values from -6 to 6
- states: float32 [64, 8, 128, 128], P(('parts', 'dp'), 'expert'), may hold values from -0.6 to 0.6
- migration: int32 [16, 4], P('parts'), may hold values from 0 to 15, as said below
- routes: int32 [64, 10], P('parts'), may hold values from 0 to 31, all different within a row; in each aligned block of 64 rows (0 to 63, 64 to 127, ...) at most 40 rows name the same one
- w_qkvz: bfloat16 [2048, 3072], P('dp', 'expert'), may hold values from -0.125 to 0.125
- w_ba: bfloat16 [2048, 16], P('dp', 'expert'), may hold values from -0.125 to 0.125
- a_log: float32 [8], P('expert'), may hold values from -2.5 to 1
- dt_bias: float32 [8], P('expert'), may hold values from -3 to 1
- attn_gain: float32 [2048], replicated, may hold values from 0.1 to 1.9
- head_gain: float32 [128], replicated, may hold values from 0.1 to 1.9
- w_out: bfloat16 [1024, 2048], P('expert'), may hold values from -0.1875 to 0.1875
- moe_gain: float32 [2048], replicated, may hold values from 0.1 to 1.9
- w_router: bfloat16 [2048, 32], P(None, ('dp', 'expert')), may hold values from -0.125 to 0.125
- w_gate_up: bfloat16 [32, 2048, 512], P(('dp', 'expert')), may hold values from -0.125 to 0.125
- w_down: bfloat16 [32, 256, 2048], P(('dp', 'expert')), may hold values from -0.375 to 0.375
Outputs:
- mixed: bfloat16 [64, 2048], P(('parts', 'dp'), 'expert')
Inputs may be any that keep to these rules, and one draw needn't show every extreme that they name: `migration`: row g * 4 + j holds group g's j-th leaving row. Each group sends 4 rows from distinct slots to 4 different groups (itself possibly), and receives exactly one row from each of 4 groups, into distinct slots. Group numbers are below 4, slots below 16. `routes`: each row names 10 different experts; no expert is named by more than 40 rows.
All inputs are finite; a program needn't handle non-finite values.
Results may differ from a plain program's by a relative error of at most 0.0064.
Values may be sent and summed in bfloat16 or wider, within the bound.
No kernel may reach another device: no remote copies, remote signals or barrier semaphores. Data moves between devices by JAX's collectives and lax.ppermute only.
A program may use at most 64 MiB of HBM per device.

v0:
```python
import jax
import jax.numpy as jnp
from jax import lax
from jax.sharding import PartitionSpec as P

DK = 128
DV = 128
MOE_FF = 256


EPS = 1e-06


def swapped(value, axis, bit):
    mask = 2**bit
    pairs = [(source, source ^ mask) for source in range(lax.axis_size(axis))]
    return lax.ppermute(value, axis, pairs)


def norm_rows(values, gain):
    values = values.astype(jnp.float32)
    return values * lax.rsqrt(jnp.mean(values * values, axis=-1, keepdims=True) + EPS) * gain


def unit_rows(values):
    return values * lax.rsqrt(jnp.sum(values * values, axis=-1, keepdims=True) + EPS)


def per_device(
    hidden,
    states,
    migration,
    routes,
    w_qkvz,
    w_ba,
    a_log,
    dt_bias,
    attn_gain,
    head_gain,
    w_out,
    moe_gain,
    w_router,
    w_gate_up,
    w_down,
):
    group_total = lax.axis_size("dp")
    member_total = lax.axis_size("expert")
    group_index = lax.axis_index("dp")
    member = lax.axis_index("expert")
    group_rows = hidden.shape[0]
    leave_count = migration.shape[0] // group_total
    source_group = migration[:, 0]
    source_slot = migration[:, 1]
    target_group = migration[:, 2]
    target_slot = migration[:, 3]
    head_state = states[:, 0]
    source_slots = lax.dynamic_slice_in_dim(source_slot, group_index * leave_count, leave_count)
    leaving = head_state[source_slots]
    my_targets = lax.dynamic_slice_in_dim(target_group, group_index * leave_count, leave_count)
    outbound = (
        jnp.zeros((group_total,) + leaving.shape[1:], jnp.float32).at[my_targets].set(leaving)
    )
    received = lax.all_to_all(outbound, "dp", split_axis=0, concat_axis=0, tiled=True)
    arrivals = received[source_group]
    target = jnp.where(target_group == group_index, target_slot, group_rows)
    head_state = head_state.at[target].set(arrivals, mode="drop")
    normed_in = norm_rows(hidden, attn_gain).astype(jnp.bfloat16)
    projected = jnp.dot(
        normed_in,
        lax.all_gather(w_qkvz, "dp", axis=0, tiled=True),
        preferred_element_type=jnp.float32,
    )
    mix_values = jnp.dot(
        normed_in,
        lax.all_gather(w_ba, "dp", axis=0, tiled=True),
        preferred_element_type=jnp.float32,
    )
    projected = projected.astype(jnp.bfloat16)
    mix_values = mix_values.astype(jnp.bfloat16).astype(jnp.float32)
    half_width = DK // 2
    own_halves = projected[:, :DK]
    other_halves = swapped(own_halves, "expert", 0)
    is_first = member % 2 == 0
    first_half = jnp.where(is_first, own_halves, other_halves).astype(jnp.float32)
    second_half = jnp.where(is_first, other_halves, own_halves).astype(jnp.float32)
    queries = unit_rows(
        jnp.concatenate([first_half[:, :half_width], second_half[:, :half_width]], axis=1)
    ) * DK ** (-0.5)
    keys_unit = unit_rows(
        jnp.concatenate([first_half[:, half_width:], second_half[:, half_width:]], axis=1)
    )
    values = projected[:, DK : DK + DV].astype(jnp.float32)
    out_gate = projected[:, DK + DV :].astype(jnp.float32)
    beta_gate = jax.nn.sigmoid(mix_values[:, 0])
    decay_rate = jnp.exp(-jnp.exp(a_log[0]) * jax.nn.softplus(mix_values[:, 1] + dt_bias[0]))
    updated = head_state * decay_rate[:, None, None]
    recalled = jnp.einsum("rk,rkv->rv", keys_unit, updated, precision=lax.Precision.HIGHEST)
    correction = (values - recalled) * beta_gate[:, None]
    updated = updated + keys_unit[:, :, None] * correction[:, None, :]
    readout = jnp.einsum("rk,rkv->rv", queries, updated, precision=lax.Precision.HIGHEST)
    gated = (norm_rows(readout, head_gain) * jax.nn.silu(out_gate)).astype(jnp.bfloat16)
    attention = lax.psum(jnp.dot(gated, w_out, preferred_element_type=jnp.float32), "expert")
    residual = hidden.astype(jnp.float32) + attention
    normed_moe = norm_rows(residual, moe_gain).astype(jnp.bfloat16)
    every_row = lax.all_gather(normed_moe, "dp", axis=0, tiled=True)
    total_rows = routes.shape[0]
    expert_total = group_total * member_total
    capacity = min(
        total_rows, (2 * total_rows * routes.shape[1] + expert_total - 1) // expert_total
    )
    expert_index = group_index * member_total + member
    hit_count = jnp.sum((routes == expert_index).astype(jnp.int32), axis=1)
    ranking = jnp.cumsum(hit_count) - 1
    slot_index = jnp.arange(capacity, dtype=jnp.int32)
    picker = (ranking[None, :] == slot_index[:, None]) & (hit_count[None, :] > 0)
    chosen = jnp.dot(
        picker.astype(jnp.bfloat16), every_row, preferred_element_type=jnp.float32
    ).astype(jnp.bfloat16)
    logit_col = jnp.dot(chosen, w_router, preferred_element_type=jnp.float32)[:, 0]
    gate_up_out = jnp.dot(chosen, w_gate_up[0], preferred_element_type=jnp.float32)
    hidden_act = (jax.nn.silu(gate_up_out[:, :MOE_FF]) * gate_up_out[:, MOE_FF:]).astype(
        jnp.bfloat16
    )
    output = jnp.dot(hidden_act, w_down[0], preferred_element_type=jnp.float32)
    weight = jnp.exp(logit_col)
    weighted = weight[:, None] * output
    spread_back = jnp.transpose(picker.astype(jnp.float32))
    numerator = jnp.dot(spread_back, weighted, precision=lax.Precision.HIGHEST)
    denominator = jnp.dot(spread_back, weight, precision=lax.Precision.HIGHEST)
    denominator_wide = jnp.broadcast_to(denominator[:, None], (total_rows, member_total))
    numerator, denominator_wide = (
        lax.psum_scatter(numerator, "expert", scatter_dimension=1, tiled=True),
        lax.psum_scatter(denominator_wide, "expert", scatter_dimension=1, tiled=True),
    )
    numerator, denominator_wide = (
        lax.psum_scatter(numerator, "dp", scatter_dimension=0, tiled=True),
        lax.psum_scatter(denominator_wide, "dp", scatter_dimension=0, tiled=True),
    )
    column_count = numerator.shape[1]
    own_residual = lax.dynamic_slice_in_dim(residual, member * column_count, column_count, 1)
    return (own_residual + numerator / denominator_wide).astype(jnp.bfloat16)


def solution(mesh):
    placed = (
        P(("parts", "dp"), None),
        P(("parts", "dp"), "expert", None, None),
        P("parts", None),
        P("parts", None),
        P("dp", "expert"),
        P("dp", "expert"),
        P("expert"),
        P("expert"),
        P(),
        P(),
        P("expert", None),
        P(),
        P(None, ("dp", "expert")),
        P(("dp", "expert"), None, None),
        P(("dp", "expert"), None, None),
    )
    return jax.shard_map(
        per_device,
        mesh=mesh,
        in_specs=placed,
        out_specs=P(("parts", "dp"), "expert"),
        check_vma=False,
    )
```

profile of v0, /device:TPU:0, one launch (start us, length us, event | category | flops | bytes accessed | tf_op | source)
XLA Modules:
  0.0 233.9 jit_solution(15059126647987268655)
XLA Ops:
  6.6 1.4 copy.31
  8.1 0.6 gather_fusion
  8.7 0.7 broadcast_in_dim.9
  9.4 2.2 scatter_fusion
  11.6 4.2 %all-to-all-start = ((f32[4,128,128]{2,1,0:T(8,128)}), f32[4,128,128]{2,1,0:T(8,128)S(1)}, u32[]{:S(2)}, u32[]{:S(2)}) async-start(f32[4,128,128]{2,1,0:T(8,128)} %scatter_fusion), calls=%async_computation | async-start | bytes 524288 | tf_op jit(solution)/shard_map/all_to_all | solution.py:63
  17.2 6.5 %all_gather.10 = bf16[2048,2]{0,1:T(2,128)(2,1)S(1)} all-gather(bf16[512,2]{0,1:T(2,128)(2,1)S(1)} %copy-done.7), channel_id=1, replica_groups=mesh['parts'=1,'dp'=4,'expert'=8] {'dp'}, dimensions={0}, use_global_device_ids=true | all-gather | bytes 10240 | tf_op jit(solution)/shard_map/all_gather | solution.py:75
  23.8 0.2 fusion.2
  24.1 7.7 %all-gather.2.cloned.1.call-done = bf16[2048,384]{1,0:T(8,128)(2,1)} async-done(((bf16[512,384]{1,0:T(8,128)(2,1)}), bf16[2048,384]{1,0:T(8,128)(2,1)}) %all-gather.2.cloned.1.call-update) | async-done | bytes 1572880 | tf_op jit(solution)/shard_map/all_gather | solution.py:70
  31.8 1.8 convolution_convert_fusion.1
  33.6 2.2 collective-permute-start
  35.8 1.6 gather_fusion.1
  37.4 2.3 scatter_fusion.1
  39.8 0.2 multiply_reduce_fusion.2
  40.1 0.2 multiply_reduce_fusion.3
  40.4 1.0 fusion.9
  41.5 1.1 fusion.5
  42.8 0.9 fusion.40
  44.1 68.8 %all-reduce.3.cloned.1.call-done = f32[16,2048]{1,0:T(8,128)} async-done(((f32[16,2048]{1,0:T(8,128)}), f32[16,2048]{1,0:T(8,128)}) %all-reduce.3.cloned.1.call-update) | async-done | bytes 131088 | tf_op jit(solution)/shard_map/psum | solution.py:102
  112.9 1.0 multiply_reduce_fusion
  114.0 5.8 %all_gather.11 = bf16[64,2048]{1,0:T(8,128)(2,1)S(1)} all-gather(bf16[16,2048]{1,0:T(8,128)(2,1)S(1)} %multiply_convert_fusion), channel_id=1, replica_groups=mesh['parts'=1,'dp'=4,'expert'=8] {'dp'}, dimensions={0}, use_global_device_ids=true | all-gather | bytes 327680 | tf_op jit(solution)/shard_map/all_gather | solution.py:105
  120.1 0.5 fusion
  120.6 0.3 convolution_multiply_fusion
  120.9 1.2 fusion.24
  122.2 0.6 dynamic-slice.2
  123.0 19.8 %all-reduce = f32[64,8]{0,1:T(8,128)S(1)} all-reduce(f32[64,8]{0,1:T(8,128)S(1)} %broadcast_in_dim.10), channel_id=4, replica_groups=mesh['parts'=1,'dp'=4,'expert'=8] {'expert'}, use_global_device_ids=true, to_apply=%region_12.13.clone | all-reduce | flops 512 | bytes 4096
  142.8 0.6 constant_dynamic-slice_fusion.2
  143.5 0.7 copy.23
  144.2 39.3 %reduce-scatter.6.cloned.1.call-done = f32[64,256]{1,0:T(8,128)} async-done(((f32[64,2048]{1,0:T(8,128)}), f32[64,256]{1,0:T(8,128)}) %reduce-scatter.6.cloned.1.call-update) | async-done | bytes 65552 | tf_op jit(solution)/shard_map/reduce_scatter | solution.py:132
  183.5 20.6 %reduce-scatter.10.cloned.1.call-done = f32[16,1]{1,0:T(8,128)} async-done(((f32[64,1]{1,0:T(8,128)}), f32[16,1]{1,0:T(8,128)}) %reduce-scatter.10.cloned.1.call-update) | async-done | bytes 80
  204.1 0.8 copy.24
  204.9 21.1 %reduce-scatter.8.cloned.1.call-done = f32[16,256]{1,0:T(8,128)} async-done(((f32[64,256]{1,0:T(8,128)}), f32[16,256]{1,0:T(8,128)}) %reduce-scatter.8.cloned.1.call-update) | async-done | bytes 16400 | tf_op jit(solution)/shard_map/reduce_scatter | solution.py:136
  226.0 1.4 add_convert_fusion
  (65 shorter events, 2.0 us)
Async XLA Ops:
  6.5 113.6 %copy-start = (bf16[1,2048,512]{2,1,0:T(8,128)(2,1)S(1)}, bf16[1,2048,512]{2,1,0:T(8,128)(2,1)}, u32[]{:S(2)}) copy-start(bf16[1,2048,512]{2,1,0:T(8,128)(2,1)} %param.28) | copy-start | bytes 6291460
  6.5 1.5 copy-start.8
  6.5 17.1 %copy-start.6 = (s32[64,10]{0,1:T(8,128)S(1)}, s32[64,10]{0,1:T(8,128)}, u32[]{:S(2)}) copy-start(s32[64,10]{0,1:T(8,128)} %param.18) | copy-start | bytes 7684
  6.5 17.2 %copy-start.2 = (bf16[16,2048]{1,0:T(8,128)(2,1)S(1)}, bf16[16,2048]{1,0:T(8,128)(2,1)}, u32[]{:S(2)}) copy-start(bf16[16,2048]{1,0:T(8,128)(2,1)} %param.15) | copy-start | bytes 196612
  6.5 10.6 %copy-start.7 = (bf16[512,2]{0,1:T(2,128)(2,1)S(1)}, bf16[512,2]{0,1:T(2,128)(2,1)}, u32[]{:S(2)}) copy-start(bf16[512,2]{0,1:T(2,128)(2,1)} %param.20) | copy-start | bytes 6148
  6.5 17.3 %copy-start.4 = (f32[2048]{0:T(1024)S(1)}, f32[2048]{0:T(1024)}, u32[]{:S(2)}) copy-start(f32[2048]{0:T(1024)} %param.23) | copy-start | bytes 24580
  6.6 25.3 %all-gather.2.cloned.1.call-start = ((), (), s32[]{:S(2)}) async-start(), calls=%async_computation.4 | async-start | bytes 1966080 | tf_op jit(solution)/shard_map/all_gather | solution.py:70
  11.6 24.2 %all-to-all-start = ((f32[4,128,128]{2,1,0:T(8,128)}), f32[4,128,128]{2,1,0:T(8,128)S(1)}, u32[]{:S(2)}, u32[]{:S(2)}) async-start(f32[4,128,128]{2,1,0:T(8,128)} %scatter_fusion), calls=%async_computation | async-start | bytes 524288 | tf_op jit(solution)/shard_map/all_to_all | solution.py:63
  15.8 97.0 %all-reduce.3.cloned.1.call-start = ((), (), s32[]{:S(2)}) async-start(), calls=%async_computation.5 | async-start | bytes 262144 | tf_op jit(solution)/shard_map/psum | solution.py:102
  33.6 6.1 %collective-permute-start = (bf16[16,128]{1,0:T(8,128)(2,1)S(1)}, bf16[16,128]{1,0:T(8,128)(2,1)S(1)}, u32[]{:S(2)}, u32[]{:S(2)}) collective-permute-start(bf16[16,128]{1,0:T(8,128)(2,1)S(1)} %slice.64), channel_id=1, source_target_pairs={{0,1},{1,0},{2,3},{3,2},{4,5},{5,4},{6,7},{7,6},{8,9},{9,8},{10,11... | collective-permute-start | bytes 12296 | tf_op jit(solution)/shard_map/ppermute | solution.py:17
  37.4 5.4 %copy-start.9 = (f32[128]{0:T(128)S(1)}, f32[128]{0:T(128)}, u32[]{:S(2)}) copy-start(f32[128]{0:T(128)} %param.24) | copy-start | bytes 1540
  39.7 3.1 %copy-start.3 = (bf16[128,2048]{1,0:T(8,128)(2,1)S(1)}, bf16[128,2048]{1,0:T(8,128)(2,1)}, u32[]{:S(2)}) copy-start(bf16[128,2048]{1,0:T(8,128)(2,1)} %param.25) | copy-start | bytes 1572868
  39.7 74.2 %copy-start.5 = (f32[2048]{0:T(1024)S(1)}, f32[2048]{0:T(1024)}, u32[]{:S(2)}) copy-start(f32[2048]{0:T(1024)} %param.26) | copy-start | bytes 24580
  40.4 79.6 %copy-start.10 = (bf16[2048,1]{0,1:T(2,128)(2,1)S(1)}, bf16[2048,1]{0,1:T(2,128)(2,1)}, u32[]{:S(2)}) copy-start(bf16[2048,1]{0,1:T(2,128)(2,1)} %param.27) | copy-start | bytes 12292
  43.7 76.9 %copy-start.1 = (bf16[1,256,2048]{2,1,0:T(8,128)(2,1)S(1)}, bf16[1,256,2048]{2,1,0:T(8,128)(2,1)}, u32[]{:S(2)}) copy-start(bf16[1,256,2048]{2,1,0:T(8,128)(2,1)} %param.29) | copy-start | bytes 3145732
  43.7 139.8 %reduce-scatter.6.cloned.1.call-start = ((), (), s32[]{:S(2)}) async-start(), calls=%async_computation.6 | async-start | bytes 589824 | tf_op jit(solution)/shard_map/reduce_scatter | solution.py:132
  120.1 2.1 copy-start.11
  122.2 81.9 %reduce-scatter.10.cloned.1.call-start = ((), (), s32[]{:S(2)}) async-start(), calls=%async_computation.8 | async-start | bytes 40960
  144.2 81.8 %reduce-scatter.8.cloned.1.call-start = ((), (), s32[]{:S(2)}) async-start(), calls=%async_computation.7 | async-start | bytes 81920 | tf_op jit(solution)/shard_map/reduce_scatter | solution.py:136
Sparse Core Ops, SparseCore 0:
  9.0 22.8 all-gather.1
  43.8 68.9 all-reduce.2
  122.3 61.1 reduce-scatter.5
  185.8 18.3 reduce-scatter.9
  206.5 19.4 reduce-scatter.7
where the time goes:
time: 234 us
  waiting for transfers between devices  158 us (68%)
  blocking collectives  32.1 us (14%)
  between operations  14.7 us (6%)
  local copies, waits for them, and re-layouts  11.7 us (5%)
  matrix products  7.53 us (3%)
  starting transfers between devices  6.57 us (3%)
  other arithmetic  3.77 us (2%)
    psum x1, waiting for transfers between devices, per_device(): lax.psum(jnp.dot(gated, w_out, preferred_element_type=jnp.float32), 'expe...  68.8 us
    reduce_scatter x1, waiting for transfers between devices, per_device(): lax.psum_scatter(numerator, 'expert', scatter_dimension=1, tiled=True)  39.3 us
    reduce_scatter x1, waiting for transfers between devices, per_device(): lax.psum_scatter(numerator, 'dp', scatter_dimension=0, tiled=True)  21.1 us
    unnamed x6, waiting for transfers between devices  20.7 us
    unnamed x1, blocking collectives  19.8 us
    all_gather x1, waiting for transfers between devices, per_device(): lax.all_gather(w_qkvz, 'dp', axis=0, tiled=True)  7.75 us
    all_gather x1, blocking collectives, per_device(): lax.all_gather(w_ba, 'dp', axis=0, tiled=True)  6.49 us
    all_gather x1, blocking collectives, per_device(): every_row = lax.all_gather(normed_moe, 'dp', axis=0, tiled=True)  5.79 us
  transfers between devices with their start and end apart: 7, of which 5 were waited for; matrix products, arithmetic and copies ran while one was open for 5% of the time, Pallas kernels for 0%

commit v1 on v0

v1 whole, which is shorter than its diff:
```python
import jax
import jax.numpy as jnp
from jax import lax
from jax.sharding import PartitionSpec as P

DK = 128
DV = 128
MOE_FF = 256

EPS = 1e-06
BF = jnp.bfloat16
F32 = jnp.float32


def swap_with(value, axis, offset):
    pairs = [(source, source ^ offset) for source in range(lax.axis_size(axis))]
    return lax.ppermute(value, axis, pairs)


def unit_rows(values):
    return values * lax.rsqrt(jnp.sum(values * values, axis=-1, keepdims=True) + EPS)


def per_device(
    hidden,
    states,
    migration,
    routes,
    w_qkvz,
    w_ba,
    a_log,
    dt_bias,
    attn_gain,
    head_gain,
    w_out,
    moe_gain,
    w_router,
    w_gate_up,
    w_down,
):
    groups = lax.axis_size("dp")
    members = lax.axis_size("expert")
    group = lax.axis_index("dp")
    member = lax.axis_index("expert")
    rows, width = hidden.shape
    depth = w_qkvz.shape[0]
    piece = width // members
    total_rows = routes.shape[0]
    head_state = states[:, 0]

    other_qk = swap_with(w_qkvz[:, :DK], "expert", 1)
    slices = []
    for i in range(groups):
        part = lax.dynamic_slice_in_dim(hidden, (group ^ i) * depth, depth, 1)
        slices.append(part if i == 0 else swap_with(part, "dp", i))
    gain_slice = lax.dynamic_slice_in_dim(attn_gain, group * depth, depth, 0)
    scaled = (jnp.concatenate(slices, axis=0).astype(F32) * gain_slice).astype(BF)

    leave_count = migration.shape[0] // groups
    mine = lax.dynamic_slice_in_dim(migration, group * leave_count, leave_count)
    to_group = mine[None, :, 2] == jnp.arange(groups)[:, None]
    slot_for = jnp.sum(jnp.where(to_group, mine[None, :, 1], 0), axis=1)
    received = lax.all_to_all(
        head_state[slot_for], "dp", split_axis=0, concat_axis=0, tiled=True
    )
    target = jnp.where(migration[:, 2] == group, migration[:, 3], rows)
    head_state = head_state.at[target].set(received[migration[:, 0]], mode="drop")

    partial = jnp.concatenate(
        [
            jnp.dot(scaled, w_qkvz, preferred_element_type=F32),
            jnp.dot(scaled, other_qk, preferred_element_type=F32),
            jnp.pad(jnp.dot(scaled, w_ba, preferred_element_type=F32), ((0, 0), (0, 126))),
        ],
        axis=1,
    )
    summed = partial[:rows]
    for i in range(1, groups):
        summed = summed + swap_with(partial[i * rows : (i + 1) * rows], "dp", i)
    hidden_f32 = hidden.astype(F32)
    scale = lax.rsqrt(jnp.mean(hidden_f32 * hidden_f32, axis=-1, keepdims=True) + EPS)
    projected = (summed * scale).astype(BF).astype(F32)

    own_qk = projected[:, :DK]
    values = projected[:, DK : DK + DV]
    out_gate = projected[:, DK + DV : DK + 2 * DV]
    other = projected[:, DK + 2 * DV : 2 * DK + 2 * DV]
    mix_values = projected[:, 2 * DK + 2 * DV :]
    first = jnp.where(member % 2 == 0, own_qk, other)
    second = jnp.where(member % 2 == 0, other, own_qk)
    half = DK // 2
    queries = unit_rows(jnp.concatenate([first[:, :half], second[:, :half]], axis=1)) * DK ** (-0.5)
    keys_unit = unit_rows(jnp.concatenate([first[:, half:], second[:, half:]], axis=1))
    beta_gate = jax.nn.sigmoid(mix_values[:, 0:1])
    decay_rate = jnp.exp(-jnp.exp(a_log[0]) * jax.nn.softplus(mix_values[:, 1:2] + dt_bias[0]))
    key_sum = jnp.sum(keys_unit[:, :, None] * head_state, axis=1)
    query_sum = jnp.sum(queries[:, :, None] * head_state, axis=1)
    correction = (values - key_sum * decay_rate) * beta_gate
    overlap = jnp.sum(queries * keys_unit, axis=1, keepdims=True)
    readout = query_sum * decay_rate + overlap * correction
    normed = readout * lax.rsqrt(jnp.mean(readout * readout, axis=-1, keepdims=True) + EPS)
    gated = (normed * head_gain * jax.nn.silu(out_gate)).astype(BF)

    attention = jnp.dot(gated, w_out, preferred_element_type=F32).astype(BF)
    attention = jnp.transpose(attention.reshape(rows, members, piece), (1, 0, 2))
    attention = lax.all_to_all(attention, "expert", split_axis=0, concat_axis=0, tiled=True)
    own_hidden = lax.dynamic_slice_in_dim(hidden, member * piece, piece, 1)
    residual = own_hidden.astype(F32) + jnp.sum(attention.astype(F32), axis=0)

    own_gain = lax.dynamic_slice_in_dim(moe_gain, member * piece, piece, 0)
    gained = (residual * own_gain).astype(BF)
    devices = groups * members
    every = lax.all_to_all(
        jnp.broadcast_to(gained[None], (devices, rows, piece)),
        ("dp", "expert"),
        split_axis=0,
        concat_axis=0,
        tiled=True,
    )
    every = every.reshape(groups, members, rows, piece)
    every = jnp.transpose(every, (0, 2, 1, 3)).reshape(total_rows, width)
    ungained = every.astype(F32) / moe_gain
    scale = lax.rsqrt(jnp.mean(ungained * ungained, axis=-1, keepdims=True) + EPS)
    logits = jnp.dot(every, w_router, preferred_element_type=F32) * scale
    gate_up = jnp.dot(every, w_gate_up[0], preferred_element_type=F32) * scale
    hidden_act = (jax.nn.silu(gate_up[:, :MOE_FF]) * gate_up[:, MOE_FF:]).astype(BF)
    output = jnp.dot(hidden_act, w_down[0], preferred_element_type=F32)
    expert_index = group * members + member
    hit = jnp.any(routes == expert_index, axis=1, keepdims=True)
    weight = jnp.where(hit, jnp.exp(logits), 0.0)
    weighted = (weight * output).astype(BF)

    weighted = jnp.transpose(weighted.reshape(groups, rows, members, piece), (0, 2, 1, 3))
    weighted = weighted.reshape(devices, rows * piece)
    high = weight.astype(BF)
    low = (weight - high.astype(F32)).astype(BF)
    tail = jnp.concatenate([high.reshape(groups, 1, rows), low.reshape(groups, 1, rows)], axis=2)
    tail = jnp.broadcast_to(tail, (groups, members, 2 * rows)).reshape(devices, 2 * rows)
    tail = jnp.pad(tail, ((0, 0), (0, 1024 - 2 * rows)))
    sent = jnp.concatenate([weighted, tail], axis=1).reshape(devices, -1, 128)
    back = lax.all_to_all(sent, ("dp", "expert"), split_axis=0, concat_axis=0, tiled=True)
    back = jnp.sum(back.reshape(devices, -1).astype(F32), axis=0)
    numerator = back[: rows * piece].reshape(rows, piece)
    denominator = back[rows * piece : rows * piece + rows] + back[rows * piece + rows : rows * piece + 2 * rows]
    return (residual + numerator / denominator[:, None]).astype(BF)


def solution(mesh):
    placed = (
        P(("parts", "dp"), None),
        P(("parts", "dp"), "expert", None, None),
        P("parts", None),
        P("parts", None),
        P("dp", "expert"),
        P("dp", "expert"),
        P("expert"),
        P("expert"),
        P(),
        P(),
        P("expert", None),
        P(),
        P(None, ("dp", "expert")),
        P(("dp", "expert"), None, None),
        P(("dp", "expert"), None, None),
    )
    return jax.shard_map(
        per_device,
        mesh=mesh,
        in_specs=placed,
        out_specs=P(("parts", "dp"), "expert"),
        check_vma=False,
    )
```

time: 234 us -> 80.4 us (0.34)
  waiting for transfers between devices: 158 us -> 19.3 us
  blocking collectives: 32.1 us -> 14.2 us
  between operations: 14.7 us -> 1.62 us
  starting transfers between devices: 6.57 us -> 17.8 us
  other arithmetic: 3.77 us -> 6.56 us
    psum x1 -> x0, waiting for transfers between devices: 68.8 us -> none  [per_device(): lax.psum(jnp.dot(gated, w_out, preferred_element_type=jnp.float32), 'expe...]
    reduce_scatter x2 -> x0, waiting for transfers between devices: 60.4 us -> none  [the longest x1 39.3 us: per_device(): lax.psum_scatter(numerator, 'expert', scatter_dimension=1, tiled=True)]
    unnamed x6 -> x0, waiting for transfers between devices: 20.7 us -> none
    unnamed x1 -> x0, blocking collectives: 19.8 us -> none
    all_to_all x1 -> x3, waiting for transfers between devices: 0.01 us -> 17.4 us  [the longest x1 10.6 us: per_device(): lax.all_to_all(jnp.broadcast_to(gained[None], (devices, rows, piece)), ('...]
    all_to_all x0 -> x1, blocking collectives: none -> 14.2 us  [per_device(): lax.all_to_all(sent, ('dp', 'expert'), split_axis=0, concat_axis=0, tiled...]
    all_gather x2 -> x0, blocking collectives: 12.3 us -> none  [the longest x1 6.49 us: per_device(): lax.all_gather(w_ba, 'dp', axis=0, tiled=True)]
    all_gather x1 -> x0, waiting for transfers between devices: 7.75 us -> none  [per_device(): lax.all_gather(w_qkvz, 'dp', axis=0, tiled=True)]
  transfers between devices with their start and end apart: 7 -> 10, of which waited for: 5 -> 3; matrix products, arithmetic and copies ran while one was open for 5% -> 15% of each run, Pallas kernels for 0% -> 0%
where the time goes in v1:
time: 80.4 us; the launch traced here: 79.7 us
  waiting for transfers between devices  19.3 us (24%)
  starting transfers between devices  17.8 us (22%)
  blocking collectives  14.2 us (18%)
  local copies, waits for them, and re-layouts  13.6 us (17%)
  other arithmetic  6.56 us (8%)
  matrix products  6.52 us (8%)
  between operations  1.62 us (2%)
    all_to_all x1, blocking collectives, per_device(): lax.all_to_all(sent, ('dp', 'expert'), split_axis=0, concat_axis=0, tiled...  14.2 us
    all_to_all x1, waiting for transfers between devices, per_device(): lax.all_to_all(jnp.broadcast_to(gained[None], (devices, rows, piece)), ('...  10.6 us
    ppermute x7, starting transfers between devices, swap_with(): return lax.ppermute(value, axis, pairs)  6.94 us
    all_to_all x1, waiting for transfers between devices, per_device(): lax.all_to_all(attention, 'expert', split_axis=0, concat_axis=0, tiled=True)  6.82 us
    all_to_all x1, starting transfers between devices, per_device(): lax.all_to_all(attention, 'expert', split_axis=0, concat_axis=0, tiled=True)  4.87 us
    all_to_all x1, starting transfers between devices, per_device(): lax.all_to_all(head_state[slot_for], 'dp', split_axis=0, concat_axis=0, t...  3.4 us
    unnamed x24, local copies, waits for them, and re-layouts  2.85 us
    all_to_all x1, starting transfers between devices, per_device(): lax.all_to_all(jnp.broadcast_to(gained[None], (devices, rows, piece)), ('...  2.58 us
  transfers between devices with their start and end apart: 10, of which 3 were waited for; matrix products, arithmetic and copies ran while one was open for 15% of the time, Pallas kernels for 0%

profile of v1, /device:TPU:0, one launch (start us, length us, event | category | flops | bytes accessed | tf_op | source)
XLA Modules:
  0.0 79.7 jit_solution(12953097513891510098)
XLA Ops:
  0.0 1.4 %copy.37 = f32[16,1,128,128]{3,2,1,0:T(8,128)S(1)} copy(f32[16,1,128,128]{3,2,1,0:T(8,128)} %param.16) | data formatting | bytes 2097152
  1.4 0.6 constant_dynamic-slice_fusion.4
  2.0 2.4 %collective-permute-start.2 = (bf16[16,512]{1,0:T(8,128)(2,1)}, bf16[16,512]{1,0:T(8,128)(2,1)S(1)}, u32[]{:S(2)}, u32[]{:S(2)}) collective-permute-start(bf16[16,512]{1,0:T(8,128)(2,1)} %get-tuple-element.20), channel_id=1, source_target_pairs={{0,24},{8,16},{16,8},{24,0},{1,25},{9,17},{17,9},{25,1},{2,26},{10... | collective-permute-start | bytes 49160 | tf_op jit(solution)/shard_map/ppermute | solution.py:17
  5.1 1.6 %slice.82 = bf16[512,128]{1,0:T(8,128)(2,1)} slice(bf16[512,384]{1,0:T(8,128)(2,1)} %param.19), slice={[0:512], [0:128]} | slice | bytes 262144 | tf_op jit(solution)/shard_map/slice | solution.py:51
  6.6 1.8 %collective-permute-start.3 = (bf16[512,128]{1,0:T(8,128)(2,1)}, bf16[512,128]{1,0:T(8,128)(2,1)}, u32[]{:S(2)}, u32[]{:S(2)}) collective-permute-start(bf16[512,128]{1,0:T(8,128)(2,1)} %slice.82), channel_id=1, source_target_pairs={{0,1},{1,0},{2,3},{3,2},{4,5},{5,4},{6,7},{7,6},{8,9},{9,8},{10,11... | collective-permute-start | bytes 393224 | tf_op jit(solution)/shard_map/ppermute | solution.py:17
  8.6 1.3 %gather_fusion = f32[4,128,128]{2,1,0:T(8,128)} fusion(f32[16,128,128]{2,1,0:T(8,128)S(1)} %bitcast.67, s32[1024]{0:T(1024)S(1)} %pad_clamp_fusion.1), kind=kCustom, calls=%fused_computation | custom fusion | bytes 524304 | tf_op jit(solution)/shard_map/gather | solution.py:64
  9.9 3.4 %all-to-all-start = ((f32[4,128,128]{2,1,0:T(8,128)}), f32[4,128,128]{2,1,0:T(8,128)S(1)}, u32[]{:S(2)}, u32[]{:S(2)}) async-start(f32[4,128,128]{2,1,0:T(8,128)} %gather_fusion), calls=%async_computation | async-start | bytes 524288 | tf_op jit(solution)/shard_map/all_to_all | solution.py:63
  13.4 1.4 %fusion.35 = (s32[16]{0:T(128)S(1)}, s32[16]{0:T(128)}) fusion(s32[16,4]{0,1:T(4,128)} %param.17, s32[]{:T(128)S(6)} %axis_index.25), kind=kLoop, calls=%fused_computation.86 | loop fusion | flops 128 | bytes 324 | tf_op jit(solution)/shard_map/select_n | solution.py:67
  15.4 0.8 dynamic_slice.29
  16.2 1.2 %fusion.41 = f32[64,384]{1,0:T(8,128)S(1)} fusion(bf16[512,384]{1,0:T(8,128)(2,1)} %param.19, bf16[16,512]{1,0:T(8,128)(2,1)S(1)} %collective-permute-done.2, bf16[16,512]{1,0:T(8,128)(2,1)S(1)} %collective-permute-done.1, bf16[16,512]{1,0:T(8,128)(2,1)S(1)} %collective-permute-done, bf16[16,512]{1,0:T(8,128)(2,1)S(1)} %get-tuple-element.17, ...), kind=kOutput, calls=%fused_computation.100 | convolution fusion | flops 25493504 | bytes 559104 | tf_op jit(solution)/shard_map/dot_general | solution.py:71
  17.4 0.8 %fusion.39 = f32[64,2]{1,0:T(8,128)S(1)} fusion(bf16[512,2]{0,1:T(2,128)(2,1)} %param.20, bf16[16,512]{1,0:T(8,128)(2,1)S(1)} %collective-permute-done.2, bf16[16,512]{1,0:T(8,128)(2,1)S(1)} %collective-permute-done.1, bf16[16,512]{1,0:T(8,128)(2,1)S(1)} %collective-permute-done, bf16[16,512]{1,0:T(8,128)(2,1)S(1)} %get-tuple-element.17, ...), kind=kOutput, calls=%fused_computation.98 | convolution fusion | flops 458752 | bytes 70144 | tf_op jit(solution)/shard_map/dot_general | solution.py:73
  18.2 1.1 %fusion.40 = f32[64,128]{1,0:T(8,128)S(1)} fusion(bf16[512,128]{1,0:T(8,128)(2,1)} %collective-permute-done.3, bf16[16,512]{1,0:T(8,128)(2,1)S(1)} %collective-permute-done.2, bf16[16,512]{1,0:T(8,128)(2,1)S(1)} %collective-permute-done.1, bf16[16,512]{1,0:T(8,128)(2,1)S(1)} %collective-permute-done, bf16[16,512]{1,0:T(8,128)(2,1)S(1)} %get-tuple-element.17, ...), kind=kOutput, calls=%fused_computation.99 | convolution fusion | flops 8716288 | bytes 231424 | tf_op jit(solution)/shard_map/dot_general | solution.py:72
  19.3 0.7 copy-done.1
  19.9 0.7 fusion.43
  20.6 1.7 %collective-permute-start.6 = (f32[16,640]{1,0:T(8,128)}, f32[16,640]{1,0:T(8,128)S(1)}, u32[]{:S(2)}, u32[]{:S(2)}) collective-permute-start(f32[16,640]{1,0:T(8,128)} %get-tuple-element.15), channel_id=1, source_target_pairs={{0,24},{8,16},{16,8},{24,0},{1,25},{9,17},{17,9},{25,1},{2,26},{10... | collective-permute-start | bytes 122888 | tf_op jit(solution)/shard_map/ppermute | solution.py:17
  22.7 0.6 pad_clamp_fusion
  24.7 1.9 %collective-permute-done.5 = f32[16,640]{1,0:T(8,128)S(1)} collective-permute-done((f32[16,640]{1,0:T(8,128)}, f32[16,640]{1,0:T(8,128)S(1)}, u32[]{:S(2)}, u32[]{:S(2)}) %collective-permute-start.5) | collective-permute-done | bytes 40992 | tf_op jit(solution)/shard_map/ppermute | solution.py:17
  26.6 0.6 copy-done.3
  27.2 0.9 %fusion.20 = f32[16,640]{1,0:T(8,128)S(1)} fusion(f32[16,640]{1,0:T(8,128)S(1)} %collective-permute-done.6, f32[16,640]{1,0:T(8,128)} %copy-done.3, f32[16,640]{1,0:T(8,128)} %collective-permute-done.4, f32[64,640]{1,0:T(8,128)} %copy-done.1, f32[16]{0:T(128)} %add_rsqrt_fusion.4), kind=kLoop, calls=%fused_computation.37 | loop fusion | flops 61440 | bytes 204864 | tf_op jit(solution)/shard_map/convert_element_type | solution.py:82
  29.0 1.7 %gather_fusion.1 = f32[16,128,128]{2,1,0:T(8,128)} fusion(f32[4,128,128]{2,1,0:T(8,128)S(1)} %all-to-all-done, s32[1024]{0:T(1024)} %pad_clamp_fusion), kind=kCustom, calls=%fused_computation.1 | custom fusion | bytes 2097216 | tf_op jit(solution)/shard_map/gather | solution.py:67
  30.7 2.3 %scatter_fusion = f32[16,128,128]{2,1,0:T(8,128)S(1)} fusion(f32[16,128,128]{2,1,0:T(8,128)S(1)} %bitcast.68, s32[16]{0:T(128)S(1)} %copy-done.7, f32[16,128,128]{2,1,0:T(8,128)} %gather_fusion.1), kind=kCustom, calls=%fused_computation.2 | custom fusion | bytes 3145792 | tf_op jit(solution)/shard_map/scatter | solution.py:67
  33.0 0.7 multiply_reduce_fusion.1
  33.9 1.3 %convolution_convert_fusion = bf16[16,2048]{1,0:T(8,128)(2,1)S(1)} fusion(bf16[128,2048]{1,0:T(8,128)(2,1)} %param.25, f32[16,640]{1,0:T(8,128)S(1)} %fusion.20, f32[16,128]{1,0:T(8,128)S(1)} %get-tuple-element.10, f32[128]{0:T(128)S(1)} %copy-done.8, f32[16]{0:T(128)S(1)} %add_rsqrt_fusion.1), kind=kOutput, calls=%fused_computation.5 | convolution fusion | flops 8437760 | bytes 607232 | tf_op jit(solution)/shard_map/dot_general | solution.py:104
  35.2 0.6 copy.32
  35.8 4.9 %all-to-all-start.1 = ((bf16[8,16,256]{2,1,0:T(8,128)(2,1)}), bf16[8,16,256]{2,1,0:T(8,128)(2,1)S(1)}, u32[]{:S(2)}, u32[]{:S(2)}) async-start(bf16[8,16,256]{2,1,0:T(8,128)(2,1)} %bitcast.65), calls=%async_computation.1 | async-start | bytes 131072 | tf_op jit(solution)/shard_map/all_to_all | solution.py:106
  40.8 6.8 %all-to-all-done.1 = bf16[8,16,256]{2,1,0:T(8,128)(2,1)S(1)} async-done(((bf16[8,16,256]{2,1,0:T(8,128)(2,1)}), bf16[8,16,256]{2,1,0:T(8,128)(2,1)S(1)}, u32[]{:S(2)}, u32[]{:S(2)}) %all-to-all-start.1) | async-done | bytes 65568 | tf_op jit(solution)/shard_map/all_to_all | solution.py:106
  47.7 0.7 broadcast_in_dim.31
  48.4 2.6 %all-to-all-start.2 = ((bf16[32,16,256]{2,1,0:T(8,128)(2,1)}), bf16[32,16,256]{2,1,0:T(8,128)(2,1)S(1)}, u32[]{:S(2)}, u32[]{:S(2)}) async-start(bf16[32,16,256]{2,1,0:T(8,128)(2,1)} %broadcast_in_dim.31), calls=%async_computation.2 | async-start | bytes 524288 | tf_op jit(solution)/shard_map/all_to_all | solution.py:113
  51.0 10.6 %all-to-all-done.2 = bf16[32,16,256]{2,1,0:T(8,128)(2,1)S(1)} async-done(((bf16[32,16,256]{2,1,0:T(8,128)(2,1)}), bf16[32,16,256]{2,1,0:T(8,128)(2,1)S(1)}, u32[]{:S(2)}, u32[]{:S(2)}) %all-to-all-start.2) | async-done | bytes 262176 | tf_op jit(solution)/shard_map/all_to_all | solution.py:113
  63.0 1.5 %fusion = bf16[64,2048]{1,0:T(8,128)(2,1)S(1)} fusion(bf16[1,256,2048]{2,1,0:T(8,128)(2,1)} %param.29, f32[64]{0:T(128)S(1)} %get-tuple-element.33, f32[64,512]{1,0:T(8,128)S(1)} %fusion.3), kind=kOutput, calls=%fused_computation.4 | convolution fusion | flops 67469312 | bytes 1442048 | tf_op jit(solution)/shard_map/dot_general | solution.py:127
  64.6 14.2 %all_to_all.20 = bf16[32,40,128]{2,1,0:T(8,128)(2,1)S(1)} all-to-all(bf16[32,40,128]{2,1,0:T(8,128)(2,1)S(1)} %bitcast.71), channel_id=1, replica_groups=mesh['parts'=1,'dp'=4,'expert'=8] {'dp','expert'}, dimensions={0} | all-to-all | bytes 655360 | tf_op jit(solution)/shard_map/all_to_all | solution.py:141
  79.0 0.7 add_convert_fusion
  (70 shorter events, 4.8 us)
Async XLA Ops:
  0.0 62.5 %copy-start = (bf16[1,2048,512]{2,1,0:T(8,128)(2,1)S(1)}, bf16[1,2048,512]{2,1,0:T(8,128)(2,1)}, u32[]{:S(2)}) copy-start(bf16[1,2048,512]{2,1,0:T(8,128)(2,1)} %param.28) | copy-start | bytes 6291460
  0.0 1.4 %copy-start.2 = (bf16[16,2048]{1,0:T(8,128)(2,1)S(1)}, bf16[16,2048]{1,0:T(8,128)(2,1)}, u32[]{:S(2)}) copy-start(bf16[16,2048]{1,0:T(8,128)(2,1)} %param.15) | copy-start | bytes 196612
  0.0 8.4 %copy-start.6 = (s32[16,4]{0,1:T(4,128)S(1)}, s32[16,4]{0,1:T(4,128)}, u32[]{:S(2)}) copy-start(s32[16,4]{0,1:T(4,128)} %param.17) | copy-start | bytes 772
  2.0 14.2 %collective-permute-start.2 = (bf16[16,512]{1,0:T(8,128)(2,1)}, bf16[16,512]{1,0:T(8,128)(2,1)S(1)}, u32[]{:S(2)}, u32[]{:S(2)}) collective-permute-start(bf16[16,512]{1,0:T(8,128)(2,1)} %get-tuple-element.20), channel_id=1, source_target_pairs={{0,24},{8,16},{16,8},{24,0},{1,25},{9,17},{17,9},{25,1},{2,26},{10... | collective-permute-start | bytes 49160 | tf_op jit(solution)/shard_map/ppermute | solution.py:17
  4.4 11.8 %collective-permute-start.1 = (bf16[16,512]{1,0:T(8,128)(2,1)}, bf16[16,512]{1,0:T(8,128)(2,1)S(1)}, u32[]{:S(2)}, u32[]{:S(2)}) collective-permute-start(bf16[16,512]{1,0:T(8,128)(2,1)} %get-tuple-element.18), channel_id=1, source_target_pairs={{0,16},{8,24},{16,0},{24,8},{1,17},{9,25},{17,1},{25,9},{2,18},{10... | collective-permute-start | bytes 49160 | tf_op jit(solution)/shard_map/ppermute | solution.py:17
  5.0 11.2 %collective-permute-start = (bf16[16,512]{1,0:T(8,128)(2,1)S(1)}, bf16[16,512]{1,0:T(8,128)(2,1)S(1)}, u32[]{:S(2)}, u32[]{:S(2)}) collective-permute-start(bf16[16,512]{1,0:T(8,128)(2,1)S(1)} %get-tuple-element.19), channel_id=1, source_target_pairs={{0,8},{8,0},{16,24},{24,16},{1,9},{9,1},{17,25},{25,17},{2,10},{10... | collective-permute-start | bytes 49160 | tf_op jit(solution)/shard_map/ppermute | solution.py:17
  6.6 11.6 %collective-permute-start.3 = (bf16[512,128]{1,0:T(8,128)(2,1)}, bf16[512,128]{1,0:T(8,128)(2,1)}, u32[]{:S(2)}, u32[]{:S(2)}) collective-permute-start(bf16[512,128]{1,0:T(8,128)(2,1)} %slice.82), channel_id=1, source_target_pairs={{0,1},{1,0},{2,3},{3,2},{4,5},{5,4},{6,7},{7,6},{8,9},{9,8},{10,11... | collective-permute-start | bytes 393224 | tf_op jit(solution)/shard_map/ppermute | solution.py:17
  9.9 19.1 %all-to-all-start = ((f32[4,128,128]{2,1,0:T(8,128)}), f32[4,128,128]{2,1,0:T(8,128)S(1)}, u32[]{:S(2)}, u32[]{:S(2)}) async-start(f32[4,128,128]{2,1,0:T(8,128)} %gather_fusion), calls=%async_computation | async-start | bytes 524288 | tf_op jit(solution)/shard_map/all_to_all | solution.py:63
  19.3 0.7 copy-start.1
  20.6 4.1 %collective-permute-start.6 = (f32[16,640]{1,0:T(8,128)}, f32[16,640]{1,0:T(8,128)S(1)}, u32[]{:S(2)}, u32[]{:S(2)}) collective-permute-start(f32[16,640]{1,0:T(8,128)} %get-tuple-element.15), channel_id=1, source_target_pairs={{0,24},{8,16},{16,8},{24,0},{1,25},{9,17},{17,9},{25,1},{2,26},{10... | collective-permute-start | bytes 122888 | tf_op jit(solution)/shard_map/ppermute | solution.py:17
  22.4 4.2 %collective-permute-start.5 = (f32[16,640]{1,0:T(8,128)}, f32[16,640]{1,0:T(8,128)S(1)}, u32[]{:S(2)}, u32[]{:S(2)}) collective-permute-start(f32[16,640]{1,0:T(8,128)} %get-tuple-element.16), channel_id=1, source_target_pairs={{0,16},{8,24},{16,0},{24,8},{1,17},{9,25},{17,1},{25,9},{2,18},{10... | collective-permute-start | bytes 122888 | tf_op jit(solution)/shard_map/ppermute | solution.py:17
  22.7 4.5 %collective-permute-start.4 = (f32[16,640]{1,0:T(8,128)}, f32[16,640]{1,0:T(8,128)}, u32[]{:S(2)}, u32[]{:S(2)}) collective-permute-start(f32[16,640]{1,0:T(8,128)} %get-tuple-element.14), channel_id=1, source_target_pairs={{0,8},{8,0},{16,24},{24,16},{1,9},{9,1},{17,25},{25,17},{2,10},{10... | collective-permute-start | bytes 122888 | tf_op jit(solution)/shard_map/ppermute | solution.py:17
  26.6 0.6 copy-start.3
  28.1 2.6 %copy-start.7 = (s32[16]{0:T(128)S(1)}, s32[16]{0:T(128)}, u32[]{:S(2)}) copy-start(s32[16]{0:T(128)} %get-tuple-element.28) | copy-start | bytes 196
  30.7 3.2 %copy-start.8 = (f32[128]{0:T(128)S(1)}, f32[128]{0:T(128)}, u32[]{:S(2)}) copy-start(f32[128]{0:T(128)} %param.24) | copy-start | bytes 1540
  30.7 10.0 %copy-start.4 = (f32[2048]{0:T(1024)S(1)}, f32[2048]{0:T(1024)}, u32[]{:S(2)}) copy-start(f32[2048]{0:T(1024)} %param.26) | copy-start | bytes 24580
  33.0 18.0 %copy-start.5 = (s32[64,10]{0,1:T(8,128)S(1)}, s32[64,10]{0,1:T(8,128)}, u32[]{:S(2)}) copy-start(s32[64,10]{0,1:T(8,128)} %param.18) | copy-start | bytes 7684
  33.0 29.0 %copy-start.9 = (bf16[2048,1]{0,1:T(2,128)(2,1)S(1)}, bf16[2048,1]{0,1:T(2,128)(2,1)}, u32[]{:S(2)}) copy-start(bf16[2048,1]{0,1:T(2,128)(2,1)} %param.27) | copy-start | bytes 12292
  35.8 11.8 %all-to-all-start.1 = ((bf16[8,16,256]{2,1,0:T(8,128)(2,1)}), bf16[8,16,256]{2,1,0:T(8,128)(2,1)S(1)}, u32[]{:S(2)}, u32[]{:S(2)}) async-start(bf16[8,16,256]{2,1,0:T(8,128)(2,1)} %bitcast.65), calls=%async_computation.1 | async-start | bytes 131072 | tf_op jit(solution)/shard_map/all_to_all | solution.py:106
  48.4 13.2 %all-to-all-start.2 = ((bf16[32,16,256]{2,1,0:T(8,128)(2,1)}), bf16[32,16,256]{2,1,0:T(8,128)(2,1)S(1)}, u32[]{:S(2)}, u32[]{:S(2)}) async-start(bf16[32,16,256]{2,1,0:T(8,128)(2,1)} %broadcast_in_dim.31), calls=%async_computation.2 | async-start | bytes 524288 | tf_op jit(solution)/shard_map/all_to_all | solution.py:113

commit v2 on v1

v2 whole, which is shorter than its diff:
```python
import functools

import jax
import jax.numpy as jnp
from jax import lax
from jax.experimental import pallas as pl
from jax.experimental.pallas import tpu as pltpu
from jax.sharding import PartitionSpec as P

DK = 128
DV = 128
MOE_FF = 256
LANES = 128
SENT = 2 * DK + 2 * DV + LANES

EPS = 1e-06
BF = jnp.bfloat16
F32 = jnp.float32

VMEM = pl.BlockSpec(memory_space=pltpu.VMEM)
SMEM = pl.BlockSpec(memory_space=pltpu.SMEM)
HBM = pl.BlockSpec(memory_space=pltpu.HBM)
ANY = pl.BlockSpec(memory_space=pl.ANY)
COST = pl.CostEstimate(flops=0, bytes_accessed=8 * 1024 * 1024, transcendentals=0)
PARAMS = pltpu.CompilerParams(vmem_limit_bytes=24 * 1024 * 1024)


def in_hbm(*values):
    return [pltpu.with_memory_space_constraint(value, pltpu.HBM) for value in values]


def copy_all(pairs, sems):
    copies = [pltpu.make_async_copy(a, b, sems.at[i]) for i, (a, b) in enumerate(pairs)]
    for copy in copies:
        copy.start()
    return copies


def swap_with(value, axis, offset):
    pairs = [(source, source ^ offset) for source in range(lax.axis_size(axis))]
    return lax.ppermute(value, axis, pairs)


def row_scale(values):
    return lax.rsqrt(jnp.mean(values * values, axis=-1, keepdims=True) + EPS)


def unit_rows(values):
    return values * lax.rsqrt(jnp.sum(values * values, axis=-1, keepdims=True) + EPS)


def group_index():
    return lax.axis_index("x") * lax.axis_size("core") + lax.axis_index("core")


def pieces_kernel(groups, hidden, w_qkvz, *refs):
    own_qk, pieces, sems = refs[0], refs[1:-1], refs[-1]
    group = group_index()
    depth = w_qkvz.shape[0]
    pairs = [(w_qkvz.at[:, pl.ds(0, DK)], own_qk)]
    for i in range(1, groups):
        first = pl.multiple_of((group ^ i) * depth, depth)
        pairs.append((hidden.at[:, pl.ds(first, depth)], pieces[i - 1]))
    for copy in copy_all(pairs, sems):
        copy.wait()


def leaving_kernel(groups, leave_count, migration, states, early, *refs):
    count = (len(refs) - groups - 3) // 2
    sources, leaving, staged = refs[:count], refs[count : count + groups], refs[count + groups : -3]
    plan, plan_sem, sems = refs[-3:]
    del early
    plan_copy = pltpu.make_async_copy(migration, plan, plan_sem)
    plan_copy.start()
    copies = copy_all(list(zip(sources, staged)), sems)
    group = group_index()
    plan_copy.wait()
    for i in range(groups):
        slot = 0
        for j in range(leave_count):
            at = group * leave_count + j
            slot = jnp.where(plan[2, at] == (group ^ i), plan[1, at], slot)
        copy = pltpu.make_async_copy(states.at[slot, 0], leaving[i], sems.at[count + i])
        copy.start()
        copies.append(copy)
    for copy in copies:
        copy.wait()


def project_kernel(groups, hidden, gain, w_ba, w_qkvz, other_qk, *refs):
    pieces, outs, scaled = refs[: groups - 1], refs[groups - 1 : -1], refs[-1]
    group = group_index()
    depth = w_qkvz.shape[0]
    rows = hidden.shape[0]
    columns = pl.ds(pl.multiple_of(group * depth, depth), depth)
    own_gain = gain[:, columns]
    for i in range(groups):
        part = hidden[:, columns] if i == 0 else pieces[i - 1][...]
        scaled[i * rows : (i + 1) * rows, :] = (part.astype(F32) * own_gain).astype(BF)
    x = scaled[...]
    main = jnp.dot(x, w_qkvz[...], preferred_element_type=F32)
    other = jnp.dot(x, other_qk[...], preferred_element_type=F32)
    wide = x.astype(F32)
    lane = lax.broadcasted_iota(jnp.int32, (groups * rows, LANES), 1)
    mixes = jnp.zeros((groups * rows, LANES), F32)
    for j in range(2):
        total = jnp.sum(wide * w_ba[j : j + 1, :].astype(F32), axis=1, keepdims=True)
        mixes = jnp.where(lane == j, total, mixes)
    for i in range(groups):
        block = slice(i * rows, (i + 1) * rows)
        outs[i][:, : DK + 2 * DV] = main[block]
        outs[i][:, DK + 2 * DV : 2 * DK + 2 * DV] = other[block]
        outs[i][:, 2 * DK + 2 * DV :] = mixes[block]


def settle_kernel(groups, leave_count, migration, states, hidden, gain, routes, after, *refs):
    arrivals, refs = refs[:groups], refs[groups:]
    held, scale, own_hidden, own_gain, hits = refs[-8:-3]
    rest = refs[:-8]
    count = len(rest) // 2
    plan, plan_sem, sems = refs[-3:]
    del after
    plan_copy = pltpu.make_async_copy(migration, plan, plan_sem)
    plan_copy.start()
    copies = copy_all([(states.at[:, 0], held)] + list(zip(rest[:count], rest[count:])), sems)
    group = group_index()
    core = lax.axis_index("core")
    member = lax.axis_index("expert")
    rows = hidden.shape[0]
    total_rows = groups * rows
    piece = own_hidden.shape[1]
    members = hidden.shape[1] // piece
    wide = hidden[...].astype(F32)
    scale[...] = jnp.broadcast_to(row_scale(wide), scale.shape)
    own, own_g = wide[:, :piece], gain[:, :piece]
    for m in range(1, members):
        columns = slice(m * piece, (m + 1) * piece)
        own = jnp.where(member == m, wide[:, columns], own)
        own_g = jnp.where(member == m, gain[:, columns], own_g)
    own_hidden[...] = own
    own_gain[...] = own_g
    found = jnp.where(routes[...] == group * members + member, 1.0, 0.0)
    found = jnp.max(found, axis=0, keepdims=True)
    row = lax.broadcasted_iota(jnp.int32, (total_rows, total_rows), 0)
    lane = lax.broadcasted_iota(jnp.int32, (total_rows, total_rows), 1)
    block, slot = row // rows, row % rows
    source_group = 2 * (block % (groups // 2)) + (core ^ (block // (groups // 2)))
    same = lane == source_group * rows + slot
    column = jnp.sum(jnp.where(same, found, 0.0), axis=1, keepdims=True)
    hits[...] = jnp.broadcast_to(column, hits.shape)
    plan_copy.wait()
    for copy in copies:
        copy.wait()
    for i in range(groups):
        for j in range(leave_count):
            at = (group ^ i) * leave_count + j

            @pl.when(plan[2, at] == group)
            def _():
                held[plan[3, at]] = arrivals[i][...]


def delta_kernel(a_log, dt_bias, scale, head_gain, w_out, held, *refs):
    partials, (out, key_sums, query_sums) = refs[:-3], refs[-3:]
    member = lax.axis_index("expert")
    rows = held.shape[0]
    summed = partials[0][...]
    for partial in partials[1:]:
        summed = summed + partial[...]
    projected = (summed * scale[:, 0:1]).astype(BF).astype(F32)
    own_qk = projected[:, :DK]
    values = projected[:, DK : DK + DV]
    out_gate = projected[:, DK + DV : DK + 2 * DV]
    other = projected[:, DK + 2 * DV : 2 * DK + 2 * DV]
    write_mix = projected[:, 2 * DK + 2 * DV : 2 * DK + 2 * DV + 1]
    decay_mix = projected[:, 2 * DK + 2 * DV + 1 : 2 * DK + 2 * DV + 2]
    is_first = member % 2 == 0
    first = jnp.where(is_first, own_qk, other)
    second = jnp.where(is_first, other, own_qk)
    low_half = lax.broadcasted_iota(jnp.int32, (rows, DK), 1) < DK // 2
    queries = unit_rows(jnp.where(low_half, first, pltpu.roll(second, DK // 2, 1))) * DK ** (-0.5)
    keys_unit = unit_rows(jnp.where(low_half, pltpu.roll(first, DK // 2, 1), second))
    shifted = decay_mix + dt_bias[0]
    soft = jnp.maximum(shifted, 0.0) + jnp.log1p(jnp.exp(-jnp.abs(shifted)))
    decay = jnp.exp(-jnp.exp(jnp.full((rows, 1), a_log[0], F32)) * soft)
    beta = jax.nn.sigmoid(write_mix)
    keys_t = jnp.transpose(keys_unit)
    queries_t = jnp.transpose(queries)
    for r in range(rows):
        state = held[r]
        key_sums[r : r + 1, :] = jnp.sum(state * keys_t[:, r : r + 1], axis=0, keepdims=True)
        query_sums[r : r + 1, :] = jnp.sum(state * queries_t[:, r : r + 1], axis=0, keepdims=True)
    correction = (values - key_sums[...] * decay) * beta
    overlap = jnp.sum(queries * keys_unit, axis=1, keepdims=True)
    readout = query_sums[...] * decay + overlap * correction
    normed = readout * row_scale(readout) * head_gain[...]
    gated = (normed * (out_gate * jax.nn.sigmoid(out_gate))).astype(BF)
    attention = jnp.dot(gated, w_out[...], preferred_element_type=F32).astype(BF)
    piece = out.shape[2]
    for m in range(out.shape[0]):
        out[m] = attention[:, m * piece : (m + 1) * piece]


def residual_kernel(attention, hidden, gain, gained, residual):
    members, rows, piece = attention.shape
    total = hidden[...]
    for m in range(members):
        total = total + attention[m].astype(F32)
    residual[...] = total
    sent = (total * gain[...]).astype(BF)
    for d in range(gained.shape[0]):
        gained[d] = sent


def packed(tile, piece):
    if piece >= LANES:
        return [tile[:, c : c + LANES] for c in range(0, piece, LANES)]
    count = LANES // piece
    part = tile.shape[0] // count
    return [jnp.concatenate([tile[c * part : (c + 1) * part] for c in range(count)], axis=1)]


def unpacked(tile, rows, piece):
    if piece >= LANES:
        return jnp.concatenate(
            [tile[c * rows : (c + 1) * rows] for c in range(piece // LANES)], axis=1
        )
    return jnp.concatenate([tile[:, c : c + piece] for c in range(0, LANES, piece)], axis=0)


def tail_of(weight):
    part = 8
    lane = lax.broadcasted_iota(jnp.int32, (part, LANES), 1)
    tail = jnp.zeros((part, LANES), F32)
    for c in range(weight.shape[0] // part):
        at = weight[c * part : (c + 1) * part]
        high = at.astype(BF).astype(F32)
        tail = jnp.where(lane == c, high, tail)
        tail = jnp.where(lane == LANES // 2 + c, at - high, tail)
    return tail


def expert_kernel(width, every, across, hits, gain, w_router, w_gate_up, w_down, out, out_across):
    devices, rows, piece = every.shape
    members = width // piece
    half = devices // members
    total_rows = 2 * half * rows
    gate_up = jnp.zeros((total_rows, 2 * MOE_FF), F32)
    squares = jnp.zeros((total_rows, piece), F32)
    routed = jnp.zeros((total_rows, piece), F32)
    inverse = 1.0 / gain[...]
    for m in range(members):
        columns = slice(m * piece, (m + 1) * piece)
        x = jnp.concatenate(
            [ref[g * members + m] for ref in (every, across) for g in range(half)], axis=0
        )
        gate_up = gate_up + jnp.dot(x, w_gate_up[0, columns, :], preferred_element_type=F32)
        wide = x.astype(F32)
        plain = wide * inverse[:, columns]
        squares = squares + plain * plain
        routed = routed + wide * w_router[:, columns].astype(F32)
    scale = lax.rsqrt(jnp.sum(squares, axis=1, keepdims=True) * (1.0 / width) + EPS)
    logits = jnp.sum(routed, axis=1, keepdims=True) * scale
    weight = jnp.where(hits[:, 0:1] > 0.0, jnp.exp(logits), 0.0)
    gate_up = gate_up * scale
    gate = gate_up[:, :MOE_FF]
    act = (gate * jax.nn.sigmoid(gate) * gate_up[:, MOE_FF:]).astype(BF)
    tails = [tail_of(weight[g * rows : (g + 1) * rows]) for g in range(2 * half)]
    step = max(piece, LANES)
    for start in range(0, width, step):
        y = jnp.dot(act, w_down[0, :, start : start + step], preferred_element_type=F32) * weight
        for m in range(step // piece):
            for g in range(2 * half):
                tile = y[g * rows : (g + 1) * rows, m * piece : (m + 1) * piece]
                target = out if g < half else out_across
                target[g % half * members + start // piece + m] = jnp.concatenate(
                    packed(tile, piece) + [tails[g]], axis=0
                ).astype(BF)


def pair_kernel(own, received, out):
    devices, height, _ = own.shape
    body = height - 8
    low_half = lax.broadcasted_iota(jnp.int32, (8, LANES), 1) < LANES // 2
    for d in range(devices):
        total = own[d].astype(F32) + received[d].astype(F32)
        tail = total[body:]
        tail = tail + pltpu.roll(tail, LANES // 2, 1)
        high = tail.astype(BF).astype(F32)
        tail = jnp.where(low_half, high, tail - high)
        out[d] = jnp.concatenate([total[:body], tail], axis=0).astype(BF)


def final_kernel(back, residual, out):
    devices, height, _ = back.shape
    rows, piece = residual.shape
    total = back[0].astype(F32)
    for d in range(1, devices):
        total = total + back[d].astype(F32)
    body = rows * piece // LANES
    numerator = unpacked(total[:body], rows, piece)
    tail = total[body:]
    tail = tail + pltpu.roll(tail, LANES // 2, 1)
    denominator = jnp.concatenate(
        [tail[:, c : c + 1] for c in range(rows // tail.shape[0])], axis=0
    )
    out[...] = (residual[...] + numerator / denominator).astype(BF)


def per_device(
    hidden,
    states,
    migration,
    routes,
    w_qkvz,
    w_ba,
    a_log,
    dt_bias,
    attn_gain,
    head_gain,
    w_out,
    moe_gain,
    w_router,
    w_gate_up,
    w_down,
):
    dp = ("x", "core")
    half = lax.axis_size("x")
    groups = half * lax.axis_size("core")
    members = lax.axis_size("expert")
    rows, width = hidden.shape
    depth = w_qkvz.shape[0]
    piece = width // members
    total_rows = routes.shape[0]
    leave_count = migration.shape[0] // groups
    plan = jnp.transpose(migration)
    shape = jax.ShapeDtypeStruct

    own_qk, *pieces = pl.pallas_call(
        functools.partial(pieces_kernel, groups),
        out_shape=[pltpu.VMEM((depth, DK), BF)] + [pltpu.VMEM((rows, depth), BF)] * (groups - 1),
        in_specs=[HBM] * 2,
        out_specs=[VMEM] * groups,
        scratch_shapes=[pltpu.SemaphoreType.DMA((groups,))],
        compiler_params=PARAMS,
        cost_estimate=COST,
        name="pieces",
    )(*in_hbm(hidden, w_qkvz))
    other_qk = swap_with(own_qk, "expert", 1)
    pieces = [swap_with(piece_i, dp, i + 1) for i, piece_i in enumerate(pieces)]
    operands = [hidden, w_qkvz, attn_gain.reshape(1, width), jnp.transpose(w_ba)]
    left = pl.pallas_call(
        functools.partial(leaving_kernel, groups, leave_count),
        out_shape=[pltpu.VMEM((DK, DV), F32)] * groups
        + [pltpu.VMEM(operand.shape, operand.dtype) for operand in operands],
        in_specs=[HBM, HBM, ANY] + [HBM] * len(operands),
        out_specs=[VMEM] * (groups + len(operands)),
        scratch_shapes=[
            pltpu.SMEM(plan.shape, jnp.int32),
            pltpu.SemaphoreType.DMA,
            pltpu.SemaphoreType.DMA((groups + len(operands),)),
        ],
        compiler_params=PARAMS,
        cost_estimate=COST,
        name="leaving",
    )(*in_hbm(plan, states), pieces[0], *in_hbm(*operands))
    leaving, (hidden_near, w_near, attn_gain_near, w_ba_near) = left[:groups], left[groups:]
    arrivals = [leaving[0]] + [swap_with(leaving[i], dp, i) for i in range(1, groups)]

    partials = pl.pallas_call(
        functools.partial(project_kernel, groups),
        out_shape=[pltpu.VMEM((rows, SENT), F32)] * groups,
        in_specs=[VMEM] * (groups + 4),
        out_specs=[VMEM] * groups,
        scratch_shapes=[pltpu.VMEM((total_rows, depth), BF)],
        compiler_params=PARAMS,
        cost_estimate=COST,
        name="project",
    )(hidden_near, attn_gain_near, w_ba_near, w_near, other_qk, *pieces)
    after = partials[0]
    partials = [partials[0]] + [swap_with(partials[i], dp, i) for i in range(1, groups)]
    operands = [
        w_out,
        head_gain.reshape(1, DV),
        moe_gain.reshape(1, width),
        jnp.transpose(w_router),
    ]
    settled = pl.pallas_call(
        functools.partial(settle_kernel, groups, leave_count),
        out_shape=[pltpu.VMEM(operand.shape, operand.dtype) for operand in operands]
        + [
            pltpu.VMEM((rows, DK, DV), F32),
            pltpu.VMEM((rows, LANES), F32),
            pltpu.VMEM((rows, piece), F32),
            pltpu.VMEM((1, piece), F32),
            pltpu.VMEM((total_rows, LANES), F32),
        ],
        in_specs=[HBM, HBM, VMEM, VMEM, VMEM, ANY] + [VMEM] * groups + [HBM] * len(operands),
        out_specs=[VMEM] * (5 + len(operands)),
        scratch_shapes=[
            pltpu.SMEM(plan.shape, jnp.int32),
            pltpu.SemaphoreType.DMA,
            pltpu.SemaphoreType.DMA((1 + len(operands),)),
        ],
        compiler_params=PARAMS,
        cost_estimate=COST,
        name="settle",
    )(
        *in_hbm(plan, states),
        hidden_near,
        *in_hbm(moe_gain.reshape(1, width), jnp.transpose(routes)),
        after,
        *arrivals,
        *in_hbm(*operands),
    )
    w_out_near, head_gain_near, moe_gain_near, router_near = settled[:-5]
    held, scale, own_hidden, own_gain, hits = settled[-5:]

    attention = pl.pallas_call(
        delta_kernel,
        out_shape=pltpu.VMEM((members, rows, piece), BF),
        in_specs=[SMEM] * 2 + [VMEM] * (4 + groups),
        out_specs=VMEM,
        scratch_shapes=[pltpu.VMEM((rows, DV), F32)] * 2,
        compiler_params=PARAMS,
        cost_estimate=COST,
        name="delta",
    )(a_log, dt_bias, scale, head_gain_near, w_out_near, held, *partials)
    attention = lax.all_to_all(attention, "expert", split_axis=0, concat_axis=0, tiled=True)

    gained, residual = pl.pallas_call(
        residual_kernel,
        out_shape=[
            pltpu.VMEM((half * members, rows, piece), BF),
            pltpu.VMEM((rows, piece), F32),
        ],
        in_specs=[VMEM] * 3,
        out_specs=[VMEM] * 2,
        compiler_params=PARAMS,
        cost_estimate=COST,
        name="residual",
    )(attention, own_hidden, own_gain)
    every = lax.all_to_all(gained, ("x", "expert"), split_axis=0, concat_axis=0, tiled=True)
    across = swap_with(every, "core", 1)

    height = rows * piece // LANES + 8
    sent, sent_across = pl.pallas_call(
        functools.partial(expert_kernel, width),
        out_shape=[pltpu.VMEM((half * members, height, LANES), BF)] * 2,
        in_specs=[VMEM] * 7,
        out_specs=[VMEM] * 2,
        compiler_params=PARAMS,
        cost_estimate=COST,
        name="experts",
    )(
        every,
        across,
        hits,
        moe_gain_near,
        router_near,
        w_gate_up,
        w_down,
    )
    sent = pl.pallas_call(
        pair_kernel,
        out_shape=pltpu.VMEM((half * members, height, LANES), BF),
        in_specs=[VMEM] * 2,
        out_specs=VMEM,
        compiler_params=PARAMS,
        cost_estimate=COST,
        name="pair",
    )(sent, swap_with(sent_across, "core", 1))
    back = lax.all_to_all(sent, ("x", "expert"), split_axis=0, concat_axis=0, tiled=True)
    return pl.pallas_call(
        final_kernel,
        out_shape=shape((rows, piece), BF),
        in_specs=[VMEM] * 2,
        out_specs=VMEM,
        compiler_params=PARAMS,
        cost_estimate=COST,
        name="finish",
    )(back, residual)


def solution(mesh):
    parts, groups, members = (mesh.shape[name] for name in ("parts", "dp", "expert"))
    devices = mesh.devices.reshape(parts, groups // 2, 2, members)
    fine = jax.sharding.Mesh(devices, ("parts", "x", "core", "expert"))
    placed = (
        P(("parts", "x", "core"), None),
        P(("parts", "x", "core"), "expert", None, None),
        P("parts", None),
        P("parts", None),
        P(("x", "core"), "expert"),
        P(("x", "core"), "expert"),
        P("expert"),
        P("expert"),
        P(),
        P(),
        P("expert", None),
        P(),
        P(None, ("x", "core", "expert")),
        P(("x", "core", "expert"), None, None),
        P(("x", "core", "expert"), None, None),
    )
    return jax.shard_map(
        per_device,
        mesh=fine,
        in_specs=placed,
        out_specs=P(("parts", "x", "core"), "expert"),
        check_vma=False,
    )
```

time: 80.4 us -> 60 us (0.75)
  blocking collectives: 14.2 us -> 33.2 us
  local copies, waits for them, and re-layouts: 13.6 us -> 0.01 us
  waiting for transfers between devices: 19.3 us -> 7.73 us
  starting transfers between devices: 17.8 us -> 8.61 us
  Pallas kernels: 0 us -> 8.65 us
  other arithmetic: 6.56 us -> 0 us
  matrix products: 6.52 us -> 0 us
    all_to_all x1 -> x3, blocking collectives: 14.2 us -> 33.2 us  [the longest x1 11.6 us: per_device(): lax.all_to_all(attention, 'expert', split_axis=0, concat_axis=0, tiled=True)]
    all_to_all x3 -> x0, waiting for transfers between devices: 17.4 us -> none  [the longest x1 10.6 us: per_device(): lax.all_to_all(jnp.broadcast_to(gained[None], (devices, rows, piece)), ('...]
    all_to_all x3 -> x0, starting transfers between devices: 10.9 us -> none  [the longest x1 4.87 us: per_device(): lax.all_to_all(attention, 'expert', split_axis=0, concat_axis=0, tiled=True)]
    pallas_call x0 -> x9, Pallas kernels: none -> 8.65 us  [the longest x1 2.55 us: per_device(): pl.pallas_call(functools.partial(settle_kernel, groups, leave_count), out...]
    dot_general x7 -> x0, matrix products: 6.52 us -> none  [the longest x1 1.51 us: per_device(): output = jnp.dot(hidden_act, w_down[0], preferred_element_type=F32)]
    ppermute x7 -> x12, waiting for transfers between devices: 1.92 us -> 7.73 us  [swap_with(): return lax.ppermute(value, axis, pairs)]
    gather x2 -> x0, local copies, waits for them, and re-layouts: 2.98 us -> none  [the longest x1 1.73 us: per_device(): received[migration[:, 0]]]
    unnamed x24 -> x4, local copies, waits for them, and re-layouts: 2.85 us -> 0.01 us
  transfers between devices with their start and end apart: 10 -> 12, of which waited for: 3 -> 5; matrix products, arithmetic and copies ran while one was open for 15% -> 0% of each run, Pallas kernels for 0% -> 8%
where the time goes in v2:
time: 60 us; the launch traced here: 59.6 us
  blocking collectives  33.2 us (55%)
  Pallas kernels  8.65 us (14%)
  starting transfers between devices  8.61 us (14%)
  waiting for transfers between devices  7.73 us (13%)
  between operations  1.42 us (2%)
    all_to_all x1, blocking collectives, per_device(): lax.all_to_all(attention, 'expert', split_axis=0, concat_axis=0, tiled=True)  11.6 us
    all_to_all x1, blocking collectives, per_device(): lax.all_to_all(sent, ('x', 'expert'), split_axis=0, concat_axis=0, tiled=...  11 us
    all_to_all x1, blocking collectives, per_device(): lax.all_to_all(gained, ('x', 'expert'), split_axis=0, concat_axis=0, tile...  10.6 us
    ppermute x12, starting transfers between devices, swap_with(): return lax.ppermute(value, axis, pairs)  8.61 us
    ppermute x12, waiting for transfers between devices, swap_with(): return lax.ppermute(value, axis, pairs)  7.73 us
    pallas_call x1, Pallas kernels, per_device(): pl.pallas_call(functools.partial(settle_kernel, groups, leave_count), out...  2.55 us
    pallas_call x1, Pallas kernels, per_device(): pl.pallas_call(functools.partial(leaving_kernel, groups, leave_count), ou...  1.87 us
    pallas_call x1, Pallas kernels, per_device(): pl.pallas_call(delta_kernel, out_shape=pltpu.VMEM((members, rows, piece),...  1.32 us
  transfers between devices with their start and end apart: 12, of which 5 were waited for; matrix products, arithmetic and copies ran while one was open for 0% of the time, Pallas kernels for 8%

profile of v2, /device:TPU:0, one launch (start us, length us, event | category | flops | bytes accessed | tf_op | source)
XLA Modules:
  0.0 59.6 jit_solution(3879804663786090262)
XLA Ops:
  0.0 0.9 %pieces.1 = (bf16[512,128]{1,0:T(8,128)(2,1)S(1)}, bf16[16,512]{1,0:T(8,128)(2,1)S(1)}, bf16[16,512]{1,0:T(8,128)(2,1)S(1)}, bf16[16,512]{1,0:T(8,128)(2,1)S(1)}) custom-call(bf16[16,2048]{1,0:T(8,128)(2,1)} %refs_0_.1, bf16[512,384]{1,0:T(8,128)(2,1)} %refs_1_.1), custom_call_target="tpu_custom_call" | custom-call | bytes 8388608 | tf_op jit(solution)/shard_map/pieces/pallas_call | solution.py:339
  1.0 3.0 %collective-permute-start.1 = (bf16[512,128]{1,0:T(8,128)(2,1)S(1)}, bf16[512,128]{1,0:T(8,128)(2,1)S(1)}, u32[]{:S(2)}, u32[]{:S(2)}) collective-permute-start(bf16[512,128]{1,0:T(8,128)(2,1)S(1)} %get-tuple-element.39), channel_id=1, source_target_pairs={{0,1},{1,0},{2,3},{3,2},{4,5},{5,4},{6,7},{7,6},{8,9},{9,8},{10,11... | collective-permute-start | bytes 393224 | tf_op jit(solution)/shard_map/ppermute | solution.py:41
  4.0 1.2 %collective-permute-done.early.refs_0_ = bf16[16,512]{1,0:T(8,128)(2,1)S(1)} collective-permute-done((bf16[16,512]{1,0:T(8,128)(2,1)S(1)}, bf16[16,512]{1,0:T(8,128)(2,1)S(1)}, u32[]{:S(2)}, u32[]{:S(2)}) %collective-permute-start) | collective-permute-done | bytes 16416 | tf_op jit(solution)/shard_map/ppermute | solution.py:41
  5.2 1.9 %leaving.1 = (f32[128,128]{1,0:T(8,128)S(1)}, f32[128,128]{1,0:T(8,128)S(1)}, f32[128,128]{1,0:T(8,128)S(1)}, f32[128,128]{1,0:T(8,128)S(1)}, bf16[16,2048]{1,0:...) custom-call(s32[4,16]{1,0:T(4,128)} %bitcast.12, ...), custom_call_target="tpu_custom_call" | custom-call | bytes 8388608 | tf_op jit(solution)/shard_map/leaving/pallas_call | solution.py:352
  7.0 0.2 collective-permute-start.4
  7.3 1.5 %collective-permute-start.2 = (bf16[16,512]{1,0:T(8,128)(2,1)S(1)}, bf16[16,512]{1,0:T(8,128)(2,1)S(1)}, u32[]{:S(2)}, u32[]{:S(2)}) collective-permute-start(bf16[16,512]{1,0:T(8,128)(2,1)S(1)} %get-tuple-element.40), channel_id=1, source_target_pairs={{0,16},{8,24},{16,0},{24,8},{1,17},{9,25},{17,1},{25,9},{2,18},{10... | collective-permute-start | bytes 49160 | tf_op jit(solution)/shard_map/ppermute | solution.py:41
  8.8 0.5 collective-permute-start.5
  9.3 0.9 %collective-permute-start.6 = (f32[128,128]{1,0:T(8,128)S(1)}, f32[128,128]{1,0:T(8,128)S(1)}, u32[]{:S(2)}, u32[]{:S(2)}) collective-permute-start(f32[128,128]{1,0:T(8,128)S(1)} %get-tuple-element.46), channel_id=1, source_target_pairs={{0,24},{8,16},{16,8},{24,0},{1,25},{9,17},{17,9},{25,1},{2,26},{10... | collective-permute-start | bytes 196616 | tf_op jit(solution)/shard_map/ppermute | solution.py:41
  10.2 0.8 %collective-permute-done.2.refs_1_ = bf16[16,512]{1,0:T(8,128)(2,1)S(1)} collective-permute-done((bf16[16,512]{1,0:T(8,128)(2,1)S(1)}, bf16[16,512]{1,0:T(8,128)(2,1)S(1)}, u32[]{:S(2)}, u32[]{:S(2)}) %collective-permute-start.2) | collective-permute-done | bytes 16416 | tf_op jit(solution)/shard_map/ppermute | solution.py:41
  11.0 0.3 collective-permute-start.3
  11.3 3.1 %collective-permute-done.3.refs_2_ = bf16[16,512]{1,0:T(8,128)(2,1)S(1)} collective-permute-done((bf16[16,512]{1,0:T(8,128)(2,1)S(1)}, bf16[16,512]{1,0:T(8,128)(2,1)S(1)}, u32[]{:S(2)}, u32[]{:S(2)}) %collective-permute-start.3) | collective-permute-done | bytes 16416 | tf_op jit(solution)/shard_map/ppermute | solution.py:41
  14.4 0.0 collective-permute-done.1.other_qk
  14.4 0.2 project.1
  14.6 0.2 collective-permute-start.7
  14.9 1.3 %collective-permute-start.8 = (f32[16,640]{1,0:T(8,128)S(1)}, f32[16,640]{1,0:T(8,128)S(1)}, u32[]{:S(2)}, u32[]{:S(2)}) collective-permute-start(f32[16,640]{1,0:T(8,128)S(1)} %get-tuple-element.52), channel_id=1, source_target_pairs={{0,16},{8,24},{16,0},{24,8},{1,17},{9,25},{17,1},{25,9},{2,18},{10... | collective-permute-start | bytes 122888 | tf_op jit(solution)/shard_map/ppermute | solution.py:41
  16.1 0.5 collective-permute-start.9
  17.9 0.0 collective-permute-done.5.refs_2_
  17.9 0.0 copy-start
  17.9 0.0 copy-start.1
  17.9 2.5 %settle.1 = (bf16[128,2048]{1,0:T(8,128)(2,1)S(1)}, f32[1,128]{1,0:T(1,128)S(1)}, f32[1,2048]{1,0:T(1,128)S(1)}, bf16[1,2048]{1,0:T(2,128)(2,1)S(1)}, f32[16,128...) custom-call(s32[4,16]{1,0:T(4,128)} %bitcast.13, ...), custom_call_target="tpu_custom_call" | custom-call | bytes 8388608 | tf_op jit(solution)/shard_map/settle/pallas_call | solution.py:388
  20.5 0.0 collective-permute-done.7.refs_1_
  20.5 0.0 collective-permute-done.9.refs_3_
  20.5 1.3 %delta.1 = bf16[8,16,256]{2,1,0:T(8,128)(2,1)S(1)} custom-call(f32[1]{0:T(128)S(6)} %copy.16.a_log, f32[1]{0:T(128)S(6)} %copy.17.dt_bias, f32[16,128]{1,0:T(8,128)S(1)} %get-tuple-element.47.scale, f32[1,128]{1,0:T(1,128)S(1)} %get-tuple-element.48.head_gain, bf16[128,2048]{1,0:T(8,128)(2,1)S(1)} %get-tuple-element.49.w_out, ...), custom_call_target="tpu_custom_call" | custom-call | bytes 8388608 | tf_op jit(solution)/shard_map/delta/pallas_call | solution.py:419
  21.8 11.6 %all_to_all.15.attention = bf16[8,16,256]{2,1,0:T(8,128)(2,1)S(1)} all-to-all(bf16[8,16,256]{2,1,0:T(8,128)(2,1)S(1)} %delta.1), channel_id=1, replica_groups=mesh['parts'=1,'x'=2,'core'=2,'expert'=8] {'expert'}, dimensions={0} | all-to-all | bytes 131072 | tf_op jit(solution)/shard_map/all_to_all | solution.py:429
  33.4 10.6 %all_to_all.16.every = bf16[16,16,256]{2,1,0:T(8,128)(2,1)S(1)} all-to-all(bf16[16,16,256]{2,1,0:T(8,128)(2,1)S(1)} %get-tuple-element.56), channel_id=1, replica_groups=mesh['parts'=1,'x'=2,'core'=2,'expert'=8] {'x','expert'}, dimensions={0} | all-to-all | bytes 262144 | tf_op jit(solution)/shard_map/all_to_all | solution.py:443
  44.0 1.3 %collective-permute-done.10.across = bf16[16,16,256]{2,1,0:T(8,128)(2,1)S(1)} collective-permute-done((bf16[16,16,256]{2,1,0:T(8,128)(2,1)S(1)}, bf16[16,16,256]{2,1,0:T(8,128)(2,1)S(1)}, u32[]{:S(2)}, u32[]{:S(2)}) %collective-permute-start.10) | collective-permute-done | bytes 131104 | tf_op jit(solution)/shard_map/ppermute | solution.py:41
  45.4 0.8 %experts.1 = (bf16[16,40,128]{2,1,0:T(8,128)(2,1)S(1)}, bf16[16,40,128]{2,1,0:T(8,128)(2,1)S(1)}) custom-call(bf16[16,16,256]{2,1,0:T(8,128)(2,1)S(1)} %all_to_all.16.every, bf16[16,16,256]{2,1,0:T(8,128)(2,1)S(1)} %collective-permute-done.10.across, f32[64,128]{1,0:T(8,128)S(1)} %get-tuple-element.57.hits, f32[1,2048]{1,0:T(1,128)S(1)} %get-tuple-element.58.gain, ...), custom_call_target="tpu_custom_call" | custom-call | bytes 8388608 | tf_op jit(solution)/shard_map/experts/pallas_call | solution.py:447
  46.2 0.2 collective-permute-start.11
  46.4 1.2 %collective-permute-done.11.received = bf16[16,40,128]{2,1,0:T(8,128)(2,1)S(1)} collective-permute-done((bf16[16,40,128]{2,1,0:T(8,128)(2,1)S(1)}, bf16[16,40,128]{2,1,0:T(8,128)(2,1)S(1)}, u32[]{:S(2)}, u32[]{:S(2)}) %collective-permute-start.11) | collective-permute-done | bytes 163872 | tf_op jit(solution)/shard_map/ppermute | solution.py:41
  47.6 0.1 pair.1
  47.8 11.0 %all_to_all.17.back = bf16[16,40,128]{2,1,0:T(8,128)(2,1)S(1)} all-to-all(bf16[16,40,128]{2,1,0:T(8,128)(2,1)S(1)} %pair.1), channel_id=1, replica_groups=mesh['parts'=1,'x'=2,'core'=2,'expert'=8] {'x','expert'}, dimensions={0} | all-to-all | bytes 327680 | tf_op jit(solution)/shard_map/all_to_all | solution.py:473
  58.8 0.8 %finish.1 = bf16[16,256]{1,0:T(8,128)(2,1)} custom-call(bf16[16,40,128]{2,1,0:T(8,128)(2,1)S(1)} %all_to_all.17.back, f32[16,256]{1,0:T(8,128)S(1)} %get-tuple-element.62.residual), custom_call_target="tpu_custom_call" | custom-call | bytes 8388608 | tf_op jit(solution)/shard_map/finish/pallas_call | solution.py:474
  (8 shorter events, 0.0 us)
Async XLA Ops:
  1.0 13.5 %collective-permute-start.1 = (bf16[512,128]{1,0:T(8,128)(2,1)S(1)}, bf16[512,128]{1,0:T(8,128)(2,1)S(1)}, u32[]{:S(2)}, u32[]{:S(2)}) collective-permute-start(bf16[512,128]{1,0:T(8,128)(2,1)S(1)} %get-tuple-element.39), channel_id=1, source_target_pairs={{0,1},{1,0},{2,3},{3,2},{4,5},{5,4},{6,7},{7,6},{8,9},{9,8},{10,11... | collective-permute-start | bytes 393224 | tf_op jit(solution)/shard_map/ppermute | solution.py:41
  4.0 1.2 %collective-permute-start = (bf16[16,512]{1,0:T(8,128)(2,1)S(1)}, bf16[16,512]{1,0:T(8,128)(2,1)S(1)}, u32[]{:S(2)}, u32[]{:S(2)}) collective-permute-start(bf16[16,512]{1,0:T(8,128)(2,1)S(1)} %get-tuple-element.34), channel_id=1, source_target_pairs={{0,8},{8,0},{16,24},{24,16},{1,9},{9,1},{17,25},{25,17},{2,10},{10... | collective-permute-start | bytes 49160 | tf_op jit(solution)/shard_map/ppermute | solution.py:41
  7.0 9.1 %collective-permute-start.4 = (f32[128,128]{1,0:T(8,128)S(1)}, f32[128,128]{1,0:T(8,128)S(1)}, u32[]{:S(2)}, u32[]{:S(2)}) collective-permute-start(f32[128,128]{1,0:T(8,128)S(1)} %get-tuple-element.44), channel_id=1, source_target_pairs={{0,8},{8,0},{16,24},{24,16},{1,9},{9,1},{17,25},{25,17},{2,10},{10... | collective-permute-start | bytes 196616 | tf_op jit(solution)/shard_map/ppermute | solution.py:41
  7.3 3.7 %collective-permute-start.2 = (bf16[16,512]{1,0:T(8,128)(2,1)S(1)}, bf16[16,512]{1,0:T(8,128)(2,1)S(1)}, u32[]{:S(2)}, u32[]{:S(2)}) collective-permute-start(bf16[16,512]{1,0:T(8,128)(2,1)S(1)} %get-tuple-element.40), channel_id=1, source_target_pairs={{0,16},{8,24},{16,0},{24,8},{1,17},{9,25},{17,1},{25,9},{2,18},{10... | collective-permute-start | bytes 49160 | tf_op jit(solution)/shard_map/ppermute | solution.py:41
  8.8 9.1 %collective-permute-start.5 = (f32[128,128]{1,0:T(8,128)S(1)}, f32[128,128]{1,0:T(8,128)S(1)}, u32[]{:S(2)}, u32[]{:S(2)}) collective-permute-start(f32[128,128]{1,0:T(8,128)S(1)} %get-tuple-element.45), channel_id=1, source_target_pairs={{0,16},{8,24},{16,0},{24,8},{1,17},{9,25},{17,1},{25,9},{2,18},{10... | collective-permute-start | bytes 196616 | tf_op jit(solution)/shard_map/ppermute | solution.py:41
  9.3 8.6 %collective-permute-start.6 = (f32[128,128]{1,0:T(8,128)S(1)}, f32[128,128]{1,0:T(8,128)S(1)}, u32[]{:S(2)}, u32[]{:S(2)}) collective-permute-start(f32[128,128]{1,0:T(8,128)S(1)} %get-tuple-element.46), channel_id=1, source_target_pairs={{0,24},{8,16},{16,8},{24,0},{1,25},{9,17},{17,9},{25,1},{2,26},{10... | collective-permute-start | bytes 196616 | tf_op jit(solution)/shard_map/ppermute | solution.py:41
  11.0 3.4 %collective-permute-start.3 = (bf16[16,512]{1,0:T(8,128)(2,1)S(1)}, bf16[16,512]{1,0:T(8,128)(2,1)S(1)}, u32[]{:S(2)}, u32[]{:S(2)}) collective-permute-start(bf16[16,512]{1,0:T(8,128)(2,1)S(1)} %get-tuple-element.41), channel_id=1, source_target_pairs={{0,24},{8,16},{16,8},{24,0},{1,25},{9,17},{17,9},{25,1},{2,26},{10... | collective-permute-start | bytes 49160 | tf_op jit(solution)/shard_map/ppermute | solution.py:41
  14.6 5.8 %collective-permute-start.7 = (f32[16,640]{1,0:T(8,128)S(1)}, f32[16,640]{1,0:T(8,128)S(1)}, u32[]{:S(2)}, u32[]{:S(2)}) collective-permute-start(f32[16,640]{1,0:T(8,128)S(1)} %get-tuple-element.51), channel_id=1, source_target_pairs={{0,8},{8,0},{16,24},{24,16},{1,9},{9,1},{17,25},{25,17},{2,10},{10... | collective-permute-start | bytes 122888 | tf_op jit(solution)/shard_map/ppermute | solution.py:41
  14.9 5.6 %collective-permute-start.8 = (f32[16,640]{1,0:T(8,128)S(1)}, f32[16,640]{1,0:T(8,128)S(1)}, u32[]{:S(2)}, u32[]{:S(2)}) collective-permute-start(f32[16,640]{1,0:T(8,128)S(1)} %get-tuple-element.52), channel_id=1, source_target_pairs={{0,16},{8,24},{16,0},{24,8},{1,17},{9,25},{17,1},{25,9},{2,18},{10... | collective-permute-start | bytes 122888 | tf_op jit(solution)/shard_map/ppermute | solution.py:41
  16.1 4.4 %collective-permute-start.9 = (f32[16,640]{1,0:T(8,128)S(1)}, f32[16,640]{1,0:T(8,128)S(1)}, u32[]{:S(2)}, u32[]{:S(2)}) collective-permute-start(f32[16,640]{1,0:T(8,128)S(1)} %get-tuple-element.53), channel_id=1, source_target_pairs={{0,24},{8,16},{16,8},{24,0},{1,25},{9,17},{17,9},{25,1},{2,26},{10... | collective-permute-start | bytes 122888 | tf_op jit(solution)/shard_map/ppermute | solution.py:41
  17.9 27.5 %copy-start = (bf16[1,2048,512]{2,1,0:T(8,128)(2,1)S(1)}, bf16[1,2048,512]{2,1,0:T(8,128)(2,1)}, u32[]{:S(2)}) copy-start(bf16[1,2048,512]{2,1,0:T(8,128)(2,1)} %w_gate_up.1) | copy-start | bytes 6291460
  17.9 27.5 %copy-start.1 = (bf16[1,256,2048]{2,1,0:T(8,128)(2,1)S(1)}, bf16[1,256,2048]{2,1,0:T(8,128)(2,1)}, u32[]{:S(2)}) copy-start(bf16[1,256,2048]{2,1,0:T(8,128)(2,1)} %w_down.1) | copy-start | bytes 3145732
  44.0 1.3 %collective-permute-start.10 = (bf16[16,16,256]{2,1,0:T(8,128)(2,1)S(1)}, bf16[16,16,256]{2,1,0:T(8,128)(2,1)S(1)}, u32[]{:S(2)}, u32[]{:S(2)}) collective-permute-start(bf16[16,16,256]{2,1,0:T(8,128)(2,1)S(1)} %all_to_all.16.every), channel_id=1, source_target_pairs={{0,8},{8,0},{1,9},{9,1},{2,10},{10,2},{3,11},{11,3},{4,12},{12,4},... | collective-permute-start | bytes 393224 | tf_op jit(solution)/shard_map/ppermute | solution.py:41
  46.2 1.5 %collective-permute-start.11 = (bf16[16,40,128]{2,1,0:T(8,128)(2,1)S(1)}, bf16[16,40,128]{2,1,0:T(8,128)(2,1)S(1)}, u32[]{:S(2)}, u32[]{:S(2)}) collective-permute-start(bf16[16,40,128]{2,1,0:T(8,128)(2,1)S(1)} %get-tuple-element.61), channel_id=1, source_target_pairs={{0,8},{8,0},{1,9},{9,1},{2,10},{10,2},{3,11},{11,3},{4,12},{12,4},... | collective-permute-start | bytes 491528 | tf_op jit(solution)/shard_map/ppermute | solution.py:41

commit v3 on v2

v3 whole, which is shorter than its diff:
```python
import functools

import jax
import jax.numpy as jnp
from jax import lax
from jax.experimental import pallas as pl
from jax.experimental.pallas import tpu as pltpu
from jax.sharding import PartitionSpec as P

DK = 128
DV = 128
MOE_FF = 256
LANES = 128
SENT = 2 * DK + 2 * DV + LANES

EPS = 1e-06
BF = jnp.bfloat16
F32 = jnp.float32

VMEM = pl.BlockSpec(memory_space=pltpu.VMEM)
SMEM = pl.BlockSpec(memory_space=pltpu.SMEM)
HBM = pl.BlockSpec(memory_space=pltpu.HBM)
ANY = pl.BlockSpec(memory_space=pl.ANY)
COST = pl.CostEstimate(flops=0, bytes_accessed=8 * 1024 * 1024, transcendentals=0)
PARAMS = pltpu.CompilerParams(vmem_limit_bytes=24 * 1024 * 1024)


def in_hbm(*values):
    return [pltpu.with_memory_space_constraint(value, pltpu.HBM) for value in values]


def copy_all(pairs, sems):
    copies = [pltpu.make_async_copy(a, b, sems.at[i]) for i, (a, b) in enumerate(pairs)]
    for copy in copies:
        copy.start()
    return copies


def swap_with(value, axis, offset):
    pairs = [(source, source ^ offset) for source in range(lax.axis_size(axis))]
    return lax.ppermute(value, axis, pairs)


def row_scale(values):
    return lax.rsqrt(jnp.mean(values * values, axis=-1, keepdims=True) + EPS)


def unit_rows(values):
    return values * lax.rsqrt(jnp.sum(values * values, axis=-1, keepdims=True) + EPS)


def group_index():
    return lax.axis_index("x") * lax.axis_size("core") + lax.axis_index("core")


def first_kernel(groups, leave_count, migration, states, hidden, w_qkvz, *refs):
    gain, w_ba, own_qk, messages = refs[0], refs[1], refs[2], refs[3 : groups + 2]
    held, hidden_near, w_near, w_ba_near, normed, gain_near, plan, plan_sem, sems = refs[groups + 2 :]
    plan_copy = pltpu.make_async_copy(migration, plan, plan_sem)
    plan_copy.start()
    pairs = [
        (hidden, hidden_near),
        (states.at[:, 0], held),
        (w_qkvz.at[:, pl.ds(0, DK)], own_qk),
        (w_qkvz, w_near),
        (gain, gain_near),
        (w_ba, w_ba_near),
    ]
    copies = copy_all(pairs, sems)
    group = group_index()
    rows = hidden.shape[0]
    depth = w_qkvz.shape[0]
    tiles = depth // LANES
    copies[0].wait()
    wide = hidden_near[...].astype(F32)
    copies[4].wait()
    normed[...] = (wide * row_scale(wide) * gain_near[...]).astype(BF)
    for i in range(1, groups):
        for c in range(tiles):
            first = pl.multiple_of((group ^ i) * depth + c * LANES, LANES)
            messages[i - 1][c * rows : (c + 1) * rows, :] = normed[:, pl.ds(first, LANES)]
    plan_copy.wait()
    copies[1].wait()
    for i in range(1, groups):
        slot = 0
        for j in range(leave_count):
            at = group * leave_count + j
            slot = jnp.where(plan[2, at] == (group ^ i), plan[1, at], slot)
        messages[i - 1][tiles * rows :, :] = held[slot].astype(BF)
    for copy in copies[2:4] + copies[5:]:
        copy.wait()


def project_kernel(groups, normed, w_ba, w_qkvz, other_qk, staged, *refs):
    messages, outs, scaled = refs[: groups - 1], refs[groups - 1 : -1], refs[-1]
    del staged
    group = group_index()
    depth = w_qkvz.shape[0]
    rows = normed.shape[0]
    for c in range(depth // LANES):
        columns = pl.ds(pl.multiple_of(group * depth + c * LANES, LANES), LANES)
        for i in range(groups):
            part = normed[:, columns] if i == 0 else messages[i - 1][c * rows : (c + 1) * rows, :]
            scaled[i * rows : (i + 1) * rows, c * LANES : (c + 1) * LANES] = part
    x = scaled[...]
    main = jnp.dot(x, w_qkvz[...], preferred_element_type=F32)
    other = jnp.dot(x, other_qk[...], preferred_element_type=F32)
    wide = x.astype(F32)
    lane = lax.broadcasted_iota(jnp.int32, (groups * rows, LANES), 1)
    mixes = jnp.zeros((groups * rows, LANES), F32)
    for j in range(2):
        total = jnp.sum(wide * w_ba[j : j + 1, :].astype(F32), axis=1, keepdims=True)
        mixes = jnp.where(lane == j, total, mixes)
    for i in range(groups):
        block = slice(i * rows, (i + 1) * rows)
        outs[i][:, : DK + 2 * DV] = main[block]
        outs[i][:, DK + 2 * DV : 2 * DK + 2 * DV] = other[block]
        outs[i][:, 2 * DK + 2 * DV :] = mixes[block]


def stage_kernel(groups, hidden, gain, routes, router, w_gate_up, w_down, *refs):
    count = (len(refs) - 5) // 2
    sources, staged = refs[:count], refs[count : 2 * count]
    own_hidden, own_gain, hits, expert, sems = refs[-5:]
    width = hidden.shape[1]
    span = 2 * MOE_FF
    pairs = [(w_gate_up.at[0], expert.at[pl.ds(0, width)])]
    for c in range(width // span):
        pairs.append(
            (
                w_down.at[0, :, pl.ds(c * span, span)],
                expert.at[pl.ds(width + c * MOE_FF, MOE_FF)],
            )
        )
    copies = copy_all(list(zip(sources, staged)) + pairs, sems)
    line = lax.broadcasted_iota(jnp.int32, (16, span), 0)
    block = jnp.zeros((16, span), F32)
    for c in range(width // span):
        block = jnp.where(line == c, router[:, c * span : (c + 1) * span].astype(F32), block)
    expert[expert.shape[0] - 16 :, :] = block.astype(BF)
    group = group_index()
    core = lax.axis_index("core")
    member = lax.axis_index("expert")
    rows = hidden.shape[0]
    total_rows = groups * rows
    piece = own_hidden.shape[1]
    members = width // piece
    own, own_g = hidden[:, :piece], gain[:, :piece]
    for m in range(1, members):
        columns = slice(m * piece, (m + 1) * piece)
        own = jnp.where(member == m, hidden[:, columns], own)
        own_g = jnp.where(member == m, gain[:, columns], own_g)
    own_hidden[...] = own.astype(F32)
    own_gain[...] = own_g
    served = total_rows // 2
    row = lax.broadcasted_iota(jnp.int32, (served, total_rows), 0)
    lane = lax.broadcasted_iota(jnp.int32, (served, total_rows), 1)
    same = lane == (2 * (row // rows) + core) * rows + row % rows
    at = lax.broadcasted_iota(jnp.int32, hits.shape, 1)
    table = jnp.zeros(hits.shape, F32)
    for i in range(2):
        found = jnp.where(routes[...] == (group ^ i) * members + member, 1.0, 0.0)
        found = jnp.max(found, axis=0, keepdims=True)
        column = jnp.sum(jnp.where(same, found, 0.0), axis=1, keepdims=True)
        table = jnp.where(at == i, column, table)
    hits[...] = table
    for copy in copies:
        copy.wait()


def settle_kernel(groups, leave_count, migration, a_log, dt_bias, states, after, *refs):
    messages, (held, mixing, own_state, plan, plan_sem) = refs[:-5], refs[-5:]
    del after
    plan_copy = pltpu.make_async_copy(migration, plan, plan_sem)
    plan_copy.start()
    mixing[0:1, :] = jnp.exp(jnp.full((1, LANES), a_log[0], F32))
    mixing[1:2, :] = jnp.full((1, LANES), dt_bias[0], F32)
    group = group_index()
    plan_copy.wait()
    for j in range(leave_count):
        at = group * leave_count + j

        @pl.when(plan[2, at] == group)
        def _():
            own_state[...] = states[plan[1, at]]

    for i in range(groups):
        for j in range(leave_count):
            at = (group ^ i) * leave_count + j

            @pl.when(plan[2, at] == group)
            def _():
                if i == 0:
                    held[plan[3, at]] = own_state[...]
                else:
                    arrival = messages[i - 1]
                    held[plan[3, at]] = arrival[arrival.shape[0] - DK :, :].astype(F32)


def delta_kernel(mixing, head_gain, w_out, held, expert, *refs):
    partials, (out, passed, key_sums, query_sums) = refs[:-4], refs[-4:]
    del expert, passed
    member = lax.axis_index("expert")
    rows = held.shape[0]
    summed = partials[0][...]
    for partial in partials[1:]:
        summed = summed + partial[...]
    projected = summed.astype(BF).astype(F32)
    own_qk = projected[:, :DK]
    values = projected[:, DK : DK + DV]
    out_gate = projected[:, DK + DV : DK + 2 * DV]
    other = projected[:, DK + 2 * DV : 2 * DK + 2 * DV]
    write_mix = projected[:, 2 * DK + 2 * DV : 2 * DK + 2 * DV + 1]
    decay_mix = projected[:, 2 * DK + 2 * DV + 1 : 2 * DK + 2 * DV + 2]
    is_first = member % 2 == 0
    first = jnp.where(is_first, own_qk, other)
    second = jnp.where(is_first, other, own_qk)
    low_half = lax.broadcasted_iota(jnp.int32, (rows, DK), 1) < DK // 2
    queries = unit_rows(jnp.where(low_half, first, pltpu.roll(second, DK // 2, 1))) * DK ** (-0.5)
    keys_unit = unit_rows(jnp.where(low_half, pltpu.roll(first, DK // 2, 1), second))
    shifted = decay_mix + mixing[1:2, 0:1]
    soft = jnp.maximum(shifted, 0.0) + jnp.log1p(jnp.exp(-jnp.abs(shifted)))
    decay = jnp.exp(-mixing[0:1, 0:1] * soft)
    beta = jax.nn.sigmoid(write_mix)
    keys_t = jnp.transpose(keys_unit)
    queries_t = jnp.transpose(queries)
    for r in range(rows):
        state = held[r]
        key_sums[r : r + 1, :] = jnp.sum(state * keys_t[:, r : r + 1], axis=0, keepdims=True)
        query_sums[r : r + 1, :] = jnp.sum(state * queries_t[:, r : r + 1], axis=0, keepdims=True)
    correction = (values - key_sums[...] * decay) * beta
    overlap = jnp.sum(queries * keys_unit, axis=1, keepdims=True)
    readout = query_sums[...] * decay + overlap * correction
    normed = readout * row_scale(readout) * head_gain[...]
    gated = (normed * (out_gate * jax.nn.sigmoid(out_gate))).astype(BF)
    attention = jnp.dot(gated, w_out[...], preferred_element_type=F32).astype(BF)
    piece = out.shape[2]
    for m in range(out.shape[0]):
        out[m] = attention[:, m * piece : (m + 1) * piece]


def residual_kernel(attention, hidden, gain, gained, residual):
    members, rows, piece = attention.shape
    total = hidden[...]
    for m in range(members):
        total = total + attention[m].astype(F32)
    residual[...] = total
    sent = (total * gain[...]).astype(BF)
    for d in range(gained.shape[0]):
        gained[d] = sent


def packed(tile, piece):
    if piece >= LANES:
        return [tile[:, c : c + LANES] for c in range(0, piece, LANES)]
    count = LANES // piece
    part = tile.shape[0] // count
    return [jnp.concatenate([tile[c * part : (c + 1) * part] for c in range(count)], axis=1)]


def unpacked(tile, rows, piece):
    if piece >= LANES:
        return jnp.concatenate(
            [tile[c * rows : (c + 1) * rows] for c in range(piece // LANES)], axis=1
        )
    return jnp.concatenate([tile[:, c : c + piece] for c in range(0, LANES, piece)], axis=0)


def tail_of(weight):
    part = 8
    lane = lax.broadcasted_iota(jnp.int32, (part, LANES), 1)
    tail = jnp.zeros((part, LANES), F32)
    for c in range(weight.shape[0] // part):
        at = weight[c * part : (c + 1) * part]
        high = at.astype(BF).astype(F32)
        tail = jnp.where(lane == c, high, tail)
        tail = jnp.where(lane == LANES // 2 + c, at - high, tail)
    return tail


def expert_kernel(width, every, hits, gain, own, other, out):
    devices, rows, piece = every.shape
    members = width // piece
    half = devices // members
    total_rows = half * rows
    span = 2 * MOE_FF
    experts = (own, other)
    gate_up = [jnp.zeros((total_rows, span), F32)] * 2
    routed = [jnp.zeros((total_rows, piece), F32)] * 2
    squares = jnp.zeros((total_rows, piece), F32)
    inverse = 1.0 / gain[...]
    last = own.shape[0] - 16
    routers = [ref[last:, :].astype(F32) for ref in experts]
    for m in range(members):
        columns = slice(m * piece, (m + 1) * piece)
        line, first = m * piece // span, m * piece % span
        x = jnp.concatenate([every[g * members + m] for g in range(half)], axis=0)
        wide = x.astype(F32)
        plain = wide * inverse[:, columns]
        squares = squares + plain * plain
        for i in range(2):
            gate_up[i] = gate_up[i] + jnp.dot(x, experts[i][columns, :], preferred_element_type=F32)
            routed[i] = routed[i] + wide * routers[i][line : line + 1, first : first + piece]
    scale = lax.rsqrt(jnp.sum(squares, axis=1, keepdims=True) * (1.0 / width) + EPS)
    weights, acts = [], []
    for i in range(2):
        logits = jnp.sum(routed[i], axis=1, keepdims=True) * scale
        weights.append(jnp.where(hits[:, i : i + 1] > 0.0, jnp.exp(logits), 0.0))
        both = gate_up[i] * scale
        gate = both[:, :MOE_FF]
        acts.append((gate * jax.nn.sigmoid(gate) * both[:, MOE_FF:]).astype(BF))
    summed = weights[0] + weights[1]
    tails = [tail_of(summed[g * rows : (g + 1) * rows]) for g in range(half)]
    for c in range(width // span):
        down = slice(width + c * MOE_FF, width + (c + 1) * MOE_FF)
        y = jnp.zeros((total_rows, span), F32)
        for i in range(2):
            y = y + jnp.dot(acts[i], experts[i][down, :], preferred_element_type=F32) * weights[i]
        for m in range(span // piece):
            for g in range(half):
                tile = y[g * rows : (g + 1) * rows, m * piece : (m + 1) * piece]
                out[g * members + c * span // piece + m] = jnp.concatenate(
                    packed(tile, piece) + [tails[g]], axis=0
                ).astype(BF)


def final_kernel(back, residual, out):
    devices, height, _ = back.shape
    rows, piece = residual.shape
    total = back[0].astype(F32)
    for d in range(1, devices):
        total = total + back[d].astype(F32)
    body = rows * piece // LANES
    numerator = unpacked(total[:body], rows, piece)
    tail = total[body:]
    tail = tail + pltpu.roll(tail, LANES // 2, 1)
    denominator = jnp.concatenate(
        [tail[:, c : c + 1] for c in range(rows // tail.shape[0])], axis=0
    )
    out[...] = (residual[...] + numerator / denominator).astype(BF)


def per_device(
    hidden,
    states,
    migration,
    routes,
    w_qkvz,
    w_ba,
    a_log,
    dt_bias,
    attn_gain,
    head_gain,
    w_out,
    moe_gain,
    w_router,
    w_gate_up,
    w_down,
):
    dp = ("x", "core")
    half = lax.axis_size("x")
    groups = half * lax.axis_size("core")
    members = lax.axis_size("expert")
    rows, width = hidden.shape
    depth = w_qkvz.shape[0]
    piece = width // members
    total_rows = routes.shape[0]
    leave_count = migration.shape[0] // groups
    plan = jnp.transpose(migration)
    shape = jax.ShapeDtypeStruct

    w_ba_t = jnp.transpose(w_ba)
    firsts = pl.pallas_call(
        functools.partial(first_kernel, groups, leave_count),
        out_shape=[pltpu.VMEM((depth, DK), BF)]
        + [pltpu.VMEM((rows * depth // LANES + DK, LANES), BF)] * (groups - 1)
        + [
            pltpu.VMEM((rows, DK, DV), F32),
            pltpu.VMEM(hidden.shape, BF),
            pltpu.VMEM(w_qkvz.shape, BF),
            pltpu.VMEM(w_ba_t.shape, BF),
            pltpu.VMEM(hidden.shape, BF),
        ],
        in_specs=[HBM] * 6,
        out_specs=[VMEM] * (groups + 5),
        scratch_shapes=[
            pltpu.VMEM((1, width), F32),
            pltpu.SMEM(plan.shape, jnp.int32),
            pltpu.SemaphoreType.DMA,
            pltpu.SemaphoreType.DMA((6,)),
        ],
        compiler_params=PARAMS,
        cost_estimate=COST,
        name="first",
    )(*in_hbm(plan, states, hidden, w_qkvz, attn_gain.reshape(1, width), w_ba_t))
    held, hidden_near, w_near, w_ba_near, normed = firsts[groups:]
    other_qk = swap_with(firsts[0], "expert", 1)
    messages = [swap_with(firsts[i], dp, i) for i in range(1, groups)]
    operands = [w_out, head_gain.reshape(1, DV), moe_gain.reshape(1, width)]
    span = 2 * MOE_FF
    staged = pl.pallas_call(
        functools.partial(stage_kernel, groups),
        out_shape=[pltpu.VMEM(operand.shape, operand.dtype) for operand in operands]
        + [
            pltpu.VMEM((rows, piece), F32),
            pltpu.VMEM((1, piece), F32),
            pltpu.VMEM((total_rows // 2, LANES), F32),
            pltpu.VMEM((width + width // span * MOE_FF + 16, span), BF),
        ],
        in_specs=[VMEM] * 4 + [HBM] * (2 + len(operands)),
        out_specs=[VMEM] * (4 + len(operands)),
        scratch_shapes=[pltpu.SemaphoreType.DMA((1 + width // span + len(operands),))],
        compiler_params=PARAMS,
        cost_estimate=COST,
        name="stage",
    )(
        hidden_near,
        *in_hbm(moe_gain.reshape(1, width), jnp.transpose(routes), jnp.transpose(w_router)),
        *in_hbm(w_gate_up, w_down, *operands),
    )
    w_out_near, head_gain_near, moe_gain_near = staged[:-4]
    own_hidden, own_gain, hits, expert = staged[-4:]

    partials = pl.pallas_call(
        functools.partial(project_kernel, groups),
        out_shape=[pltpu.VMEM((rows, SENT), F32)] * groups,
        in_specs=[VMEM] * 4 + [ANY] + [VMEM] * (groups - 1),
        out_specs=[VMEM] * groups,
        scratch_shapes=[pltpu.VMEM((total_rows, depth), BF)],
        compiler_params=PARAMS,
        cost_estimate=COST,
        name="project",
    )(normed, w_ba_near, w_near, other_qk, own_gain, *messages)
    after = partials[0]
    partials = [partials[0]] + [swap_with(partials[i], dp, i) for i in range(1, groups)]
    held, mixing = pl.pallas_call(
        functools.partial(settle_kernel, groups, leave_count),
        out_shape=[pltpu.VMEM((rows, DK, DV), F32), pltpu.VMEM((2, LANES), F32)],
        in_specs=[HBM] + [SMEM] * 2 + [VMEM, ANY] + [VMEM] * (groups - 1),
        out_specs=[VMEM] * 2,
        scratch_shapes=[
            pltpu.VMEM((DK, DV), F32),
            pltpu.SMEM(plan.shape, jnp.int32),
            pltpu.SemaphoreType.DMA,
        ],
        input_output_aliases={3: 0},
        compiler_params=PARAMS,
        cost_estimate=COST,
        name="settle",
    )(*in_hbm(plan), a_log, dt_bias, held, after, *messages)

    attention, expert = pl.pallas_call(
        delta_kernel,
        out_shape=[
            pltpu.VMEM((members, rows, piece), BF),
            pltpu.VMEM(expert.shape, expert.dtype),
        ],
        in_specs=[VMEM] * 4 + [ANY] + [VMEM] * groups,
        out_specs=[VMEM, ANY],
        scratch_shapes=[pltpu.VMEM((rows, DV), F32)] * 2,
        input_output_aliases={4: 1},
        compiler_params=PARAMS,
        cost_estimate=COST,
        name="delta",
    )(mixing, head_gain_near, w_out_near, held, expert, *partials)
    other_expert = swap_with(expert, "core", 1)
    attention = lax.all_to_all(attention, "expert", split_axis=0, concat_axis=0, tiled=True)

    gained, residual = pl.pallas_call(
        residual_kernel,
        out_shape=[
            pltpu.VMEM((half * members, rows, piece), BF),
            pltpu.VMEM((rows, piece), F32),
        ],
        in_specs=[VMEM] * 3,
        out_specs=[VMEM] * 2,
        compiler_params=PARAMS,
        cost_estimate=COST,
        name="residual",
    )(attention, own_hidden, own_gain)
    every = lax.all_to_all(gained, ("x", "expert"), split_axis=0, concat_axis=0, tiled=True)

    height = rows * piece // LANES + 8
    sent = pl.pallas_call(
        functools.partial(expert_kernel, width),
        out_shape=pltpu.VMEM((half * members, height, LANES), BF),
        in_specs=[VMEM] * 5,
        out_specs=VMEM,
        compiler_params=PARAMS,
        cost_estimate=COST,
        name="experts",
    )(every, hits, moe_gain_near, expert, other_expert)
    back = lax.all_to_all(sent, ("x", "expert"), split_axis=0, concat_axis=0, tiled=True)
    return pl.pallas_call(
        final_kernel,
        out_shape=shape((rows, piece), BF),
        in_specs=[VMEM] * 2,
        out_specs=VMEM,
        compiler_params=PARAMS,
        cost_estimate=COST,
        name="finish",
    )(back, residual)


def solution(mesh):
    parts, groups, members = (mesh.shape[name] for name in ("parts", "dp", "expert"))
    devices = mesh.devices.reshape(parts, groups // 2, 2, members)
    fine = jax.sharding.Mesh(devices, ("parts", "x", "core", "expert"))
    placed = (
        P(("parts", "x", "core"), None),
        P(("parts", "x", "core"), "expert", None, None),
        P("parts", None),
        P("parts", None),
        P(("x", "core"), "expert"),
        P(("x", "core"), "expert"),
        P("expert"),
        P("expert"),
        P(),
        P(),
        P("expert", None),
        P(),
        P(None, ("x", "core", "expert")),
        P(("x", "core", "expert"), None, None),
        P(("x", "core", "expert"), None, None),
    )
    return jax.shard_map(
        per_device,
        mesh=fine,
        in_specs=placed,
        out_specs=P(("parts", "x", "core"), "expert"),
        check_vma=False,
    )
```

time: 60 us -> 51.4 us (0.86)
  waiting for transfers between devices: 7.73 us -> 1.37 us
  starting transfers between devices: 8.61 us -> 6.98 us
  blocking collectives: 33.2 us -> 32.5 us
    ppermute x12 -> x8, waiting for transfers between devices: 7.73 us -> 1.37 us  [swap_with(): return lax.ppermute(value, axis, pairs)]
    pallas_call x5 -> x4, Pallas kernels: 5.05 us -> 6.77 us  [the longest x1 2.82 us: per_device(): pl.pallas_call(functools.partial(stage_kernel, groups), out_shape=[pltpu....]
    ppermute x12 -> x8, starting transfers between devices: 8.61 us -> 6.98 us  [swap_with(): return lax.ppermute(value, axis, pairs)]
    pallas_call x1, Pallas kernels: 2.55 us -> 0.94 us  [per_device(): pl.pallas_call(functools.partial(settle_kernel, groups, leave_count), out...]
  transfers between devices with their start and end apart: 12 -> 8, of which waited for: 5 -> 2; matrix products, arithmetic and copies ran while one was open for 0% -> 0% of each run, Pallas kernels for 8% -> 7%
where the time goes in v3:
time: 51.4 us; the launch traced here: 51 us
  blocking collectives  32.5 us (63%)
  Pallas kernels  8.77 us (17%)
  starting transfers between devices  6.98 us (14%)
  waiting for transfers between devices  1.37 us (3%)
  between operations  1.37 us (3%)
    all_to_all x1, blocking collectives, per_device(): lax.all_to_all(attention, 'expert', split_axis=0, concat_axis=0, tiled=True)  11.6 us
    all_to_all x1, blocking collectives, per_device(): lax.all_to_all(sent, ('x', 'expert'), split_axis=0, concat_axis=0, tiled=...  10.5 us
    all_to_all x1, blocking collectives, per_device(): lax.all_to_all(gained, ('x', 'expert'), split_axis=0, concat_axis=0, tile...  10.4 us
    ppermute x8, starting transfers between devices, swap_with(): return lax.ppermute(value, axis, pairs)  6.98 us
    pallas_call x1, Pallas kernels, per_device(): pl.pallas_call(functools.partial(stage_kernel, groups), out_shape=[pltpu....  2.82 us
    pallas_call x1, Pallas kernels, per_device(): pl.pallas_call(functools.partial(first_kernel, groups, leave_count), out_...  1.45 us
    ppermute x8, waiting for transfers between devices, swap_with(): return lax.ppermute(value, axis, pairs)  1.37 us
    pallas_call x1, Pallas kernels, per_device(): pl.pallas_call(delta_kernel, out_shape=[pltpu.VMEM((members, rows, piece)...  1.25 us
  transfers between devices with their start and end apart: 8, of which 2 were waited for; matrix products, arithmetic and copies ran while one was open for 0% of the time, Pallas kernels for 7%

profile of v3, /device:TPU:0, one launch (start us, length us, event | category | flops | bytes accessed | tf_op | source)
XLA Modules:
  0.0 51.0 jit_solution(6052540106190770774)
XLA Ops:
  0.0 1.5 %first.1 = (bf16[512,128]{1,0:T(8,128)(2,1)S(1)}, bf16[192,128]{1,0:T(8,128)(2,1)S(1)}, bf16[192,128]{1,0:T(8,128)(2,1)S(1)}, bf16[192,128]{1,0:T(8,128)(2,1)S(1...) custom-call(s32[4,16]{1,0:T(4,128)} %bitcast.12, ...), custom_call_target="tpu_custom_call" | custom-call | bytes 8388608 | tf_op jit(solution)/shard_map/first/pallas_call | solution.py:373
  1.5 3.0 %collective-permute-start = (bf16[512,128]{1,0:T(8,128)(2,1)S(1)}, bf16[512,128]{1,0:T(8,128)(2,1)S(1)}, u32[]{:S(2)}, u32[]{:S(2)}) collective-permute-start(bf16[512,128]{1,0:T(8,128)(2,1)S(1)} %get-tuple-element.35), channel_id=1, source_target_pairs={{0,1},{1,0},{2,3},{3,2},{4,5},{5,4},{6,7},{7,6},{8,9},{9,8},{10,11... | collective-permute-start | bytes 393224 | tf_op jit(solution)/shard_map/ppermute | solution.py:41
  4.5 0.0 collective-permute-start.1
  4.5 1.5 %collective-permute-start.2 = (bf16[192,128]{1,0:T(8,128)(2,1)S(1)}, bf16[192,128]{1,0:T(8,128)(2,1)S(1)}, u32[]{:S(2)}, u32[]{:S(2)}) collective-permute-start(bf16[192,128]{1,0:T(8,128)(2,1)S(1)} %get-tuple-element.39), channel_id=1, source_target_pairs={{0,16},{8,24},{16,0},{24,8},{1,17},{9,25},{17,1},{25,9},{2,18},{10... | collective-permute-start | bytes 147464 | tf_op jit(solution)/shard_map/ppermute | solution.py:41
  6.0 0.4 collective-permute-start.3
  6.4 2.8 %stage.1 = (bf16[128,2048]{1,0:T(8,128)(2,1)S(1)}, f32[1,128]{1,0:T(1,128)S(1)}, f32[1,2048]{1,0:T(1,128)S(1)}, f32[16,256]{1,0:T(8,128)S(1)}, f32[1,256]{1,0:T(...) custom-call(bf16[16,2048]{1,0:T(8,128)(2,1)S(1)} %get-tuple-element.36.hidden, f32[1,2048]{1,0:T(1,128)} %bitcast.7, ...), custom_call_target="tpu_custom_call" | custom-call | bytes 8388608 | tf_op jit(solution)/shard_map/stage/pallas_call | solution.py:401
  9.2 0.0 collective-permute-done.1.refs_0_
  9.2 0.0 collective-permute-done.2.refs_1_
  9.2 0.5 collective-permute-done.3.refs_2_
  9.7 0.0 collective-permute-done.other_qk
  9.7 0.2 project.1
  9.9 0.2 collective-permute-start.4
  10.1 1.2 %collective-permute-start.5 = (f32[16,640]{1,0:T(8,128)S(1)}, f32[16,640]{1,0:T(8,128)S(1)}, u32[]{:S(2)}, u32[]{:S(2)}) collective-permute-start(f32[16,640]{1,0:T(8,128)S(1)} %get-tuple-element.48), channel_id=1, source_target_pairs={{0,16},{8,24},{16,0},{24,8},{1,17},{9,25},{17,1},{25,9},{2,18},{10... | collective-permute-start | bytes 122888 | tf_op jit(solution)/shard_map/ppermute | solution.py:41
  11.3 0.6 %collective-permute-start.6 = (f32[16,640]{1,0:T(8,128)S(1)}, f32[16,640]{1,0:T(8,128)S(1)}, u32[]{:S(2)}, u32[]{:S(2)}) collective-permute-start(f32[16,640]{1,0:T(8,128)S(1)} %get-tuple-element.49), channel_id=1, source_target_pairs={{0,24},{8,16},{16,8},{24,0},{1,25},{9,17},{17,9},{25,1},{2,26},{10... | collective-permute-start | bytes 122888 | tf_op jit(solution)/shard_map/ppermute | solution.py:41
  13.2 0.9 %settle.1 = (f32[16,128,128]{2,1,0:T(8,128)S(1)}, f32[2,128]{1,0:T(2,128)S(1)}) custom-call(s32[4,16]{1,0:T(4,128)} %bitcast.13, f32[1]{0:T(128)S(6)} %copy.20.a_log, f32[1]{0:T(128)S(6)} %copy.21.dt_bias, f32[16,128,128]{2,1,0:T(8,128)S(1)} %get-tuple-element.31.states, ...), custom_call_target="tpu_custom_call", output_to_operand_aliasing={{0}: (3, {})} | custom-call | bytes 8388608 | tf_op jit(solution)/shard_map/settle/pallas_call | solution.py:436
  14.1 0.0 collective-permute-done.4.refs_1_
  14.1 0.0 collective-permute-done.5.refs_2_
  14.2 0.8 %collective-permute-done.6.refs_3_ = f32[16,640]{1,0:T(8,128)S(1)} collective-permute-done((f32[16,640]{1,0:T(8,128)S(1)}, f32[16,640]{1,0:T(8,128)S(1)}, u32[]{:S(2)}, u32[]{:S(2)}) %collective-permute-start.6) | collective-permute-done | bytes 40992 | tf_op jit(solution)/shard_map/ppermute | solution.py:41
  15.0 1.2 %delta.1 = (bf16[8,16,256]{2,1,0:T(8,128)(2,1)S(1)}, bf16[3088,512]{1,0:T(8,128)(2,1)S(1)}) custom-call(f32[2,128]{1,0:T(2,128)S(1)} %get-tuple-element.42.mixing, f32[1,128]{1,0:T(1,128)S(1)} %get-tuple-element.43.head_gain, bf16[128,2048]{1,0:T(8,128)(2,1)S(1)} %get-tuple-element.44.w_out, ...), custom_call_target="tpu_custom_call", output_to_operand_aliasing={{1}: (4, {})} | custom-call | bytes 8388608 | tf_op jit(solution)/shard_map/delta/pallas_call | solution.py:452
  16.2 0.2 collective-permute-start.7
  16.4 11.6 %all_to_all.15.attention = bf16[8,16,256]{2,1,0:T(8,128)(2,1)S(1)} all-to-all(bf16[8,16,256]{2,1,0:T(8,128)(2,1)S(1)} %get-tuple-element.50), channel_id=1, replica_groups=mesh['parts'=1,'x'=2,'core'=2,'expert'=8] {'expert'}, dimensions={0} | all-to-all | bytes 131072 | tf_op jit(solution)/shard_map/all_to_all | solution.py:467
  28.0 10.4 %all_to_all.16.every = bf16[16,16,256]{2,1,0:T(8,128)(2,1)S(1)} all-to-all(bf16[16,16,256]{2,1,0:T(8,128)(2,1)S(1)} %get-tuple-element.52), channel_id=1, replica_groups=mesh['parts'=1,'x'=2,'core'=2,'expert'=8] {'x','expert'}, dimensions={0} | all-to-all | bytes 262144 | tf_op jit(solution)/shard_map/all_to_all | solution.py:481
  38.4 0.0 collective-permute-done.7.other
  38.4 1.2 %experts.1 = bf16[16,40,128]{2,1,0:T(8,128)(2,1)S(1)} custom-call(bf16[16,16,256]{2,1,0:T(8,128)(2,1)S(1)} %all_to_all.16.every, f32[32,128]{1,0:T(8,128)S(1)} %get-tuple-element.53.hits, f32[1,2048]{1,0:T(1,128)S(1)} %get-tuple-element.54.gain, bf16[3088,512]{1,0:T(8,128)(2,1)S(1)} %get-tuple-element.55.own, bf16[3088,512]{1,0:T(8,128)(2,1)S(1)} %collective-permute-done.7.other), custom_call_target="tpu_custom_call" | custom-call | bytes 8388608 | tf_op jit(solution)/shard_map/experts/pallas_call | solution.py:484
  39.7 10.5 %all_to_all.17.back = bf16[16,40,128]{2,1,0:T(8,128)(2,1)S(1)} all-to-all(bf16[16,40,128]{2,1,0:T(8,128)(2,1)S(1)} %experts.1), channel_id=1, replica_groups=mesh['parts'=1,'x'=2,'core'=2,'expert'=8] {'x','expert'}, dimensions={0} | all-to-all | bytes 327680 | tf_op jit(solution)/shard_map/all_to_all | solution.py:493
  50.2 0.8 %finish.1 = bf16[16,256]{1,0:T(8,128)(2,1)} custom-call(bf16[16,40,128]{2,1,0:T(8,128)(2,1)S(1)} %all_to_all.17.back, f32[16,256]{1,0:T(8,128)S(1)} %get-tuple-element.56.residual), custom_call_target="tpu_custom_call" | custom-call | bytes 8388608 | tf_op jit(solution)/shard_map/finish/pallas_call | solution.py:494
  (1 shorter events, 0.0 us)
Async XLA Ops:
  1.5 8.2 %collective-permute-start = (bf16[512,128]{1,0:T(8,128)(2,1)S(1)}, bf16[512,128]{1,0:T(8,128)(2,1)S(1)}, u32[]{:S(2)}, u32[]{:S(2)}) collective-permute-start(bf16[512,128]{1,0:T(8,128)(2,1)S(1)} %get-tuple-element.35), channel_id=1, source_target_pairs={{0,1},{1,0},{2,3},{3,2},{4,5},{5,4},{6,7},{7,6},{8,9},{9,8},{10,11... | collective-permute-start | bytes 393224 | tf_op jit(solution)/shard_map/ppermute | solution.py:41
  4.5 4.7 %collective-permute-start.1 = (bf16[192,128]{1,0:T(8,128)(2,1)S(1)}, bf16[192,128]{1,0:T(8,128)(2,1)S(1)}, u32[]{:S(2)}, u32[]{:S(2)}) collective-permute-start(bf16[192,128]{1,0:T(8,128)(2,1)S(1)} %get-tuple-element.38), channel_id=1, source_target_pairs={{0,8},{8,0},{16,24},{24,16},{1,9},{9,1},{17,25},{25,17},{2,10},{10... | collective-permute-start | bytes 147464 | tf_op jit(solution)/shard_map/ppermute | solution.py:41
  4.5 4.7 %collective-permute-start.2 = (bf16[192,128]{1,0:T(8,128)(2,1)S(1)}, bf16[192,128]{1,0:T(8,128)(2,1)S(1)}, u32[]{:S(2)}, u32[]{:S(2)}) collective-permute-start(bf16[192,128]{1,0:T(8,128)(2,1)S(1)} %get-tuple-element.39), channel_id=1, source_target_pairs={{0,16},{8,24},{16,0},{24,8},{1,17},{9,25},{17,1},{25,9},{2,18},{10... | collective-permute-start | bytes 147464 | tf_op jit(solution)/shard_map/ppermute | solution.py:41
  6.0 3.7 %collective-permute-start.3 = (bf16[192,128]{1,0:T(8,128)(2,1)S(1)}, bf16[192,128]{1,0:T(8,128)(2,1)S(1)}, u32[]{:S(2)}, u32[]{:S(2)}) collective-permute-start(bf16[192,128]{1,0:T(8,128)(2,1)S(1)} %get-tuple-element.40), channel_id=1, source_target_pairs={{0,24},{8,16},{16,8},{24,0},{1,25},{9,17},{17,9},{25,1},{2,26},{10... | collective-permute-start | bytes 147464 | tf_op jit(solution)/shard_map/ppermute | solution.py:41
  9.9 4.2 %collective-permute-start.4 = (f32[16,640]{1,0:T(8,128)S(1)}, f32[16,640]{1,0:T(8,128)S(1)}, u32[]{:S(2)}, u32[]{:S(2)}) collective-permute-start(f32[16,640]{1,0:T(8,128)S(1)} %get-tuple-element.47), channel_id=1, source_target_pairs={{0,8},{8,0},{16,24},{24,16},{1,9},{9,1},{17,25},{25,17},{2,10},{10... | collective-permute-start | bytes 122888 | tf_op jit(solution)/shard_map/ppermute | solution.py:41
  10.1 4.0 %collective-permute-start.5 = (f32[16,640]{1,0:T(8,128)S(1)}, f32[16,640]{1,0:T(8,128)S(1)}, u32[]{:S(2)}, u32[]{:S(2)}) collective-permute-start(f32[16,640]{1,0:T(8,128)S(1)} %get-tuple-element.48), channel_id=1, source_target_pairs={{0,16},{8,24},{16,0},{24,8},{1,17},{9,25},{17,1},{25,9},{2,18},{10... | collective-permute-start | bytes 122888 | tf_op jit(solution)/shard_map/ppermute | solution.py:41
  11.3 3.7 %collective-permute-start.6 = (f32[16,640]{1,0:T(8,128)S(1)}, f32[16,640]{1,0:T(8,128)S(1)}, u32[]{:S(2)}, u32[]{:S(2)}) collective-permute-start(f32[16,640]{1,0:T(8,128)S(1)} %get-tuple-element.49), channel_id=1, source_target_pairs={{0,24},{8,16},{16,8},{24,0},{1,25},{9,17},{17,9},{25,1},{2,26},{10... | collective-permute-start | bytes 122888 | tf_op jit(solution)/shard_map/ppermute | solution.py:41
  16.2 22.2 %collective-permute-start.7 = (bf16[3088,512]{1,0:T(8,128)(2,1)S(1)}, bf16[3088,512]{1,0:T(8,128)(2,1)S(1)}, u32[]{:S(2)}, u32[]{:S(2)}) collective-permute-start(bf16[3088,512]{1,0:T(8,128)(2,1)S(1)} %get-tuple-element.55.own), channel_id=1, source_target_pairs={{0,8},{8,0},{1,9},{9,1},{2,10},{10,2},{3,11},{11,3},{4,12},{12,4},... | collective-permute-start | bytes 9486344 | tf_op jit(solution)/shard_map/ppermute | solution.py:41

commit v4 on v3

--- a/solution.py
+++ b/solution.py
@@ -91,9 +91,9 @@
         copy.wait()
 
 
-def project_kernel(groups, normed, w_ba, w_qkvz, other_qk, staged, *refs):
-    messages, outs, scaled = refs[: groups - 1], refs[groups - 1 : -1], refs[-1]
-    del staged
+def project_kernel(groups, normed, w_ba, w_qkvz, *refs):
+    messages, outs, scaled = refs[: groups - 1][::-1], refs[groups + 1 : -1], refs[-1]
+    other_qk = refs[groups - 1]
     group = group_index()
     depth = w_qkvz.shape[0]
     rows = normed.shape[0]
@@ -424,13 +424,13 @@
     partials = pl.pallas_call(
         functools.partial(project_kernel, groups),
         out_shape=[pltpu.VMEM((rows, SENT), F32)] * groups,
-        in_specs=[VMEM] * 4 + [ANY] + [VMEM] * (groups - 1),
+        in_specs=[VMEM] * (3 + groups) + [ANY],
         out_specs=[VMEM] * groups,
         scratch_shapes=[pltpu.VMEM((total_rows, depth), BF)],
         compiler_params=PARAMS,
         cost_estimate=COST,
         name="project",
-    )(normed, w_ba_near, w_near, other_qk, own_gain, *messages)
+    )(normed, w_ba_near, w_near, *messages[::-1], other_qk, own_gain)
     after = partials[0]
     partials = [partials[0]] + [swap_with(partials[i], dp, i) for i in range(1, groups)]
     held, mixing = pl.pallas_call(
@@ -462,7 +462,7 @@
         compiler_params=PARAMS,
         cost_estimate=COST,
         name="delta",
-    )(mixing, head_gain_near, w_out_near, held, expert, *partials)
+    )(mixing, head_gain_near, w_out_near, held, expert, *partials[::-1])
     other_expert = swap_with(expert, "core", 1)
     attention = lax.all_to_all(attention, "expert", split_axis=0, concat_axis=0, tiled=True)
 

time: 51.4 us -> 51.1 us (level)
  no operation moved by 1% of the time
where the time goes in v4:
time: 51.1 us; the launch traced here: 50.7 us
  blocking collectives  32.5 us (64%)
  Pallas kernels  8.78 us (17%)
  starting transfers between devices  6.89 us (13%)
  between operations  1.37 us (3%)
  waiting for transfers between devices  1.18 us (2%)
    all_to_all x1, blocking collectives, per_device(): lax.all_to_all(attention, 'expert', split_axis=0, concat_axis=0, tiled=True)  11.6 us
    all_to_all x1, blocking collectives, per_device(): lax.all_to_all(sent, ('x', 'expert'), split_axis=0, concat_axis=0, tiled=...  10.5 us
    all_to_all x1, blocking collectives, per_device(): lax.all_to_all(gained, ('x', 'expert'), split_axis=0, concat_axis=0, tile...  10.4 us
    ppermute x8, starting transfers between devices, swap_with(): return lax.ppermute(value, axis, pairs)  6.89 us
    pallas_call x1, Pallas kernels, per_device(): pl.pallas_call(functools.partial(stage_kernel, groups), out_shape=[pltpu....  2.82 us
    pallas_call x1, Pallas kernels, per_device(): pl.pallas_call(functools.partial(first_kernel, groups, leave_count), out_...  1.45 us
    pallas_call x1, Pallas kernels, per_device(): pl.pallas_call(delta_kernel, out_shape=[pltpu.VMEM((members, rows, piece)...  1.25 us
    pallas_call x1, Pallas kernels, per_device(): pl.pallas_call(functools.partial(expert_kernel, width), out_shape=pltpu.V...  1.24 us
  transfers between devices with their start and end apart: 8, of which 2 were waited for; matrix products, arithmetic and copies ran while one was open for 0% of the time, Pallas kernels for 7%

profile of v4, /device:TPU:0, one launch (start us, length us, event | category | flops | bytes accessed | tf_op | source)
XLA Modules:
  0.0 50.7 jit_solution(13017372073159237441)
XLA Ops:
  0.0 1.5 %first.1 = (bf16[512,128]{1,0:T(8,128)(2,1)S(1)}, bf16[192,128]{1,0:T(8,128)(2,1)S(1)}, bf16[192,128]{1,0:T(8,128)(2,1)S(1)}, bf16[192,128]{1,0:T(8,128)(2,1)S(1...) custom-call(s32[4,16]{1,0:T(4,128)} %bitcast.12, ...), custom_call_target="tpu_custom_call" | custom-call | bytes 8388608 | tf_op jit(solution)/shard_map/first/pallas_call | solution.py:373
  1.5 3.0 %collective-permute-start.3 = (bf16[512,128]{1,0:T(8,128)(2,1)S(1)}, bf16[512,128]{1,0:T(8,128)(2,1)S(1)}, u32[]{:S(2)}, u32[]{:S(2)}) collective-permute-start(bf16[512,128]{1,0:T(8,128)(2,1)S(1)} %get-tuple-element.38), channel_id=1, source_target_pairs={{0,1},{1,0},{2,3},{3,2},{4,5},{5,4},{6,7},{7,6},{8,9},{9,8},{10,11... | collective-permute-start | bytes 393224 | tf_op jit(solution)/shard_map/ppermute | solution.py:41
  4.5 0.7 %collective-permute-start = (bf16[192,128]{1,0:T(8,128)(2,1)S(1)}, bf16[192,128]{1,0:T(8,128)(2,1)S(1)}, u32[]{:S(2)}, u32[]{:S(2)}) collective-permute-start(bf16[192,128]{1,0:T(8,128)(2,1)S(1)} %get-tuple-element.35), channel_id=1, source_target_pairs={{0,24},{8,16},{16,8},{24,0},{1,25},{9,17},{17,9},{25,1},{2,26},{10... | collective-permute-start | bytes 147464 | tf_op jit(solution)/shard_map/ppermute | solution.py:41
  5.1 0.9 %collective-permute-start.1 = (bf16[192,128]{1,0:T(8,128)(2,1)S(1)}, bf16[192,128]{1,0:T(8,128)(2,1)S(1)}, u32[]{:S(2)}, u32[]{:S(2)}) collective-permute-start(bf16[192,128]{1,0:T(8,128)(2,1)S(1)} %get-tuple-element.36), channel_id=1, source_target_pairs={{0,16},{8,24},{16,0},{24,8},{1,17},{9,25},{17,1},{25,9},{2,18},{10... | collective-permute-start | bytes 147464 | tf_op jit(solution)/shard_map/ppermute | solution.py:41
  6.0 0.3 collective-permute-start.2
  6.4 2.8 %stage.1 = (bf16[128,2048]{1,0:T(8,128)(2,1)S(1)}, f32[1,128]{1,0:T(1,128)S(1)}, f32[1,2048]{1,0:T(1,128)S(1)}, f32[16,256]{1,0:T(8,128)S(1)}, f32[1,256]{1,0:T(...) custom-call(bf16[16,2048]{1,0:T(8,128)(2,1)S(1)} %get-tuple-element.39.hidden, f32[1,2048]{1,0:T(1,128)} %bitcast.7, ...), custom_call_target="tpu_custom_call" | custom-call | bytes 8388608 | tf_op jit(solution)/shard_map/stage/pallas_call | solution.py:401
  9.2 0.0 collective-permute-done.refs_0_.refs_2_
  9.2 0.6 %collective-permute-done.1.refs_1_ = bf16[192,128]{1,0:T(8,128)(2,1)S(1)} collective-permute-done((bf16[192,128]{1,0:T(8,128)(2,1)S(1)}, bf16[192,128]{1,0:T(8,128)(2,1)S(1)}, u32[]{:S(2)}, u32[]{:S(2)}) %collective-permute-start.1) | collective-permute-done | bytes 49184 | tf_op jit(solution)/shard_map/ppermute | solution.py:41
  9.7 0.0 collective-permute-done.2.refs_2_.refs_0_
  9.7 0.0 collective-permute-done.3.refs_3_
  9.8 0.2 project.1
  10.0 0.6 %collective-permute-start.4 = (f32[16,640]{1,0:T(8,128)S(1)}, f32[16,640]{1,0:T(8,128)S(1)}, u32[]{:S(2)}, u32[]{:S(2)}) collective-permute-start(f32[16,640]{1,0:T(8,128)S(1)} %get-tuple-element.47), channel_id=1, source_target_pairs={{0,24},{8,16},{16,8},{24,0},{1,25},{9,17},{17,9},{25,1},{2,26},{10... | collective-permute-start | bytes 122888 | tf_op jit(solution)/shard_map/ppermute | solution.py:41
  10.6 1.2 %collective-permute-start.5 = (f32[16,640]{1,0:T(8,128)S(1)}, f32[16,640]{1,0:T(8,128)S(1)}, u32[]{:S(2)}, u32[]{:S(2)}) collective-permute-start(f32[16,640]{1,0:T(8,128)S(1)} %get-tuple-element.48), channel_id=1, source_target_pairs={{0,16},{8,24},{16,0},{24,8},{1,17},{9,25},{17,1},{25,9},{2,18},{10... | collective-permute-start | bytes 122888 | tf_op jit(solution)/shard_map/ppermute | solution.py:41
  11.8 0.1 collective-permute-start.6
  13.2 0.9 %settle.1 = (f32[16,128,128]{2,1,0:T(8,128)S(1)}, f32[2,128]{1,0:T(2,128)S(1)}) custom-call(s32[4,16]{1,0:T(4,128)} %bitcast.13, f32[1]{0:T(128)S(6)} %copy.20.a_log, f32[1]{0:T(128)S(6)} %copy.21.dt_bias, f32[16,128,128]{2,1,0:T(8,128)S(1)} %get-tuple-element.31.states, ...), custom_call_target="tpu_custom_call", output_to_operand_aliasing={{0}: (3, {})} | custom-call | bytes 8388608 | tf_op jit(solution)/shard_map/settle/pallas_call | solution.py:436
  14.2 0.0 collective-permute-done.4.refs_0_
  14.2 0.6 %collective-permute-done.5.refs_1_ = f32[16,640]{1,0:T(8,128)S(1)} collective-permute-done((f32[16,640]{1,0:T(8,128)S(1)}, f32[16,640]{1,0:T(8,128)S(1)}, u32[]{:S(2)}, u32[]{:S(2)}) %collective-permute-start.5) | collective-permute-done | bytes 40992 | tf_op jit(solution)/shard_map/ppermute | solution.py:41
  14.8 0.0 collective-permute-done.6.refs_2_
  14.8 1.2 %delta.1 = (bf16[8,16,256]{2,1,0:T(8,128)(2,1)S(1)}, bf16[3088,512]{1,0:T(8,128)(2,1)S(1)}) custom-call(f32[2,128]{1,0:T(2,128)S(1)} %get-tuple-element.42.mixing, f32[1,128]{1,0:T(1,128)S(1)} %get-tuple-element.43.head_gain, bf16[128,2048]{1,0:T(8,128)(2,1)S(1)} %get-tuple-element.44.w_out, ...), custom_call_target="tpu_custom_call", output_to_operand_aliasing={{1}: (4, {})} | custom-call | bytes 8388608 | tf_op jit(solution)/shard_map/delta/pallas_call | solution.py:452
  16.0 0.1 collective-permute-start.7
  16.1 11.6 %all_to_all.15.attention = bf16[8,16,256]{2,1,0:T(8,128)(2,1)S(1)} all-to-all(bf16[8,16,256]{2,1,0:T(8,128)(2,1)S(1)} %get-tuple-element.50), channel_id=1, replica_groups=mesh['parts'=1,'x'=2,'core'=2,'expert'=8] {'expert'}, dimensions={0} | all-to-all | bytes 131072 | tf_op jit(solution)/shard_map/all_to_all | solution.py:467
  27.7 10.4 %all_to_all.16.every = bf16[16,16,256]{2,1,0:T(8,128)(2,1)S(1)} all-to-all(bf16[16,16,256]{2,1,0:T(8,128)(2,1)S(1)} %get-tuple-element.52), channel_id=1, replica_groups=mesh['parts'=1,'x'=2,'core'=2,'expert'=8] {'x','expert'}, dimensions={0} | all-to-all | bytes 262144 | tf_op jit(solution)/shard_map/all_to_all | solution.py:481
  38.1 0.0 collective-permute-done.7.other
  38.1 1.2 %experts.1 = bf16[16,40,128]{2,1,0:T(8,128)(2,1)S(1)} custom-call(bf16[16,16,256]{2,1,0:T(8,128)(2,1)S(1)} %all_to_all.16.every, f32[32,128]{1,0:T(8,128)S(1)} %get-tuple-element.53.hits, f32[1,2048]{1,0:T(1,128)S(1)} %get-tuple-element.54.gain, bf16[3088,512]{1,0:T(8,128)(2,1)S(1)} %get-tuple-element.55.own, bf16[3088,512]{1,0:T(8,128)(2,1)S(1)} %collective-permute-done.7.other), custom_call_target="tpu_custom_call" | custom-call | bytes 8388608 | tf_op jit(solution)/shard_map/experts/pallas_call | solution.py:484
  39.4 10.5 %all_to_all.17.back = bf16[16,40,128]{2,1,0:T(8,128)(2,1)S(1)} all-to-all(bf16[16,40,128]{2,1,0:T(8,128)(2,1)S(1)} %experts.1), channel_id=1, replica_groups=mesh['parts'=1,'x'=2,'core'=2,'expert'=8] {'x','expert'}, dimensions={0} | all-to-all | bytes 327680 | tf_op jit(solution)/shard_map/all_to_all | solution.py:493
  49.9 0.8 %finish.1 = bf16[16,256]{1,0:T(8,128)(2,1)} custom-call(bf16[16,40,128]{2,1,0:T(8,128)(2,1)S(1)} %all_to_all.17.back, f32[16,256]{1,0:T(8,128)S(1)} %get-tuple-element.56.residual), custom_call_target="tpu_custom_call" | custom-call | bytes 8388608 | tf_op jit(solution)/shard_map/finish/pallas_call | solution.py:494
  (1 shorter events, 0.0 us)
Async XLA Ops:
  1.5 8.3 %collective-permute-start.3 = (bf16[512,128]{1,0:T(8,128)(2,1)S(1)}, bf16[512,128]{1,0:T(8,128)(2,1)S(1)}, u32[]{:S(2)}, u32[]{:S(2)}) collective-permute-start(bf16[512,128]{1,0:T(8,128)(2,1)S(1)} %get-tuple-element.38), channel_id=1, source_target_pairs={{0,1},{1,0},{2,3},{3,2},{4,5},{5,4},{6,7},{7,6},{8,9},{9,8},{10,11... | collective-permute-start | bytes 393224 | tf_op jit(solution)/shard_map/ppermute | solution.py:41
  4.5 4.7 %collective-permute-start = (bf16[192,128]{1,0:T(8,128)(2,1)S(1)}, bf16[192,128]{1,0:T(8,128)(2,1)S(1)}, u32[]{:S(2)}, u32[]{:S(2)}) collective-permute-start(bf16[192,128]{1,0:T(8,128)(2,1)S(1)} %get-tuple-element.35), channel_id=1, source_target_pairs={{0,24},{8,16},{16,8},{24,0},{1,25},{9,17},{17,9},{25,1},{2,26},{10... | collective-permute-start | bytes 147464 | tf_op jit(solution)/shard_map/ppermute | solution.py:41
  5.1 4.6 %collective-permute-start.1 = (bf16[192,128]{1,0:T(8,128)(2,1)S(1)}, bf16[192,128]{1,0:T(8,128)(2,1)S(1)}, u32[]{:S(2)}, u32[]{:S(2)}) collective-permute-start(bf16[192,128]{1,0:T(8,128)(2,1)S(1)} %get-tuple-element.36), channel_id=1, source_target_pairs={{0,16},{8,24},{16,0},{24,8},{1,17},{9,25},{17,1},{25,9},{2,18},{10... | collective-permute-start | bytes 147464 | tf_op jit(solution)/shard_map/ppermute | solution.py:41
  6.0 3.7 %collective-permute-start.2 = (bf16[192,128]{1,0:T(8,128)(2,1)S(1)}, bf16[192,128]{1,0:T(8,128)(2,1)S(1)}, u32[]{:S(2)}, u32[]{:S(2)}) collective-permute-start(bf16[192,128]{1,0:T(8,128)(2,1)S(1)} %get-tuple-element.37), channel_id=1, source_target_pairs={{0,8},{8,0},{16,24},{24,16},{1,9},{9,1},{17,25},{25,17},{2,10},{10... | collective-permute-start | bytes 147464 | tf_op jit(solution)/shard_map/ppermute | solution.py:41
  10.0 4.2 %collective-permute-start.4 = (f32[16,640]{1,0:T(8,128)S(1)}, f32[16,640]{1,0:T(8,128)S(1)}, u32[]{:S(2)}, u32[]{:S(2)}) collective-permute-start(f32[16,640]{1,0:T(8,128)S(1)} %get-tuple-element.47), channel_id=1, source_target_pairs={{0,24},{8,16},{16,8},{24,0},{1,25},{9,17},{17,9},{25,1},{2,26},{10... | collective-permute-start | bytes 122888 | tf_op jit(solution)/shard_map/ppermute | solution.py:41
  10.6 4.2 %collective-permute-start.5 = (f32[16,640]{1,0:T(8,128)S(1)}, f32[16,640]{1,0:T(8,128)S(1)}, u32[]{:S(2)}, u32[]{:S(2)}) collective-permute-start(f32[16,640]{1,0:T(8,128)S(1)} %get-tuple-element.48), channel_id=1, source_target_pairs={{0,16},{8,24},{16,0},{24,8},{1,17},{9,25},{17,1},{25,9},{2,18},{10... | collective-permute-start | bytes 122888 | tf_op jit(solution)/shard_map/ppermute | solution.py:41
  11.8 3.0 %collective-permute-start.6 = (f32[16,640]{1,0:T(8,128)S(1)}, f32[16,640]{1,0:T(8,128)S(1)}, u32[]{:S(2)}, u32[]{:S(2)}) collective-permute-start(f32[16,640]{1,0:T(8,128)S(1)} %get-tuple-element.49), channel_id=1, source_target_pairs={{0,8},{8,0},{16,24},{24,16},{1,9},{9,1},{17,25},{25,17},{2,10},{10... | collective-permute-start | bytes 122888 | tf_op jit(solution)/shard_map/ppermute | solution.py:41
  16.0 22.1 %collective-permute-start.7 = (bf16[3088,512]{1,0:T(8,128)(2,1)S(1)}, bf16[3088,512]{1,0:T(8,128)(2,1)S(1)}, u32[]{:S(2)}, u32[]{:S(2)}) collective-permute-start(bf16[3088,512]{1,0:T(8,128)(2,1)S(1)} %get-tuple-element.55.own), channel_id=1, source_target_pairs={{0,8},{8,0},{1,9},{9,1},{2,10},{10,2},{3,11},{11,3},{4,12},{12,4},... | collective-permute-start | bytes 9486344 | tf_op jit(solution)/shard_map/ppermute | solution.py:41

commit v5 on v4

--- a/solution.py
+++ b/solution.py
@@ -168,22 +168,24 @@
         copy.wait()
 
 
+def store_split(out, row, state):
+    high = state.astype(BF)
+    where = pl.ds(pl.multiple_of(row * DK, DK), DK)
+    out[where, :DV] = high
+    out[where, DV:] = (state - high.astype(F32)).astype(BF)
+
+
 def settle_kernel(groups, leave_count, migration, a_log, dt_bias, states, after, *refs):
-    messages, (held, mixing, own_state, plan, plan_sem) = refs[:-5], refs[-5:]
+    messages, (split, mixing, plan, plan_sem) = refs[:-4], refs[-4:]
     del after
     plan_copy = pltpu.make_async_copy(migration, plan, plan_sem)
     plan_copy.start()
     mixing[0:1, :] = jnp.exp(jnp.full((1, LANES), a_log[0], F32))
     mixing[1:2, :] = jnp.full((1, LANES), dt_bias[0], F32)
     group = group_index()
+    for r in range(states.shape[0]):
+        store_split(split, r, states[r])
     plan_copy.wait()
-    for j in range(leave_count):
-        at = group * leave_count + j
-
-        @pl.when(plan[2, at] == group)
-        def _():
-            own_state[...] = states[plan[1, at]]
-
     for i in range(groups):
         for j in range(leave_count):
             at = (group ^ i) * leave_count + j
@@ -191,17 +193,18 @@
             @pl.when(plan[2, at] == group)
             def _():
                 if i == 0:
-                    held[plan[3, at]] = own_state[...]
+                    state = states[plan[1, at]]
                 else:
                     arrival = messages[i - 1]
-                    held[plan[3, at]] = arrival[arrival.shape[0] - DK :, :].astype(F32)
-
-
-def delta_kernel(mixing, head_gain, w_out, held, expert, *refs):
-    partials, (out, passed, key_sums, query_sums) = refs[:-4], refs[-4:]
+                    state = arrival[arrival.shape[0] - DK :, :].astype(F32)
+                store_split(split, plan[3, at], state)
+
+
+def delta_kernel(mixing, head_gain, w_out, split, expert, *refs):
+    partials, (out, passed, blocks) = refs[:-3], refs[-3:]
     del expert, passed
     member = lax.axis_index("expert")
-    rows = held.shape[0]
+    rows = split.shape[0] // DK
     summed = partials[0][...]
     for partial in partials[1:]:
         summed = summed + partial[...]
@@ -222,15 +225,19 @@
     soft = jnp.maximum(shifted, 0.0) + jnp.log1p(jnp.exp(-jnp.abs(shifted)))
     decay = jnp.exp(-mixing[0:1, 0:1] * soft)
     beta = jax.nn.sigmoid(write_mix)
-    keys_t = jnp.transpose(keys_unit)
-    queries_t = jnp.transpose(queries)
+    both = jnp.concatenate([keys_unit, queries], axis=0)
+    high = both.astype(BF).astype(F32)
+    both = jnp.concatenate([high, both - high], axis=0)
+    row = lax.broadcasted_iota(jnp.int32, both.shape, 0) % rows
     for r in range(rows):
-        state = held[r]
-        key_sums[r : r + 1, :] = jnp.sum(state * keys_t[:, r : r + 1], axis=0, keepdims=True)
-        query_sums[r : r + 1, :] = jnp.sum(state * queries_t[:, r : r + 1], axis=0, keepdims=True)
-    correction = (values - key_sums[...] * decay) * beta
+        blocks[:, r * DK : (r + 1) * DK] = jnp.where(row == r, both, 0.0).astype(BF)
+    sums = jnp.dot(blocks[...], split[...], preferred_element_type=F32)
+    sums = sums[:, :DV] + sums[:, DV:]
+    sums = sums[: 2 * rows] + sums[2 * rows :]
+    key_sums, query_sums = sums[:rows], sums[rows:]
+    correction = (values - key_sums * decay) * beta
     overlap = jnp.sum(queries * keys_unit, axis=1, keepdims=True)
-    readout = query_sums[...] * decay + overlap * correction
+    readout = query_sums * decay + overlap * correction
     normed = readout * row_scale(readout) * head_gain[...]
     gated = (normed * (out_gate * jax.nn.sigmoid(out_gate))).astype(BF)
     attention = jnp.dot(gated, w_out[...], preferred_element_type=F32).astype(BF)
@@ -433,17 +440,12 @@
     )(normed, w_ba_near, w_near, *messages[::-1], other_qk, own_gain)
     after = partials[0]
     partials = [partials[0]] + [swap_with(partials[i], dp, i) for i in range(1, groups)]
-    held, mixing = pl.pallas_call(
+    split, mixing = pl.pallas_call(
         functools.partial(settle_kernel, groups, leave_count),
-        out_shape=[pltpu.VMEM((rows, DK, DV), F32), pltpu.VMEM((2, LANES), F32)],
+        out_shape=[pltpu.VMEM((rows * DK, 2 * DV), BF), pltpu.VMEM((2, LANES), F32)],
         in_specs=[HBM] + [SMEM] * 2 + [VMEM, ANY] + [VMEM] * (groups - 1),
         out_specs=[VMEM] * 2,
-        scratch_shapes=[
-            pltpu.VMEM((DK, DV), F32),
-            pltpu.SMEM(plan.shape, jnp.int32),
-            pltpu.SemaphoreType.DMA,
-        ],
-        input_output_aliases={3: 0},
+        scratch_shapes=[pltpu.SMEM(plan.shape, jnp.int32), pltpu.SemaphoreType.DMA],
         compiler_params=PARAMS,
         cost_estimate=COST,
         name="settle",
@@ -457,12 +459,12 @@
         ],
         in_specs=[VMEM] * 4 + [ANY] + [VMEM] * groups,
         out_specs=[VMEM, ANY],
-        scratch_shapes=[pltpu.VMEM((rows, DV), F32)] * 2,
+        scratch_shapes=[pltpu.VMEM((4 * rows, rows * DK), BF)],
         input_output_aliases={4: 1},
         compiler_params=PARAMS,
         cost_estimate=COST,
         name="delta",
-    )(mixing, head_gain_near, w_out_near, held, expert, *partials[::-1])
+    )(mixing, head_gain_near, w_out_near, split, expert, *partials[::-1])
     other_expert = swap_with(expert, "core", 1)
     attention = lax.all_to_all(attention, "expert", split_axis=0, concat_axis=0, tiled=True)
 

time: 51.1 us -> 50.6 us (level)
  no operation moved by 1% of the time
where the time goes in v5:
time: 50.6 us; the launch traced here: 50.3 us
  blocking collectives  32.5 us (64%)
  Pallas kernels  8.34 us (16%)
  starting transfers between devices  6.9 us (14%)
  between operations  1.37 us (3%)
  waiting for transfers between devices  1.19 us (2%)
    all_to_all x1, blocking collectives, per_device(): lax.all_to_all(attention, 'expert', split_axis=0, concat_axis=0, tiled=True)  11.6 us
    all_to_all x1, blocking collectives, per_device(): lax.all_to_all(sent, ('x', 'expert'), split_axis=0, concat_axis=0, tiled=...  10.5 us
    all_to_all x1, blocking collectives, per_device(): lax.all_to_all(gained, ('x', 'expert'), split_axis=0, concat_axis=0, tile...  10.4 us
    ppermute x8, starting transfers between devices, swap_with(): return lax.ppermute(value, axis, pairs)  6.9 us
    pallas_call x1, Pallas kernels, per_device(): pl.pallas_call(functools.partial(stage_kernel, groups), out_shape=[pltpu....  2.82 us
    pallas_call x1, Pallas kernels, per_device(): pl.pallas_call(functools.partial(first_kernel, groups, leave_count), out_...  1.45 us
    pallas_call x1, Pallas kernels, per_device(): pl.pallas_call(functools.partial(expert_kernel, width), out_shape=pltpu.V...  1.24 us
    ppermute x8, waiting for transfers between devices, swap_with(): return lax.ppermute(value, axis, pairs)  1.19 us
  transfers between devices with their start and end apart: 8, of which 2 were waited for; matrix products, arithmetic and copies ran while one was open for 0% of the time, Pallas kernels for 7%

profile of v5, /device:TPU:0, one launch (start us, length us, event | category | flops | bytes accessed | tf_op | source)
XLA Modules:
  0.0 50.3 jit_solution(4995978263526682863)
XLA Ops:
  0.0 1.5 %first.1 = (bf16[512,128]{1,0:T(8,128)(2,1)S(1)}, bf16[192,128]{1,0:T(8,128)(2,1)S(1)}, bf16[192,128]{1,0:T(8,128)(2,1)S(1)}, bf16[192,128]{1,0:T(8,128)(2,1)S(1...) custom-call(s32[4,16]{1,0:T(4,128)} %bitcast.12, ...), custom_call_target="tpu_custom_call" | custom-call | bytes 8388608 | tf_op jit(solution)/shard_map/first/pallas_call | solution.py:380
  1.5 3.0 %collective-permute-start.3 = (bf16[512,128]{1,0:T(8,128)(2,1)S(1)}, bf16[512,128]{1,0:T(8,128)(2,1)S(1)}, u32[]{:S(2)}, u32[]{:S(2)}) collective-permute-start(bf16[512,128]{1,0:T(8,128)(2,1)S(1)} %get-tuple-element.38), channel_id=1, source_target_pairs={{0,1},{1,0},{2,3},{3,2},{4,5},{5,4},{6,7},{7,6},{8,9},{9,8},{10,11... | collective-permute-start | bytes 393224 | tf_op jit(solution)/shard_map/ppermute | solution.py:41
  4.5 0.7 %collective-permute-start = (bf16[192,128]{1,0:T(8,128)(2,1)S(1)}, bf16[192,128]{1,0:T(8,128)(2,1)S(1)}, u32[]{:S(2)}, u32[]{:S(2)}) collective-permute-start(bf16[192,128]{1,0:T(8,128)(2,1)S(1)} %get-tuple-element.35), channel_id=1, source_target_pairs={{0,24},{8,16},{16,8},{24,0},{1,25},{9,17},{17,9},{25,1},{2,26},{10... | collective-permute-start | bytes 147464 | tf_op jit(solution)/shard_map/ppermute | solution.py:41
  5.1 0.9 %collective-permute-start.1 = (bf16[192,128]{1,0:T(8,128)(2,1)S(1)}, bf16[192,128]{1,0:T(8,128)(2,1)S(1)}, u32[]{:S(2)}, u32[]{:S(2)}) collective-permute-start(bf16[192,128]{1,0:T(8,128)(2,1)S(1)} %get-tuple-element.36), channel_id=1, source_target_pairs={{0,16},{8,24},{16,0},{24,8},{1,17},{9,25},{17,1},{25,9},{2,18},{10... | collective-permute-start | bytes 147464 | tf_op jit(solution)/shard_map/ppermute | solution.py:41
  6.0 0.3 collective-permute-start.2
  6.4 2.8 %stage.1 = (bf16[128,2048]{1,0:T(8,128)(2,1)S(1)}, f32[1,128]{1,0:T(1,128)S(1)}, f32[1,2048]{1,0:T(1,128)S(1)}, f32[16,256]{1,0:T(8,128)S(1)}, f32[1,256]{1,0:T(...) custom-call(bf16[16,2048]{1,0:T(8,128)(2,1)S(1)} %get-tuple-element.39.hidden, f32[1,2048]{1,0:T(1,128)} %bitcast.7, ...), custom_call_target="tpu_custom_call" | custom-call | bytes 8388608 | tf_op jit(solution)/shard_map/stage/pallas_call | solution.py:408
  9.2 0.0 collective-permute-done.refs_0_.refs_2_
  9.2 0.6 %collective-permute-done.1.refs_1_ = bf16[192,128]{1,0:T(8,128)(2,1)S(1)} collective-permute-done((bf16[192,128]{1,0:T(8,128)(2,1)S(1)}, bf16[192,128]{1,0:T(8,128)(2,1)S(1)}, u32[]{:S(2)}, u32[]{:S(2)}) %collective-permute-start.1) | collective-permute-done | bytes 49184 | tf_op jit(solution)/shard_map/ppermute | solution.py:41
  9.7 0.0 collective-permute-done.2.refs_2_.refs_0_
  9.7 0.0 collective-permute-done.3.refs_3_
  9.8 0.2 project.1
  10.0 0.6 %collective-permute-start.4 = (f32[16,640]{1,0:T(8,128)S(1)}, f32[16,640]{1,0:T(8,128)S(1)}, u32[]{:S(2)}, u32[]{:S(2)}) collective-permute-start(f32[16,640]{1,0:T(8,128)S(1)} %get-tuple-element.47), channel_id=1, source_target_pairs={{0,24},{8,16},{16,8},{24,0},{1,25},{9,17},{17,9},{25,1},{2,26},{10... | collective-permute-start | bytes 122888 | tf_op jit(solution)/shard_map/ppermute | solution.py:41
  10.6 1.2 %collective-permute-start.5 = (f32[16,640]{1,0:T(8,128)S(1)}, f32[16,640]{1,0:T(8,128)S(1)}, u32[]{:S(2)}, u32[]{:S(2)}) collective-permute-start(f32[16,640]{1,0:T(8,128)S(1)} %get-tuple-element.48), channel_id=1, source_target_pairs={{0,16},{8,24},{16,0},{24,8},{1,17},{9,25},{17,1},{25,9},{2,18},{10... | collective-permute-start | bytes 122888 | tf_op jit(solution)/shard_map/ppermute | solution.py:41
  11.8 0.1 collective-permute-start.6
  13.2 0.9 %settle.1 = (bf16[2048,256]{1,0:T(8,128)(2,1)S(1)}, f32[2,128]{1,0:T(2,128)S(1)}) custom-call(s32[4,16]{1,0:T(4,128)} %bitcast.13, f32[1]{0:T(128)S(6)} %copy.18.a_log, f32[1]{0:T(128)S(6)} %copy.19.dt_bias, f32[16,128,128]{2,1,0:T(8,128)S(1)} %get-tuple-element.31.states, f32[16,640]{1,0:T(8,128)S(1)} %get-tuple-element.41.after.refs_3_, ...), custom_call_target="tpu_custom_call" | custom-call | bytes 8388608 | tf_op jit(solution)/shard_map/settle/pallas_call | solution.py:443
  14.2 0.0 collective-permute-done.4.refs_0_
  14.2 0.6 %collective-permute-done.5.refs_1_ = f32[16,640]{1,0:T(8,128)S(1)} collective-permute-done((f32[16,640]{1,0:T(8,128)S(1)}, f32[16,640]{1,0:T(8,128)S(1)}, u32[]{:S(2)}, u32[]{:S(2)}) %collective-permute-start.5) | collective-permute-done | bytes 40992 | tf_op jit(solution)/shard_map/ppermute | solution.py:41
  14.8 0.0 collective-permute-done.6.refs_2_
  14.8 0.8 %delta.1 = (bf16[8,16,256]{2,1,0:T(8,128)(2,1)S(1)}, bf16[3088,512]{1,0:T(8,128)(2,1)S(1)}) custom-call(f32[2,128]{1,0:T(2,128)S(1)} %get-tuple-element.42.mixing, f32[1,128]{1,0:T(1,128)S(1)} %get-tuple-element.43.head_gain, bf16[128,2048]{1,0:T(8,128)(2,1)S(1)} %get-tuple-element.44.w_out, ...), custom_call_target="tpu_custom_call", output_to_operand_aliasing={{1}: (4, {})} | custom-call | bytes 8388608 | tf_op jit(solution)/shard_map/delta/pallas_call | solution.py:454
  15.6 0.1 collective-permute-start.7
  15.7 11.6 %all_to_all.15.attention = bf16[8,16,256]{2,1,0:T(8,128)(2,1)S(1)} all-to-all(bf16[8,16,256]{2,1,0:T(8,128)(2,1)S(1)} %get-tuple-element.50), channel_id=1, replica_groups=mesh['parts'=1,'x'=2,'core'=2,'expert'=8] {'expert'}, dimensions={0} | all-to-all | bytes 131072 | tf_op jit(solution)/shard_map/all_to_all | solution.py:469
  27.3 10.4 %all_to_all.16.every = bf16[16,16,256]{2,1,0:T(8,128)(2,1)S(1)} all-to-all(bf16[16,16,256]{2,1,0:T(8,128)(2,1)S(1)} %get-tuple-element.52), channel_id=1, replica_groups=mesh['parts'=1,'x'=2,'core'=2,'expert'=8] {'x','expert'}, dimensions={0} | all-to-all | bytes 262144 | tf_op jit(solution)/shard_map/all_to_all | solution.py:483
  37.7 0.0 collective-permute-done.7.other
  37.7 1.2 %experts.1 = bf16[16,40,128]{2,1,0:T(8,128)(2,1)S(1)} custom-call(bf16[16,16,256]{2,1,0:T(8,128)(2,1)S(1)} %all_to_all.16.every, f32[32,128]{1,0:T(8,128)S(1)} %get-tuple-element.53.hits, f32[1,2048]{1,0:T(1,128)S(1)} %get-tuple-element.54.gain, bf16[3088,512]{1,0:T(8,128)(2,1)S(1)} %get-tuple-element.55.own, bf16[3088,512]{1,0:T(8,128)(2,1)S(1)} %collective-permute-done.7.other), custom_call_target="tpu_custom_call" | custom-call | bytes 8388608 | tf_op jit(solution)/shard_map/experts/pallas_call | solution.py:486
  38.9 10.5 %all_to_all.17.back = bf16[16,40,128]{2,1,0:T(8,128)(2,1)S(1)} all-to-all(bf16[16,40,128]{2,1,0:T(8,128)(2,1)S(1)} %experts.1), channel_id=1, replica_groups=mesh['parts'=1,'x'=2,'core'=2,'expert'=8] {'x','expert'}, dimensions={0} | all-to-all | bytes 327680 | tf_op jit(solution)/shard_map/all_to_all | solution.py:495
  49.5 0.8 %finish.1 = bf16[16,256]{1,0:T(8,128)(2,1)} custom-call(bf16[16,40,128]{2,1,0:T(8,128)(2,1)S(1)} %all_to_all.17.back, f32[16,256]{1,0:T(8,128)S(1)} %get-tuple-element.56.residual), custom_call_target="tpu_custom_call" | custom-call | bytes 8388608 | tf_op jit(solution)/shard_map/finish/pallas_call | solution.py:496
  (1 shorter events, 0.0 us)
Async XLA Ops:
  1.5 8.3 %collective-permute-start.3 = (bf16[512,128]{1,0:T(8,128)(2,1)S(1)}, bf16[512,128]{1,0:T(8,128)(2,1)S(1)}, u32[]{:S(2)}, u32[]{:S(2)}) collective-permute-start(bf16[512,128]{1,0:T(8,128)(2,1)S(1)} %get-tuple-element.38), channel_id=1, source_target_pairs={{0,1},{1,0},{2,3},{3,2},{4,5},{5,4},{6,7},{7,6},{8,9},{9,8},{10,11... | collective-permute-start | bytes 393224 | tf_op jit(solution)/shard_map/ppermute | solution.py:41
  4.5 4.7 %collective-permute-start = (bf16[192,128]{1,0:T(8,128)(2,1)S(1)}, bf16[192,128]{1,0:T(8,128)(2,1)S(1)}, u32[]{:S(2)}, u32[]{:S(2)}) collective-permute-start(bf16[192,128]{1,0:T(8,128)(2,1)S(1)} %get-tuple-element.35), channel_id=1, source_target_pairs={{0,24},{8,16},{16,8},{24,0},{1,25},{9,17},{17,9},{25,1},{2,26},{10... | collective-permute-start | bytes 147464 | tf_op jit(solution)/shard_map/ppermute | solution.py:41
  5.1 4.6 %collective-permute-start.1 = (bf16[192,128]{1,0:T(8,128)(2,1)S(1)}, bf16[192,128]{1,0:T(8,128)(2,1)S(1)}, u32[]{:S(2)}, u32[]{:S(2)}) collective-permute-start(bf16[192,128]{1,0:T(8,128)(2,1)S(1)} %get-tuple-element.36), channel_id=1, source_target_pairs={{0,16},{8,24},{16,0},{24,8},{1,17},{9,25},{17,1},{25,9},{2,18},{10... | collective-permute-start | bytes 147464 | tf_op jit(solution)/shard_map/ppermute | solution.py:41
  6.0 3.7 %collective-permute-start.2 = (bf16[192,128]{1,0:T(8,128)(2,1)S(1)}, bf16[192,128]{1,0:T(8,128)(2,1)S(1)}, u32[]{:S(2)}, u32[]{:S(2)}) collective-permute-start(bf16[192,128]{1,0:T(8,128)(2,1)S(1)} %get-tuple-element.37), channel_id=1, source_target_pairs={{0,8},{8,0},{16,24},{24,16},{1,9},{9,1},{17,25},{25,17},{2,10},{10... | collective-permute-start | bytes 147464 | tf_op jit(solution)/shard_map/ppermute | solution.py:41
  10.0 4.2 %collective-permute-start.4 = (f32[16,640]{1,0:T(8,128)S(1)}, f32[16,640]{1,0:T(8,128)S(1)}, u32[]{:S(2)}, u32[]{:S(2)}) collective-permute-start(f32[16,640]{1,0:T(8,128)S(1)} %get-tuple-element.47), channel_id=1, source_target_pairs={{0,24},{8,16},{16,8},{24,0},{1,25},{9,17},{17,9},{25,1},{2,26},{10... | collective-permute-start | bytes 122888 | tf_op jit(solution)/shard_map/ppermute | solution.py:41
  10.6 4.2 %collective-permute-start.5 = (f32[16,640]{1,0:T(8,128)S(1)}, f32[16,640]{1,0:T(8,128)S(1)}, u32[]{:S(2)}, u32[]{:S(2)}) collective-permute-start(f32[16,640]{1,0:T(8,128)S(1)} %get-tuple-element.48), channel_id=1, source_target_pairs={{0,16},{8,24},{16,0},{24,8},{1,17},{9,25},{17,1},{25,9},{2,18},{10... | collective-permute-start | bytes 122888 | tf_op jit(solution)/shard_map/ppermute | solution.py:41
  11.8 3.0 %collective-permute-start.6 = (f32[16,640]{1,0:T(8,128)S(1)}, f32[16,640]{1,0:T(8,128)S(1)}, u32[]{:S(2)}, u32[]{:S(2)}) collective-permute-start(f32[16,640]{1,0:T(8,128)S(1)} %get-tuple-element.49), channel_id=1, source_target_pairs={{0,8},{8,0},{16,24},{24,16},{1,9},{9,1},{17,25},{25,17},{2,10},{10... | collective-permute-start | bytes 122888 | tf_op jit(solution)/shard_map/ppermute | solution.py:41
  15.6 22.1 %collective-permute-start.7 = (bf16[3088,512]{1,0:T(8,128)(2,1)S(1)}, bf16[3088,512]{1,0:T(8,128)(2,1)S(1)}, u32[]{:S(2)}, u32[]{:S(2)}) collective-permute-start(bf16[3088,512]{1,0:T(8,128)(2,1)S(1)} %get-tuple-element.55.own), channel_id=1, source_target_pairs={{0,8},{8,0},{1,9},{9,1},{2,10},{10,2},{3,11},{11,3},{4,12},{12,4},... | collective-permute-start | bytes 9486344 | tf_op jit(solution)/shard_map/ppermute | solution.py:41

commit v6 on v5

--- a/solution.py
+++ b/solution.py
@@ -55,14 +55,13 @@
 
 def first_kernel(groups, leave_count, migration, states, hidden, w_qkvz, *refs):
     gain, w_ba, own_qk, messages = refs[0], refs[1], refs[2], refs[3 : groups + 2]
-    held, hidden_near, w_near, w_ba_near, normed, gain_near, plan, plan_sem, sems = refs[groups + 2 :]
+    held, hidden_near, w_ba_near, normed, gain_near, plan, plan_sem, sems = refs[groups + 2 :]
     plan_copy = pltpu.make_async_copy(migration, plan, plan_sem)
     plan_copy.start()
     pairs = [
         (hidden, hidden_near),
         (states.at[:, 0], held),
         (w_qkvz.at[:, pl.ds(0, DK)], own_qk),
-        (w_qkvz, w_near),
         (gain, gain_near),
         (w_ba, w_ba_near),
     ]
@@ -73,7 +72,7 @@
     tiles = depth // LANES
     copies[0].wait()
     wide = hidden_near[...].astype(F32)
-    copies[4].wait()
+    copies[3].wait()
     normed[...] = (wide * row_scale(wide) * gain_near[...]).astype(BF)
     for i in range(1, groups):
         for c in range(tiles):
@@ -87,7 +86,7 @@
             at = group * leave_count + j
             slot = jnp.where(plan[2, at] == (group ^ i), plan[1, at], slot)
         messages[i - 1][tiles * rows :, :] = held[slot].astype(BF)
-    for copy in copies[2:4] + copies[5:]:
+    for copy in copies[2:3] + copies[4:]:
         copy.wait()
 
 
@@ -384,26 +383,25 @@
         + [
             pltpu.VMEM((rows, DK, DV), F32),
             pltpu.VMEM(hidden.shape, BF),
-            pltpu.VMEM(w_qkvz.shape, BF),
             pltpu.VMEM(w_ba_t.shape, BF),
             pltpu.VMEM(hidden.shape, BF),
         ],
         in_specs=[HBM] * 6,
-        out_specs=[VMEM] * (groups + 5),
+        out_specs=[VMEM] * (groups + 4),
         scratch_shapes=[
             pltpu.VMEM((1, width), F32),
             pltpu.SMEM(plan.shape, jnp.int32),
             pltpu.SemaphoreType.DMA,
-            pltpu.SemaphoreType.DMA((6,)),
+            pltpu.SemaphoreType.DMA((5,)),
         ],
         compiler_params=PARAMS,
         cost_estimate=COST,
         name="first",
     )(*in_hbm(plan, states, hidden, w_qkvz, attn_gain.reshape(1, width), w_ba_t))
-    held, hidden_near, w_near, w_ba_near, normed = firsts[groups:]
+    held, hidden_near, w_ba_near, normed = firsts[groups:]
     other_qk = swap_with(firsts[0], "expert", 1)
     messages = [swap_with(firsts[i], dp, i) for i in range(1, groups)]
-    operands = [w_out, head_gain.reshape(1, DV), moe_gain.reshape(1, width)]
+    operands = [head_gain.reshape(1, DV), moe_gain.reshape(1, width)]
     span = 2 * MOE_FF
     staged = pl.pallas_call(
         functools.partial(stage_kernel, groups),
@@ -425,7 +423,7 @@
         *in_hbm(moe_gain.reshape(1, width), jnp.transpose(routes), jnp.transpose(w_router)),
         *in_hbm(w_gate_up, w_down, *operands),
     )
-    w_out_near, head_gain_near, moe_gain_near = staged[:-4]
+    head_gain_near, moe_gain_near = staged[:-4]
     own_hidden, own_gain, hits, expert = staged[-4:]
 
     partials = pl.pallas_call(
@@ -437,7 +435,7 @@
         compiler_params=PARAMS,
         cost_estimate=COST,
         name="project",
-    )(normed, w_ba_near, w_near, *messages[::-1], other_qk, own_gain)
+    )(normed, w_ba_near, w_qkvz, *messages[::-1], other_qk, own_gain)
     after = partials[0]
     partials = [partials[0]] + [swap_with(partials[i], dp, i) for i in range(1, groups)]
     split, mixing = pl.pallas_call(
@@ -464,7 +462,7 @@
         compiler_params=PARAMS,
         cost_estimate=COST,
         name="delta",
-    )(mixing, head_gain_near, w_out_near, split, expert, *partials[::-1])
+    )(mixing, head_gain_near, w_out, split, expert, *partials[::-1])
     other_expert = swap_with(expert, "core", 1)
     attention = lax.all_to_all(attention, "expert", split_axis=0, concat_axis=0, tiled=True)
 

time: 50.6 us -> 50.6 us (level)
  no operation moved by 1% of the time
where the time goes in v6:
time: 50.6 us; the launch traced here: 50.3 us
  blocking collectives  32.5 us (64%)
  Pallas kernels  8.15 us (16%)
  starting transfers between devices  6.9 us (14%)
  between operations  1.37 us (3%)
  waiting for transfers between devices  1.35 us (3%)
    all_to_all x1, blocking collectives, per_device(): lax.all_to_all(attention, 'expert', split_axis=0, concat_axis=0, tiled=True)  11.6 us
    all_to_all x1, blocking collectives, per_device(): lax.all_to_all(sent, ('x', 'expert'), split_axis=0, concat_axis=0, tiled=...  10.5 us
    all_to_all x1, blocking collectives, per_device(): lax.all_to_all(gained, ('x', 'expert'), split_axis=0, concat_axis=0, tile...  10.4 us
    ppermute x8, starting transfers between devices, swap_with(): return lax.ppermute(value, axis, pairs)  6.9 us
    pallas_call x1, Pallas kernels, per_device(): pl.pallas_call(functools.partial(stage_kernel, groups), out_shape=[pltpu....  2.66 us
    pallas_call x1, Pallas kernels, per_device(): pl.pallas_call(functools.partial(first_kernel, groups, leave_count), out_...  1.41 us
    ppermute x8, waiting for transfers between devices, swap_with(): return lax.ppermute(value, axis, pairs)  1.35 us
    pallas_call x1, Pallas kernels, per_device(): pl.pallas_call(functools.partial(expert_kernel, width), out_shape=pltpu.V...  1.24 us
  transfers between devices with their start and end apart: 8, of which 2 were waited for; matrix products, arithmetic and copies ran while one was open for 0% of the time, Pallas kernels for 7%

profile of v6, /device:TPU:0, one launch (start us, length us, event | category | flops | bytes accessed | tf_op | source)
XLA Modules:
  0.0 50.3 jit_solution(11230472044910977545)
XLA Ops:
  0.0 0.0 copy-start
  0.0 0.0 copy-start.1
  0.0 1.4 %first.1 = (bf16[512,128]{1,0:T(8,128)(2,1)S(1)}, bf16[192,128]{1,0:T(8,128)(2,1)S(1)}, bf16[192,128]{1,0:T(8,128)(2,1)S(1)}, bf16[192,128]{1,0:T(8,128)(2,1)S(1...) custom-call(s32[4,16]{1,0:T(4,128)} %bitcast.12, ...), custom_call_target="tpu_custom_call" | custom-call | bytes 8388608 | tf_op jit(solution)/shard_map/first/pallas_call | solution.py:379
  1.4 3.0 %collective-permute-start.3 = (bf16[512,128]{1,0:T(8,128)(2,1)S(1)}, bf16[512,128]{1,0:T(8,128)(2,1)S(1)}, u32[]{:S(2)}, u32[]{:S(2)}) collective-permute-start(bf16[512,128]{1,0:T(8,128)(2,1)S(1)} %get-tuple-element.35), channel_id=1, source_target_pairs={{0,1},{1,0},{2,3},{3,2},{4,5},{5,4},{6,7},{7,6},{8,9},{9,8},{10,11... | collective-permute-start | bytes 393224 | tf_op jit(solution)/shard_map/ppermute | solution.py:41
  4.5 0.7 %collective-permute-start = (bf16[192,128]{1,0:T(8,128)(2,1)S(1)}, bf16[192,128]{1,0:T(8,128)(2,1)S(1)}, u32[]{:S(2)}, u32[]{:S(2)}) collective-permute-start(bf16[192,128]{1,0:T(8,128)(2,1)S(1)} %get-tuple-element.32), channel_id=1, source_target_pairs={{0,24},{8,16},{16,8},{24,0},{1,25},{9,17},{17,9},{25,1},{2,26},{10... | collective-permute-start | bytes 147464 | tf_op jit(solution)/shard_map/ppermute | solution.py:41
  5.1 0.9 %collective-permute-start.1 = (bf16[192,128]{1,0:T(8,128)(2,1)S(1)}, bf16[192,128]{1,0:T(8,128)(2,1)S(1)}, u32[]{:S(2)}, u32[]{:S(2)}) collective-permute-start(bf16[192,128]{1,0:T(8,128)(2,1)S(1)} %get-tuple-element.33), channel_id=1, source_target_pairs={{0,16},{8,24},{16,0},{24,8},{1,17},{9,25},{17,1},{25,9},{2,18},{10... | collective-permute-start | bytes 147464 | tf_op jit(solution)/shard_map/ppermute | solution.py:41
  6.0 0.3 collective-permute-start.2
  6.3 2.7 %stage.1 = (f32[1,128]{1,0:T(1,128)S(1)}, f32[1,2048]{1,0:T(1,128)S(1)}, f32[16,256]{1,0:T(8,128)S(1)}, f32[1,256]{1,0:T(1,128)S(1)}, f32[32,128]{1,0:T(8,128)S(1)}, /*index=5*/bf16[3088,512]{1,0:T(8,128)(2,1)S(1)}) custom-call(bf16[16,2048]{1,0:T(8,128)(2,1)S(1)} %get-tuple-element.36.hidden, f32[1,2048]{1,0:T(1,128)} %bitcast.7, s32[10,64]{1,0:T(8,128)} %bitcast.10, ...), custom_call_target="tpu_custom_call" | custom-call | bytes 8388608 | tf_op jit(solution)/shard_map/stage/pallas_call | solution.py:406
  9.0 0.0 collective-permute-done.refs_0_.refs_2_
  9.0 0.7 %collective-permute-done.1.refs_1_ = bf16[192,128]{1,0:T(8,128)(2,1)S(1)} collective-permute-done((bf16[192,128]{1,0:T(8,128)(2,1)S(1)}, bf16[192,128]{1,0:T(8,128)(2,1)S(1)}, u32[]{:S(2)}, u32[]{:S(2)}) %collective-permute-start.1) | collective-permute-done | bytes 49184 | tf_op jit(solution)/shard_map/ppermute | solution.py:41
  9.7 0.0 collective-permute-done.2.refs_2_.refs_0_
  9.7 0.0 collective-permute-done.3.refs_3_
  9.7 0.0 copy-done
  9.7 0.2 project.1
  10.0 0.6 %collective-permute-start.4 = (f32[16,640]{1,0:T(8,128)S(1)}, f32[16,640]{1,0:T(8,128)S(1)}, u32[]{:S(2)}, u32[]{:S(2)}) collective-permute-start(f32[16,640]{1,0:T(8,128)S(1)} %get-tuple-element.43), channel_id=1, source_target_pairs={{0,24},{8,16},{16,8},{24,0},{1,25},{9,17},{17,9},{25,1},{2,26},{10... | collective-permute-start | bytes 122888 | tf_op jit(solution)/shard_map/ppermute | solution.py:41
  10.6 1.2 %collective-permute-start.5 = (f32[16,640]{1,0:T(8,128)S(1)}, f32[16,640]{1,0:T(8,128)S(1)}, u32[]{:S(2)}, u32[]{:S(2)}) collective-permute-start(f32[16,640]{1,0:T(8,128)S(1)} %get-tuple-element.44), channel_id=1, source_target_pairs={{0,16},{8,24},{16,0},{24,8},{1,17},{9,25},{17,1},{25,9},{2,18},{10... | collective-permute-start | bytes 122888 | tf_op jit(solution)/shard_map/ppermute | solution.py:41
  11.7 0.1 collective-permute-start.6
  13.2 0.9 %settle.1 = (bf16[2048,256]{1,0:T(8,128)(2,1)S(1)}, f32[2,128]{1,0:T(2,128)S(1)}) custom-call(s32[4,16]{1,0:T(4,128)} %bitcast.13, f32[1]{0:T(128)S(6)} %copy.18.a_log, f32[1]{0:T(128)S(6)} %copy.19.dt_bias, f32[16,128,128]{2,1,0:T(8,128)S(1)} %get-tuple-element.29.states, f32[16,640]{1,0:T(8,128)S(1)} %get-tuple-element.38.after.refs_3_, ...), custom_call_target="tpu_custom_call" | custom-call | bytes 8388608 | tf_op jit(solution)/shard_map/settle/pallas_call | solution.py:441
  14.1 0.0 collective-permute-done.4.refs_0_
  14.1 0.6 %collective-permute-done.5.refs_1_ = f32[16,640]{1,0:T(8,128)S(1)} collective-permute-done((f32[16,640]{1,0:T(8,128)S(1)}, f32[16,640]{1,0:T(8,128)S(1)}, u32[]{:S(2)}, u32[]{:S(2)}) %collective-permute-start.5) | collective-permute-done | bytes 40992 | tf_op jit(solution)/shard_map/ppermute | solution.py:41
  14.8 0.0 collective-permute-done.6.refs_2_
  14.8 0.0 copy-done.1
  14.8 0.8 %delta.1 = (bf16[8,16,256]{2,1,0:T(8,128)(2,1)S(1)}, bf16[3088,512]{1,0:T(8,128)(2,1)S(1)}) custom-call(f32[2,128]{1,0:T(2,128)S(1)} %get-tuple-element.39.mixing, f32[1,128]{1,0:T(1,128)S(1)} %get-tuple-element.40.head_gain, bf16[128,2048]{1,0:T(8,128)(2,1)S(1)} %copy-done.1, ...), custom_call_target="tpu_custom_call", output_to_operand_aliasing={{1}: (4, {})} | custom-call | bytes 8388608 | tf_op jit(solution)/shard_map/delta/pallas_call | solution.py:452
  15.6 0.1 collective-permute-start.7
  15.7 11.6 %all_to_all.15.attention = bf16[8,16,256]{2,1,0:T(8,128)(2,1)S(1)} all-to-all(bf16[8,16,256]{2,1,0:T(8,128)(2,1)S(1)} %get-tuple-element.46), channel_id=1, replica_groups=mesh['parts'=1,'x'=2,'core'=2,'expert'=8] {'expert'}, dimensions={0} | all-to-all | bytes 131072 | tf_op jit(solution)/shard_map/all_to_all | solution.py:467
  27.3 10.4 %all_to_all.16.every = bf16[16,16,256]{2,1,0:T(8,128)(2,1)S(1)} all-to-all(bf16[16,16,256]{2,1,0:T(8,128)(2,1)S(1)} %get-tuple-element.48), channel_id=1, replica_groups=mesh['parts'=1,'x'=2,'core'=2,'expert'=8] {'x','expert'}, dimensions={0} | all-to-all | bytes 262144 | tf_op jit(solution)/shard_map/all_to_all | solution.py:481
  37.7 0.0 collective-permute-done.7.other
  37.7 1.2 %experts.1 = bf16[16,40,128]{2,1,0:T(8,128)(2,1)S(1)} custom-call(bf16[16,16,256]{2,1,0:T(8,128)(2,1)S(1)} %all_to_all.16.every, f32[32,128]{1,0:T(8,128)S(1)} %get-tuple-element.49.hits, f32[1,2048]{1,0:T(1,128)S(1)} %get-tuple-element.50.gain, bf16[3088,512]{1,0:T(8,128)(2,1)S(1)} %get-tuple-element.51.own, bf16[3088,512]{1,0:T(8,128)(2,1)S(1)} %collective-permute-done.7.other), custom_call_target="tpu_custom_call" | custom-call | bytes 8388608 | tf_op jit(solution)/shard_map/experts/pallas_call | solution.py:484
  38.9 10.5 %all_to_all.17.back = bf16[16,40,128]{2,1,0:T(8,128)(2,1)S(1)} all-to-all(bf16[16,40,128]{2,1,0:T(8,128)(2,1)S(1)} %experts.1), channel_id=1, replica_groups=mesh['parts'=1,'x'=2,'core'=2,'expert'=8] {'x','expert'}, dimensions={0} | all-to-all | bytes 327680 | tf_op jit(solution)/shard_map/all_to_all | solution.py:493
  49.4 0.8 %finish.1 = bf16[16,256]{1,0:T(8,128)(2,1)} custom-call(bf16[16,40,128]{2,1,0:T(8,128)(2,1)S(1)} %all_to_all.17.back, f32[16,256]{1,0:T(8,128)S(1)} %get-tuple-element.52.residual), custom_call_target="tpu_custom_call" | custom-call | bytes 8388608 | tf_op jit(solution)/shard_map/finish/pallas_call | solution.py:494
  (1 shorter events, 0.0 us)
Async XLA Ops:
  0.0 9.7 %copy-start = (bf16[512,384]{1,0:T(8,128)(2,1)S(1)}, bf16[512,384]{1,0:T(8,128)(2,1)}, u32[]{:S(2)}) copy-start(bf16[512,384]{1,0:T(8,128)(2,1)} %w_qkvz.3) | copy-start | bytes 1179652
  0.0 14.8 %copy-start.1 = (bf16[128,2048]{1,0:T(8,128)(2,1)S(1)}, bf16[128,2048]{1,0:T(8,128)(2,1)}, u32[]{:S(2)}) copy-start(bf16[128,2048]{1,0:T(8,128)(2,1)} %w_out.1) | copy-start | bytes 1572868
  1.4 8.3 %collective-permute-start.3 = (bf16[512,128]{1,0:T(8,128)(2,1)S(1)}, bf16[512,128]{1,0:T(8,128)(2,1)S(1)}, u32[]{:S(2)}, u32[]{:S(2)}) collective-permute-start(bf16[512,128]{1,0:T(8,128)(2,1)S(1)} %get-tuple-element.35), channel_id=1, source_target_pairs={{0,1},{1,0},{2,3},{3,2},{4,5},{5,4},{6,7},{7,6},{8,9},{9,8},{10,11... | collective-permute-start | bytes 393224 | tf_op jit(solution)/shard_map/ppermute | solution.py:41
  4.5 4.5 %collective-permute-start = (bf16[192,128]{1,0:T(8,128)(2,1)S(1)}, bf16[192,128]{1,0:T(8,128)(2,1)S(1)}, u32[]{:S(2)}, u32[]{:S(2)}) collective-permute-start(bf16[192,128]{1,0:T(8,128)(2,1)S(1)} %get-tuple-element.32), channel_id=1, source_target_pairs={{0,24},{8,16},{16,8},{24,0},{1,25},{9,17},{17,9},{25,1},{2,26},{10... | collective-permute-start | bytes 147464 | tf_op jit(solution)/shard_map/ppermute | solution.py:41
  5.1 4.6 %collective-permute-start.1 = (bf16[192,128]{1,0:T(8,128)(2,1)S(1)}, bf16[192,128]{1,0:T(8,128)(2,1)S(1)}, u32[]{:S(2)}, u32[]{:S(2)}) collective-permute-start(bf16[192,128]{1,0:T(8,128)(2,1)S(1)} %get-tuple-element.33), channel_id=1, source_target_pairs={{0,16},{8,24},{16,0},{24,8},{1,17},{9,25},{17,1},{25,9},{2,18},{10... | collective-permute-start | bytes 147464 | tf_op jit(solution)/shard_map/ppermute | solution.py:41
  6.0 3.7 %collective-permute-start.2 = (bf16[192,128]{1,0:T(8,128)(2,1)S(1)}, bf16[192,128]{1,0:T(8,128)(2,1)S(1)}, u32[]{:S(2)}, u32[]{:S(2)}) collective-permute-start(bf16[192,128]{1,0:T(8,128)(2,1)S(1)} %get-tuple-element.34), channel_id=1, source_target_pairs={{0,8},{8,0},{16,24},{24,16},{1,9},{9,1},{17,25},{25,17},{2,10},{10... | collective-permute-start | bytes 147464 | tf_op jit(solution)/shard_map/ppermute | solution.py:41
  10.0 4.2 %collective-permute-start.4 = (f32[16,640]{1,0:T(8,128)S(1)}, f32[16,640]{1,0:T(8,128)S(1)}, u32[]{:S(2)}, u32[]{:S(2)}) collective-permute-start(f32[16,640]{1,0:T(8,128)S(1)} %get-tuple-element.43), channel_id=1, source_target_pairs={{0,24},{8,16},{16,8},{24,0},{1,25},{9,17},{17,9},{25,1},{2,26},{10... | collective-permute-start | bytes 122888 | tf_op jit(solution)/shard_map/ppermute | solution.py:41
  10.6 4.2 %collective-permute-start.5 = (f32[16,640]{1,0:T(8,128)S(1)}, f32[16,640]{1,0:T(8,128)S(1)}, u32[]{:S(2)}, u32[]{:S(2)}) collective-permute-start(f32[16,640]{1,0:T(8,128)S(1)} %get-tuple-element.44), channel_id=1, source_target_pairs={{0,16},{8,24},{16,0},{24,8},{1,17},{9,25},{17,1},{25,9},{2,18},{10... | collective-permute-start | bytes 122888 | tf_op jit(solution)/shard_map/ppermute | solution.py:41
  11.7 3.0 %collective-permute-start.6 = (f32[16,640]{1,0:T(8,128)S(1)}, f32[16,640]{1,0:T(8,128)S(1)}, u32[]{:S(2)}, u32[]{:S(2)}) collective-permute-start(f32[16,640]{1,0:T(8,128)S(1)} %get-tuple-element.45), channel_id=1, source_target_pairs={{0,8},{8,0},{16,24},{24,16},{1,9},{9,1},{17,25},{25,17},{2,10},{10... | collective-permute-start | bytes 122888 | tf_op jit(solution)/shard_map/ppermute | solution.py:41
  15.6 22.1 %collective-permute-start.7 = (bf16[3088,512]{1,0:T(8,128)(2,1)S(1)}, bf16[3088,512]{1,0:T(8,128)(2,1)S(1)}, u32[]{:S(2)}, u32[]{:S(2)}) collective-permute-start(bf16[3088,512]{1,0:T(8,128)(2,1)S(1)} %get-tuple-element.51.own), channel_id=1, source_target_pairs={{0,8},{8,0},{1,9},{9,1},{2,10},{10,2},{3,11},{11,3},{4,12},{12,4},... | collective-permute-start | bytes 9486344 | tf_op jit(solution)/shard_map/ppermute | solution.py:41

commit v7 on v6

--- a/solution.py
+++ b/solution.py
@@ -55,7 +55,7 @@
 
 def first_kernel(groups, leave_count, migration, states, hidden, w_qkvz, *refs):
     gain, w_ba, own_qk, messages = refs[0], refs[1], refs[2], refs[3 : groups + 2]
-    held, hidden_near, w_ba_near, normed, gain_near, plan, plan_sem, sems = refs[groups + 2 :]
+    held, hidden_near, w_ba_near, normed, plan, gain_near, plan_sem, sems = refs[groups + 2 :]
     plan_copy = pltpu.make_async_copy(migration, plan, plan_sem)
     plan_copy.start()
     pairs = [
@@ -112,9 +112,10 @@
         mixes = jnp.where(lane == j, total, mixes)
     for i in range(groups):
         block = slice(i * rows, (i + 1) * rows)
-        outs[i][:, : DK + 2 * DV] = main[block]
-        outs[i][:, DK + 2 * DV : 2 * DK + 2 * DV] = other[block]
-        outs[i][:, 2 * DK + 2 * DV :] = mixes[block]
+        kind = outs[i].dtype
+        outs[i][:, : DK + 2 * DV] = main[block].astype(kind)
+        outs[i][:, DK + 2 * DV : 2 * DK + 2 * DV] = other[block].astype(kind)
+        outs[i][:, 2 * DK + 2 * DV :] = mixes[block].astype(kind)
 
 
 def stage_kernel(groups, hidden, gain, routes, router, w_gate_up, w_down, *refs):
@@ -174,17 +175,14 @@
     out[where, DV:] = (state - high.astype(F32)).astype(BF)
 
 
-def settle_kernel(groups, leave_count, migration, a_log, dt_bias, states, after, *refs):
-    messages, (split, mixing, plan, plan_sem) = refs[:-4], refs[-4:]
+def settle_kernel(groups, leave_count, plan, a_log, dt_bias, states, after, *refs):
+    messages, (split, mixing) = refs[:-2], refs[-2:]
     del after
-    plan_copy = pltpu.make_async_copy(migration, plan, plan_sem)
-    plan_copy.start()
     mixing[0:1, :] = jnp.exp(jnp.full((1, LANES), a_log[0], F32))
     mixing[1:2, :] = jnp.full((1, LANES), dt_bias[0], F32)
     group = group_index()
     for r in range(states.shape[0]):
         store_split(split, r, states[r])
-    plan_copy.wait()
     for i in range(groups):
         for j in range(leave_count):
             at = (group ^ i) * leave_count + j
@@ -204,9 +202,9 @@
     del expert, passed
     member = lax.axis_index("expert")
     rows = split.shape[0] // DK
-    summed = partials[0][...]
+    summed = partials[0][...].astype(F32)
     for partial in partials[1:]:
-        summed = summed + partial[...]
+        summed = summed + partial[...].astype(F32)
     projected = summed.astype(BF).astype(F32)
     own_qk = projected[:, :DK]
     values = projected[:, DK : DK + DV]
@@ -385,12 +383,12 @@
             pltpu.VMEM(hidden.shape, BF),
             pltpu.VMEM(w_ba_t.shape, BF),
             pltpu.VMEM(hidden.shape, BF),
+            pltpu.SMEM(plan.shape, jnp.int32),
         ],
         in_specs=[HBM] * 6,
-        out_specs=[VMEM] * (groups + 4),
+        out_specs=[VMEM] * (groups + 4) + [SMEM],
         scratch_shapes=[
             pltpu.VMEM((1, width), F32),
-            pltpu.SMEM(plan.shape, jnp.int32),
             pltpu.SemaphoreType.DMA,
             pltpu.SemaphoreType.DMA((5,)),
         ],
@@ -398,7 +396,7 @@
         cost_estimate=COST,
         name="first",
     )(*in_hbm(plan, states, hidden, w_qkvz, attn_gain.reshape(1, width), w_ba_t))
-    held, hidden_near, w_ba_near, normed = firsts[groups:]
+    held, hidden_near, w_ba_near, normed, plan_near = firsts[groups:]
     other_qk = swap_with(firsts[0], "expert", 1)
     messages = [swap_with(firsts[i], dp, i) for i in range(1, groups)]
     operands = [head_gain.reshape(1, DV), moe_gain.reshape(1, width)]
@@ -428,7 +426,7 @@
 
     partials = pl.pallas_call(
         functools.partial(project_kernel, groups),
-        out_shape=[pltpu.VMEM((rows, SENT), F32)] * groups,
+        out_shape=[pltpu.VMEM((rows, SENT), F32)] + [pltpu.VMEM((rows, SENT), BF)] * (groups - 1),
         in_specs=[VMEM] * (3 + groups) + [ANY],
         out_specs=[VMEM] * groups,
         scratch_shapes=[pltpu.VMEM((total_rows, depth), BF)],
@@ -441,13 +439,12 @@
     split, mixing = pl.pallas_call(
         functools.partial(settle_kernel, groups, leave_count),
         out_shape=[pltpu.VMEM((rows * DK, 2 * DV), BF), pltpu.VMEM((2, LANES), F32)],
-        in_specs=[HBM] + [SMEM] * 2 + [VMEM, ANY] + [VMEM] * (groups - 1),
+        in_specs=[SMEM] * 3 + [VMEM, ANY] + [VMEM] * (groups - 1),
         out_specs=[VMEM] * 2,
-        scratch_shapes=[pltpu.SMEM(plan.shape, jnp.int32), pltpu.SemaphoreType.DMA],
         compiler_params=PARAMS,
         cost_estimate=COST,
         name="settle",
-    )(*in_hbm(plan), a_log, dt_bias, held, after, *messages)
+    )(plan_near, a_log, dt_bias, held, after, *messages)
 
     attention, expert = pl.pallas_call(
         delta_kernel,

time: 50.6 us -> 50.3 us (level)
  Pallas kernels: 8.15 us -> 7.61 us
    pallas_call x1, Pallas kernels: 0.93 us -> 0.39 us  [per_device(): pl.pallas_call(functools.partial(settle_kernel, groups, leave_count), out...]
  transfers between devices with their start and end apart: 8 -> 8, of which waited for: 2 -> 2; matrix products, arithmetic and copies ran while one was open for 0% -> 0% of each run, Pallas kernels for 7% -> 6%
where the time goes in v7:
time: 50.3 us; the launch traced here: 50 us
  blocking collectives  32.6 us (65%)
  Pallas kernels  7.61 us (15%)
  starting transfers between devices  6.9 us (14%)
  waiting for transfers between devices  1.48 us (3%)
  between operations  1.37 us (3%)
    all_to_all x1, blocking collectives, per_device(): lax.all_to_all(attention, 'expert', split_axis=0, concat_axis=0, tiled=True)  11.7 us
    all_to_all x1, blocking collectives, per_device(): lax.all_to_all(sent, ('x', 'expert'), split_axis=0, concat_axis=0, tiled=...  10.5 us
    all_to_all x1, blocking collectives, per_device(): lax.all_to_all(gained, ('x', 'expert'), split_axis=0, concat_axis=0, tile...  10.4 us
    ppermute x8, starting transfers between devices, swap_with(): return lax.ppermute(value, axis, pairs)  6.9 us
    pallas_call x1, Pallas kernels, per_device(): pl.pallas_call(functools.partial(stage_kernel, groups), out_shape=[pltpu....  2.66 us
    ppermute x8, waiting for transfers between devices, swap_with(): return lax.ppermute(value, axis, pairs)  1.48 us
    pallas_call x1, Pallas kernels, per_device(): pl.pallas_call(functools.partial(first_kernel, groups, leave_count), out_...  1.41 us
    pallas_call x1, Pallas kernels, per_device(): pl.pallas_call(functools.partial(expert_kernel, width), out_shape=pltpu.V...  1.24 us
  transfers between devices with their start and end apart: 8, of which 2 were waited for; matrix products, arithmetic and copies ran while one was open for 0% of the time, Pallas kernels for 6%

profile of v7, /device:TPU:0, one launch (start us, length us, event | category | flops | bytes accessed | tf_op | source)
XLA Modules:
  0.0 50.0 jit_solution(196535990742076366)
XLA Ops:
  0.0 0.0 copy-start
  0.0 0.0 copy-start.1
  0.0 1.4 %first.1 = (bf16[512,128]{1,0:T(8,128)(2,1)S(1)}, bf16[192,128]{1,0:T(8,128)(2,1)S(1)}, bf16[192,128]{1,0:T(8,128)(2,1)S(1)}, bf16[192,128]{1,0:T(8,128)(2,1)S(1...) custom-call(s32[4,16]{1,0:T(4,128)} %bitcast.12, ...), custom_call_target="tpu_custom_call" | custom-call | bytes 8388608 | tf_op jit(solution)/shard_map/first/pallas_call | solution.py:377
  1.4 3.0 %collective-permute-start.3 = (bf16[512,128]{1,0:T(8,128)(2,1)S(1)}, bf16[512,128]{1,0:T(8,128)(2,1)S(1)}, u32[]{:S(2)}, u32[]{:S(2)}) collective-permute-start(bf16[512,128]{1,0:T(8,128)(2,1)S(1)} %get-tuple-element.37), channel_id=1, source_target_pairs={{0,1},{1,0},{2,3},{3,2},{4,5},{5,4},{6,7},{7,6},{8,9},{9,8},{10,11... | collective-permute-start | bytes 393224 | tf_op jit(solution)/shard_map/ppermute | solution.py:41
  4.5 0.7 %collective-permute-start = (bf16[192,128]{1,0:T(8,128)(2,1)S(1)}, bf16[192,128]{1,0:T(8,128)(2,1)S(1)}, u32[]{:S(2)}, u32[]{:S(2)}) collective-permute-start(bf16[192,128]{1,0:T(8,128)(2,1)S(1)} %get-tuple-element.34), channel_id=1, source_target_pairs={{0,24},{8,16},{16,8},{24,0},{1,25},{9,17},{17,9},{25,1},{2,26},{10... | collective-permute-start | bytes 147464 | tf_op jit(solution)/shard_map/ppermute | solution.py:41
  5.1 0.9 %collective-permute-start.1 = (bf16[192,128]{1,0:T(8,128)(2,1)S(1)}, bf16[192,128]{1,0:T(8,128)(2,1)S(1)}, u32[]{:S(2)}, u32[]{:S(2)}) collective-permute-start(bf16[192,128]{1,0:T(8,128)(2,1)S(1)} %get-tuple-element.35), channel_id=1, source_target_pairs={{0,16},{8,24},{16,0},{24,8},{1,17},{9,25},{17,1},{25,9},{2,18},{10... | collective-permute-start | bytes 147464 | tf_op jit(solution)/shard_map/ppermute | solution.py:41
  6.0 0.3 collective-permute-start.2
  6.3 2.7 %stage.1 = (f32[1,128]{1,0:T(1,128)S(1)}, f32[1,2048]{1,0:T(1,128)S(1)}, f32[16,256]{1,0:T(8,128)S(1)}, f32[1,256]{1,0:T(1,128)S(1)}, f32[32,128]{1,0:T(8,128)S(1)}, /*index=5*/bf16[3088,512]{1,0:T(8,128)(2,1)S(1)}) custom-call(bf16[16,2048]{1,0:T(8,128)(2,1)S(1)} %get-tuple-element.38.hidden, f32[1,2048]{1,0:T(1,128)} %bitcast.7, s32[10,64]{1,0:T(8,128)} %bitcast.10, ...), custom_call_target="tpu_custom_call" | custom-call | bytes 8388608 | tf_op jit(solution)/shard_map/stage/pallas_call | solution.py:404
  9.0 0.0 collective-permute-done.refs_0_.refs_2_
  9.0 0.7 %collective-permute-done.1.refs_1_ = bf16[192,128]{1,0:T(8,128)(2,1)S(1)} collective-permute-done((bf16[192,128]{1,0:T(8,128)(2,1)S(1)}, bf16[192,128]{1,0:T(8,128)(2,1)S(1)}, u32[]{:S(2)}, u32[]{:S(2)}) %collective-permute-start.1) | collective-permute-done | bytes 49184 | tf_op jit(solution)/shard_map/ppermute | solution.py:41
  9.7 0.0 collective-permute-done.2.refs_2_.refs_0_
  9.7 0.0 collective-permute-done.3.refs_3_
  9.7 0.0 copy-done
  9.7 0.2 project.1
  10.0 0.6 %collective-permute-start.4 = (bf16[16,640]{1,0:T(8,128)(2,1)S(1)}, bf16[16,640]{1,0:T(8,128)(2,1)S(1)}, u32[]{:S(2)}, u32[]{:S(2)}) collective-permute-start(bf16[16,640]{1,0:T(8,128)(2,1)S(1)} %get-tuple-element.45), channel_id=1, source_target_pairs={{0,24},{8,16},{16,8},{24,0},{1,25},{9,17},{17,9},{25,1},{2,26},{10... | collective-permute-start | bytes 61448 | tf_op jit(solution)/shard_map/ppermute | solution.py:41
  10.6 1.2 %collective-permute-start.5 = (bf16[16,640]{1,0:T(8,128)(2,1)S(1)}, bf16[16,640]{1,0:T(8,128)(2,1)S(1)}, u32[]{:S(2)}, u32[]{:S(2)}) collective-permute-start(bf16[16,640]{1,0:T(8,128)(2,1)S(1)} %get-tuple-element.46), channel_id=1, source_target_pairs={{0,16},{8,24},{16,0},{24,8},{1,17},{9,25},{17,1},{25,9},{2,18},{10... | collective-permute-start | bytes 61448 | tf_op jit(solution)/shard_map/ppermute | solution.py:41
  11.7 0.1 collective-permute-start.6
  13.2 0.4 settle.1
  13.6 0.0 collective-permute-done.4.refs_0_
  13.6 0.7 %collective-permute-done.5.refs_1_ = bf16[16,640]{1,0:T(8,128)(2,1)S(1)} collective-permute-done((bf16[16,640]{1,0:T(8,128)(2,1)S(1)}, bf16[16,640]{1,0:T(8,128)(2,1)S(1)}, u32[]{:S(2)}, u32[]{:S(2)}) %collective-permute-start.5) | collective-permute-done | bytes 20512 | tf_op jit(solution)/shard_map/ppermute | solution.py:41
  14.4 0.0 collective-permute-done.6.refs_2_
  14.4 0.0 copy-done.1
  14.4 0.8 %delta.1 = (bf16[8,16,256]{2,1,0:T(8,128)(2,1)S(1)}, bf16[3088,512]{1,0:T(8,128)(2,1)S(1)}) custom-call(f32[2,128]{1,0:T(2,128)S(1)} %get-tuple-element.41.mixing, f32[1,128]{1,0:T(1,128)S(1)} %get-tuple-element.42.head_gain, bf16[128,2048]{1,0:T(8,128)(2,1)S(1)} %copy-done.1, ...), custom_call_target="tpu_custom_call", output_to_operand_aliasing={{1}: (4, {})} | custom-call | bytes 8388608 | tf_op jit(solution)/shard_map/delta/pallas_call | solution.py:449
  15.2 0.1 collective-permute-start.7
  15.3 11.7 %all_to_all.15.attention = bf16[8,16,256]{2,1,0:T(8,128)(2,1)S(1)} all-to-all(bf16[8,16,256]{2,1,0:T(8,128)(2,1)S(1)} %get-tuple-element.48), channel_id=1, replica_groups=mesh['parts'=1,'x'=2,'core'=2,'expert'=8] {'expert'}, dimensions={0} | all-to-all | bytes 131072 | tf_op jit(solution)/shard_map/all_to_all | solution.py:464
  27.0 10.4 %all_to_all.16.every = bf16[16,16,256]{2,1,0:T(8,128)(2,1)S(1)} all-to-all(bf16[16,16,256]{2,1,0:T(8,128)(2,1)S(1)} %get-tuple-element.50), channel_id=1, replica_groups=mesh['parts'=1,'x'=2,'core'=2,'expert'=8] {'x','expert'}, dimensions={0} | all-to-all | bytes 262144 | tf_op jit(solution)/shard_map/all_to_all | solution.py:478
  37.4 0.0 collective-permute-done.7.other
  37.4 1.2 %experts.1 = bf16[16,40,128]{2,1,0:T(8,128)(2,1)S(1)} custom-call(bf16[16,16,256]{2,1,0:T(8,128)(2,1)S(1)} %all_to_all.16.every, f32[32,128]{1,0:T(8,128)S(1)} %get-tuple-element.51.hits, f32[1,2048]{1,0:T(1,128)S(1)} %get-tuple-element.52.gain, bf16[3088,512]{1,0:T(8,128)(2,1)S(1)} %get-tuple-element.53.own, bf16[3088,512]{1,0:T(8,128)(2,1)S(1)} %collective-permute-done.7.other), custom_call_target="tpu_custom_call" | custom-call | bytes 8388608 | tf_op jit(solution)/shard_map/experts/pallas_call | solution.py:481
  38.6 10.5 %all_to_all.17.back = bf16[16,40,128]{2,1,0:T(8,128)(2,1)S(1)} all-to-all(bf16[16,40,128]{2,1,0:T(8,128)(2,1)S(1)} %experts.1), channel_id=1, replica_groups=mesh['parts'=1,'x'=2,'core'=2,'expert'=8] {'x','expert'}, dimensions={0} | all-to-all | bytes 327680 | tf_op jit(solution)/shard_map/all_to_all | solution.py:490
  49.1 0.8 %finish.1 = bf16[16,256]{1,0:T(8,128)(2,1)} custom-call(bf16[16,40,128]{2,1,0:T(8,128)(2,1)S(1)} %all_to_all.17.back, f32[16,256]{1,0:T(8,128)S(1)} %get-tuple-element.54.residual), custom_call_target="tpu_custom_call" | custom-call | bytes 8388608 | tf_op jit(solution)/shard_map/finish/pallas_call | solution.py:491
  (1 shorter events, 0.0 us)
Async XLA Ops:
  0.0 9.7 %copy-start = (bf16[512,384]{1,0:T(8,128)(2,1)S(1)}, bf16[512,384]{1,0:T(8,128)(2,1)}, u32[]{:S(2)}) copy-start(bf16[512,384]{1,0:T(8,128)(2,1)} %w_qkvz.3) | copy-start | bytes 1179652
  0.0 14.4 %copy-start.1 = (bf16[128,2048]{1,0:T(8,128)(2,1)S(1)}, bf16[128,2048]{1,0:T(8,128)(2,1)}, u32[]{:S(2)}) copy-start(bf16[128,2048]{1,0:T(8,128)(2,1)} %w_out.1) | copy-start | bytes 1572868
  1.4 8.3 %collective-permute-start.3 = (bf16[512,128]{1,0:T(8,128)(2,1)S(1)}, bf16[512,128]{1,0:T(8,128)(2,1)S(1)}, u32[]{:S(2)}, u32[]{:S(2)}) collective-permute-start(bf16[512,128]{1,0:T(8,128)(2,1)S(1)} %get-tuple-element.37), channel_id=1, source_target_pairs={{0,1},{1,0},{2,3},{3,2},{4,5},{5,4},{6,7},{7,6},{8,9},{9,8},{10,11... | collective-permute-start | bytes 393224 | tf_op jit(solution)/shard_map/ppermute | solution.py:41
  4.5 4.5 %collective-permute-start = (bf16[192,128]{1,0:T(8,128)(2,1)S(1)}, bf16[192,128]{1,0:T(8,128)(2,1)S(1)}, u32[]{:S(2)}, u32[]{:S(2)}) collective-permute-start(bf16[192,128]{1,0:T(8,128)(2,1)S(1)} %get-tuple-element.34), channel_id=1, source_target_pairs={{0,24},{8,16},{16,8},{24,0},{1,25},{9,17},{17,9},{25,1},{2,26},{10... | collective-permute-start | bytes 147464 | tf_op jit(solution)/shard_map/ppermute | solution.py:41
  5.1 4.6 %collective-permute-start.1 = (bf16[192,128]{1,0:T(8,128)(2,1)S(1)}, bf16[192,128]{1,0:T(8,128)(2,1)S(1)}, u32[]{:S(2)}, u32[]{:S(2)}) collective-permute-start(bf16[192,128]{1,0:T(8,128)(2,1)S(1)} %get-tuple-element.35), channel_id=1, source_target_pairs={{0,16},{8,24},{16,0},{24,8},{1,17},{9,25},{17,1},{25,9},{2,18},{10... | collective-permute-start | bytes 147464 | tf_op jit(solution)/shard_map/ppermute | solution.py:41
  6.0 3.7 %collective-permute-start.2 = (bf16[192,128]{1,0:T(8,128)(2,1)S(1)}, bf16[192,128]{1,0:T(8,128)(2,1)S(1)}, u32[]{:S(2)}, u32[]{:S(2)}) collective-permute-start(bf16[192,128]{1,0:T(8,128)(2,1)S(1)} %get-tuple-element.36), channel_id=1, source_target_pairs={{0,8},{8,0},{16,24},{24,16},{1,9},{9,1},{17,25},{25,17},{2,10},{10... | collective-permute-start | bytes 147464 | tf_op jit(solution)/shard_map/ppermute | solution.py:41
  10.0 3.6 %collective-permute-start.4 = (bf16[16,640]{1,0:T(8,128)(2,1)S(1)}, bf16[16,640]{1,0:T(8,128)(2,1)S(1)}, u32[]{:S(2)}, u32[]{:S(2)}) collective-permute-start(bf16[16,640]{1,0:T(8,128)(2,1)S(1)} %get-tuple-element.45), channel_id=1, source_target_pairs={{0,24},{8,16},{16,8},{24,0},{1,25},{9,17},{17,9},{25,1},{2,26},{10... | collective-permute-start | bytes 61448 | tf_op jit(solution)/shard_map/ppermute | solution.py:41
  10.6 3.8 %collective-permute-start.5 = (bf16[16,640]{1,0:T(8,128)(2,1)S(1)}, bf16[16,640]{1,0:T(8,128)(2,1)S(1)}, u32[]{:S(2)}, u32[]{:S(2)}) collective-permute-start(bf16[16,640]{1,0:T(8,128)(2,1)S(1)} %get-tuple-element.46), channel_id=1, source_target_pairs={{0,16},{8,24},{16,0},{24,8},{1,17},{9,25},{17,1},{25,9},{2,18},{10... | collective-permute-start | bytes 61448 | tf_op jit(solution)/shard_map/ppermute | solution.py:41
  11.7 2.6 %collective-permute-start.6 = (bf16[16,640]{1,0:T(8,128)(2,1)S(1)}, bf16[16,640]{1,0:T(8,128)(2,1)S(1)}, u32[]{:S(2)}, u32[]{:S(2)}) collective-permute-start(bf16[16,640]{1,0:T(8,128)(2,1)S(1)} %get-tuple-element.47), channel_id=1, source_target_pairs={{0,8},{8,0},{16,24},{24,16},{1,9},{9,1},{17,25},{25,17},{2,10},{10... | collective-permute-start | bytes 61448 | tf_op jit(solution)/shard_map/ppermute | solution.py:41
  15.2 22.2 %collective-permute-start.7 = (bf16[3088,512]{1,0:T(8,128)(2,1)S(1)}, bf16[3088,512]{1,0:T(8,128)(2,1)S(1)}, u32[]{:S(2)}, u32[]{:S(2)}) collective-permute-start(bf16[3088,512]{1,0:T(8,128)(2,1)S(1)} %get-tuple-element.53.own), channel_id=1, source_target_pairs={{0,8},{8,0},{1,9},{9,1},{2,10},{10,2},{3,11},{11,3},{4,12},{12,4},... | collective-permute-start | bytes 9486344 | tf_op jit(solution)/shard_map/ppermute | solution.py:41

commit v8 on v7

--- a/solution.py
+++ b/solution.py
@@ -459,7 +459,7 @@
         compiler_params=PARAMS,
         cost_estimate=COST,
         name="delta",
-    )(mixing, head_gain_near, w_out, split, expert, *partials[::-1])
+    )(mixing, head_gain_near, w_out, split, expert, *partials)
     other_expert = swap_with(expert, "core", 1)
     attention = lax.all_to_all(attention, "expert", split_axis=0, concat_axis=0, tiled=True)
 

time: 50.3 us -> 50.3 us (level)
  transfers between devices with their start and end apart: 8 -> 8, of which waited for: 2 -> 3; matrix products, arithmetic and copies ran while one was open for 0% -> 0% of each run, Pallas kernels for 6% -> 6%
where the time goes in v8:
time: 50.3 us; the launch traced here: 49.9 us
  blocking collectives  32.6 us (65%)
  Pallas kernels  7.61 us (15%)
  starting transfers between devices  7.04 us (14%)
  between operations  1.37 us (3%)
  waiting for transfers between devices  1.3 us (3%)
    all_to_all x1, blocking collectives, per_device(): lax.all_to_all(attention, 'expert', split_axis=0, concat_axis=0, tiled=True)  11.7 us
    all_to_all x1, blocking collectives, per_device(): lax.all_to_all(sent, ('x', 'expert'), split_axis=0, concat_axis=0, tiled=...  10.5 us
    all_to_all x1, blocking collectives, per_device(): lax.all_to_all(gained, ('x', 'expert'), split_axis=0, concat_axis=0, tile...  10.4 us
    ppermute x8, starting transfers between devices, swap_with(): return lax.ppermute(value, axis, pairs)  7.04 us
    pallas_call x1, Pallas kernels, per_device(): pl.pallas_call(functools.partial(stage_kernel, groups), out_shape=[pltpu....  2.66 us
    pallas_call x1, Pallas kernels, per_device(): pl.pallas_call(functools.partial(first_kernel, groups, leave_count), out_...  1.41 us
    ppermute x8, waiting for transfers between devices, swap_with(): return lax.ppermute(value, axis, pairs)  1.3 us
    pallas_call x1, Pallas kernels, per_device(): pl.pallas_call(functools.partial(expert_kernel, width), out_shape=pltpu.V...  1.24 us
  transfers between devices with their start and end apart: 8, of which 3 were waited for; matrix products, arithmetic and copies ran while one was open for 0% of the time, Pallas kernels for 6%

profile of v8, /device:TPU:0, one launch (start us, length us, event | category | flops | bytes accessed | tf_op | source)
XLA Modules:
  0.0 49.9 jit_solution(3840798128759528077)
XLA Ops:
  0.0 0.0 copy-start
  0.0 0.0 copy-start.1
  0.0 1.4 %first.1 = (bf16[512,128]{1,0:T(8,128)(2,1)S(1)}, bf16[192,128]{1,0:T(8,128)(2,1)S(1)}, bf16[192,128]{1,0:T(8,128)(2,1)S(1)}, bf16[192,128]{1,0:T(8,128)(2,1)S(1...) custom-call(s32[4,16]{1,0:T(4,128)} %bitcast.12, ...), custom_call_target="tpu_custom_call" | custom-call | bytes 8388608 | tf_op jit(solution)/shard_map/first/pallas_call | solution.py:377
  1.4 3.0 %collective-permute-start.3 = (bf16[512,128]{1,0:T(8,128)(2,1)S(1)}, bf16[512,128]{1,0:T(8,128)(2,1)S(1)}, u32[]{:S(2)}, u32[]{:S(2)}) collective-permute-start(bf16[512,128]{1,0:T(8,128)(2,1)S(1)} %get-tuple-element.37), channel_id=1, source_target_pairs={{0,1},{1,0},{2,3},{3,2},{4,5},{5,4},{6,7},{7,6},{8,9},{9,8},{10,11... | collective-permute-start | bytes 393224 | tf_op jit(solution)/shard_map/ppermute | solution.py:41
  4.5 0.7 %collective-permute-start = (bf16[192,128]{1,0:T(8,128)(2,1)S(1)}, bf16[192,128]{1,0:T(8,128)(2,1)S(1)}, u32[]{:S(2)}, u32[]{:S(2)}) collective-permute-start(bf16[192,128]{1,0:T(8,128)(2,1)S(1)} %get-tuple-element.34), channel_id=1, source_target_pairs={{0,24},{8,16},{16,8},{24,0},{1,25},{9,17},{17,9},{25,1},{2,26},{10... | collective-permute-start | bytes 147464 | tf_op jit(solution)/shard_map/ppermute | solution.py:41
  5.1 0.9 %collective-permute-start.1 = (bf16[192,128]{1,0:T(8,128)(2,1)S(1)}, bf16[192,128]{1,0:T(8,128)(2,1)S(1)}, u32[]{:S(2)}, u32[]{:S(2)}) collective-permute-start(bf16[192,128]{1,0:T(8,128)(2,1)S(1)} %get-tuple-element.35), channel_id=1, source_target_pairs={{0,16},{8,24},{16,0},{24,8},{1,17},{9,25},{17,1},{25,9},{2,18},{10... | collective-permute-start | bytes 147464 | tf_op jit(solution)/shard_map/ppermute | solution.py:41
  6.0 0.3 collective-permute-start.2
  6.3 2.7 %stage.1 = (f32[1,128]{1,0:T(1,128)S(1)}, f32[1,2048]{1,0:T(1,128)S(1)}, f32[16,256]{1,0:T(8,128)S(1)}, f32[1,256]{1,0:T(1,128)S(1)}, f32[32,128]{1,0:T(8,128)S(1)}, /*index=5*/bf16[3088,512]{1,0:T(8,128)(2,1)S(1)}) custom-call(bf16[16,2048]{1,0:T(8,128)(2,1)S(1)} %get-tuple-element.38.hidden, f32[1,2048]{1,0:T(1,128)} %bitcast.7, s32[10,64]{1,0:T(8,128)} %bitcast.10, ...), custom_call_target="tpu_custom_call" | custom-call | bytes 8388608 | tf_op jit(solution)/shard_map/stage/pallas_call | solution.py:404
  9.0 0.0 collective-permute-done.refs_0_.refs_2_
  9.0 0.7 %collective-permute-done.1.refs_1_ = bf16[192,128]{1,0:T(8,128)(2,1)S(1)} collective-permute-done((bf16[192,128]{1,0:T(8,128)(2,1)S(1)}, bf16[192,128]{1,0:T(8,128)(2,1)S(1)}, u32[]{:S(2)}, u32[]{:S(2)}) %collective-permute-start.1) | collective-permute-done | bytes 49184 | tf_op jit(solution)/shard_map/ppermute | solution.py:41
  9.7 0.0 collective-permute-done.2.refs_2_.refs_0_
  9.7 0.0 collective-permute-done.3.refs_3_
  9.7 0.0 copy-done
  9.7 0.2 project.1
  10.0 0.2 collective-permute-start.4
  10.1 0.8 %collective-permute-start.5 = (bf16[16,640]{1,0:T(8,128)(2,1)S(1)}, bf16[16,640]{1,0:T(8,128)(2,1)S(1)}, u32[]{:S(2)}, u32[]{:S(2)}) collective-permute-start(bf16[16,640]{1,0:T(8,128)(2,1)S(1)} %get-tuple-element.46), channel_id=1, source_target_pairs={{0,16},{8,24},{16,0},{24,8},{1,17},{9,25},{17,1},{25,9},{2,18},{10... | collective-permute-start | bytes 61448 | tf_op jit(solution)/shard_map/ppermute | solution.py:41
  11.0 0.9 %collective-permute-start.6 = (bf16[16,640]{1,0:T(8,128)(2,1)S(1)}, bf16[16,640]{1,0:T(8,128)(2,1)S(1)}, u32[]{:S(2)}, u32[]{:S(2)}) collective-permute-start(bf16[16,640]{1,0:T(8,128)(2,1)S(1)} %get-tuple-element.47), channel_id=1, source_target_pairs={{0,24},{8,16},{16,8},{24,0},{1,25},{9,17},{17,9},{25,1},{2,26},{10... | collective-permute-start | bytes 61448 | tf_op jit(solution)/shard_map/ppermute | solution.py:41
  13.2 0.4 settle.1
  13.6 0.0 collective-permute-done.4.refs_1_
  13.6 0.3 collective-permute-done.5.refs_2_
  13.9 0.3 collective-permute-done.6.refs_3_
  14.2 0.0 copy-done.1
  14.2 0.8 %delta.1 = (bf16[8,16,256]{2,1,0:T(8,128)(2,1)S(1)}, bf16[3088,512]{1,0:T(8,128)(2,1)S(1)}) custom-call(f32[2,128]{1,0:T(2,128)S(1)} %get-tuple-element.41.mixing, f32[1,128]{1,0:T(1,128)S(1)} %get-tuple-element.42.head_gain, bf16[128,2048]{1,0:T(8,128)(2,1)S(1)} %copy-done.1, ...), custom_call_target="tpu_custom_call", output_to_operand_aliasing={{1}: (4, {})} | custom-call | bytes 8388608 | tf_op jit(solution)/shard_map/delta/pallas_call | solution.py:449
  15.0 0.2 collective-permute-start.7
  15.2 11.7 %all_to_all.15.attention = bf16[8,16,256]{2,1,0:T(8,128)(2,1)S(1)} all-to-all(bf16[8,16,256]{2,1,0:T(8,128)(2,1)S(1)} %get-tuple-element.48), channel_id=1, replica_groups=mesh['parts'=1,'x'=2,'core'=2,'expert'=8] {'expert'}, dimensions={0} | all-to-all | bytes 131072 | tf_op jit(solution)/shard_map/all_to_all | solution.py:464
  26.9 10.4 %all_to_all.16.every = bf16[16,16,256]{2,1,0:T(8,128)(2,1)S(1)} all-to-all(bf16[16,16,256]{2,1,0:T(8,128)(2,1)S(1)} %get-tuple-element.50), channel_id=1, replica_groups=mesh['parts'=1,'x'=2,'core'=2,'expert'=8] {'x','expert'}, dimensions={0} | all-to-all | bytes 262144 | tf_op jit(solution)/shard_map/all_to_all | solution.py:478
  37.3 0.0 collective-permute-done.7.other
  37.3 1.2 %experts.1 = bf16[16,40,128]{2,1,0:T(8,128)(2,1)S(1)} custom-call(bf16[16,16,256]{2,1,0:T(8,128)(2,1)S(1)} %all_to_all.16.every, f32[32,128]{1,0:T(8,128)S(1)} %get-tuple-element.51.hits, f32[1,2048]{1,0:T(1,128)S(1)} %get-tuple-element.52.gain, bf16[3088,512]{1,0:T(8,128)(2,1)S(1)} %get-tuple-element.53.own, bf16[3088,512]{1,0:T(8,128)(2,1)S(1)} %collective-permute-done.7.other), custom_call_target="tpu_custom_call" | custom-call | bytes 8388608 | tf_op jit(solution)/shard_map/experts/pallas_call | solution.py:481
  38.5 10.5 %all_to_all.17.back = bf16[16,40,128]{2,1,0:T(8,128)(2,1)S(1)} all-to-all(bf16[16,40,128]{2,1,0:T(8,128)(2,1)S(1)} %experts.1), channel_id=1, replica_groups=mesh['parts'=1,'x'=2,'core'=2,'expert'=8] {'x','expert'}, dimensions={0} | all-to-all | bytes 327680 | tf_op jit(solution)/shard_map/all_to_all | solution.py:490
  49.1 0.8 %finish.1 = bf16[16,256]{1,0:T(8,128)(2,1)} custom-call(bf16[16,40,128]{2,1,0:T(8,128)(2,1)S(1)} %all_to_all.17.back, f32[16,256]{1,0:T(8,128)S(1)} %get-tuple-element.54.residual), custom_call_target="tpu_custom_call" | custom-call | bytes 8388608 | tf_op jit(solution)/shard_map/finish/pallas_call | solution.py:491
  (1 shorter events, 0.0 us)
Async XLA Ops:
  0.0 9.7 %copy-start = (bf16[512,384]{1,0:T(8,128)(2,1)S(1)}, bf16[512,384]{1,0:T(8,128)(2,1)}, u32[]{:S(2)}) copy-start(bf16[512,384]{1,0:T(8,128)(2,1)} %w_qkvz.3) | copy-start | bytes 1179652
  0.0 14.2 %copy-start.1 = (bf16[128,2048]{1,0:T(8,128)(2,1)S(1)}, bf16[128,2048]{1,0:T(8,128)(2,1)}, u32[]{:S(2)}) copy-start(bf16[128,2048]{1,0:T(8,128)(2,1)} %w_out.1) | copy-start | bytes 1572868
  1.4 8.3 %collective-permute-start.3 = (bf16[512,128]{1,0:T(8,128)(2,1)S(1)}, bf16[512,128]{1,0:T(8,128)(2,1)S(1)}, u32[]{:S(2)}, u32[]{:S(2)}) collective-permute-start(bf16[512,128]{1,0:T(8,128)(2,1)S(1)} %get-tuple-element.37), channel_id=1, source_target_pairs={{0,1},{1,0},{2,3},{3,2},{4,5},{5,4},{6,7},{7,6},{8,9},{9,8},{10,11... | collective-permute-start | bytes 393224 | tf_op jit(solution)/shard_map/ppermute | solution.py:41
  4.5 4.5 %collective-permute-start = (bf16[192,128]{1,0:T(8,128)(2,1)S(1)}, bf16[192,128]{1,0:T(8,128)(2,1)S(1)}, u32[]{:S(2)}, u32[]{:S(2)}) collective-permute-start(bf16[192,128]{1,0:T(8,128)(2,1)S(1)} %get-tuple-element.34), channel_id=1, source_target_pairs={{0,24},{8,16},{16,8},{24,0},{1,25},{9,17},{17,9},{25,1},{2,26},{10... | collective-permute-start | bytes 147464 | tf_op jit(solution)/shard_map/ppermute | solution.py:41
  5.1 4.6 %collective-permute-start.1 = (bf16[192,128]{1,0:T(8,128)(2,1)S(1)}, bf16[192,128]{1,0:T(8,128)(2,1)S(1)}, u32[]{:S(2)}, u32[]{:S(2)}) collective-permute-start(bf16[192,128]{1,0:T(8,128)(2,1)S(1)} %get-tuple-element.35), channel_id=1, source_target_pairs={{0,16},{8,24},{16,0},{24,8},{1,17},{9,25},{17,1},{25,9},{2,18},{10... | collective-permute-start | bytes 147464 | tf_op jit(solution)/shard_map/ppermute | solution.py:41
  6.0 3.7 %collective-permute-start.2 = (bf16[192,128]{1,0:T(8,128)(2,1)S(1)}, bf16[192,128]{1,0:T(8,128)(2,1)S(1)}, u32[]{:S(2)}, u32[]{:S(2)}) collective-permute-start(bf16[192,128]{1,0:T(8,128)(2,1)S(1)} %get-tuple-element.36), channel_id=1, source_target_pairs={{0,8},{8,0},{16,24},{24,16},{1,9},{9,1},{17,25},{25,17},{2,10},{10... | collective-permute-start | bytes 147464 | tf_op jit(solution)/shard_map/ppermute | solution.py:41
  10.0 3.6 %collective-permute-start.4 = (bf16[16,640]{1,0:T(8,128)(2,1)S(1)}, bf16[16,640]{1,0:T(8,128)(2,1)S(1)}, u32[]{:S(2)}, u32[]{:S(2)}) collective-permute-start(bf16[16,640]{1,0:T(8,128)(2,1)S(1)} %get-tuple-element.45), channel_id=1, source_target_pairs={{0,8},{8,0},{16,24},{24,16},{1,9},{9,1},{17,25},{25,17},{2,10},{10... | collective-permute-start | bytes 61448 | tf_op jit(solution)/shard_map/ppermute | solution.py:41
  10.1 3.8 %collective-permute-start.5 = (bf16[16,640]{1,0:T(8,128)(2,1)S(1)}, bf16[16,640]{1,0:T(8,128)(2,1)S(1)}, u32[]{:S(2)}, u32[]{:S(2)}) collective-permute-start(bf16[16,640]{1,0:T(8,128)(2,1)S(1)} %get-tuple-element.46), channel_id=1, source_target_pairs={{0,16},{8,24},{16,0},{24,8},{1,17},{9,25},{17,1},{25,9},{2,18},{10... | collective-permute-start | bytes 61448 | tf_op jit(solution)/shard_map/ppermute | solution.py:41
  11.0 3.2 %collective-permute-start.6 = (bf16[16,640]{1,0:T(8,128)(2,1)S(1)}, bf16[16,640]{1,0:T(8,128)(2,1)S(1)}, u32[]{:S(2)}, u32[]{:S(2)}) collective-permute-start(bf16[16,640]{1,0:T(8,128)(2,1)S(1)} %get-tuple-element.47), channel_id=1, source_target_pairs={{0,24},{8,16},{16,8},{24,0},{1,25},{9,17},{17,9},{25,1},{2,26},{10... | collective-permute-start | bytes 61448 | tf_op jit(solution)/shard_map/ppermute | solution.py:41
  15.0 22.3 %collective-permute-start.7 = (bf16[3088,512]{1,0:T(8,128)(2,1)S(1)}, bf16[3088,512]{1,0:T(8,128)(2,1)S(1)}, u32[]{:S(2)}, u32[]{:S(2)}) collective-permute-start(bf16[3088,512]{1,0:T(8,128)(2,1)S(1)} %get-tuple-element.53.own), channel_id=1, source_target_pairs={{0,8},{8,0},{1,9},{9,1},{2,10},{10,2},{3,11},{11,3},{4,12},{12,4},... | collective-permute-start | bytes 9486344 | tf_op jit(solution)/shard_map/ppermute | solution.py:41
